TPU v7x, 256 devices: a whole 4x4x8 slice. The times are simulated.
256 devices in a mesh: phase: 2 (over z_lo), slab: 4 (over y), tile: 32 (over z_hi, x, core).
Axes of the slice: x: 4, y: 4, z: 8 (z_hi: 4, z_lo: 2; z = z_hi * 2 + z_lo), core: 2. Of those that a mesh axis runs over, the one named last changes fastest.
Arguments:
- volume: float32 [128, 1024, 512], P('slab', 'tile'), may hold values from -6 to 6
- frac: float32 [2, 1024, 512], P('phase', 'tile'), may hold values from 0 to 1
- shift: int32 [2, 1024], P('phase', 'tile'), may hold values from -16 to 15
- angle_index: int32 [2, 32], P('phase'), may hold values from 0 to 679
- depth_weights: float32 [680, 128], P(None, 'slab'), may hold values from -0.5 to 0.5
- measured: float32 [2, 32, 1024, 512], P('phase', None, 'tile'), may hold values from -6 to 6
Outputs:
- image_grad: float32 [128, 1024, 512], P('slab', 'tile')
- field_grad: float32 [2, 1024, 512], P('phase', 'tile')
All inputs are finite; a program needn't handle non-finite values.
Results may differ from a plain program's by a relative error of at most 0.0001.
Values sent between devices are 32-bit elements; how exact they have to be, the bound alone decides.
No kernel may reach another device: no remote copies, remote signals or barrier semaphores. Data moves between devices by JAX's collectives and lax.ppermute only.
A program may use at most 128 MiB of HBM per device.

v0:
```python
import jax
import jax.numpy as jnp
from jax import lax
from jax.sharding import PartitionSpec as P

HALO = 16
ITS = 4


DIFFUSION = 0.2


def with_halo(cells, sides, width):
    for axis, dim in sides:
        count = lax.axis_size(axis)
        ends = count - 1
        head = lax.slice_in_dim(cells, 0, width, axis=dim)
        tail = lax.slice_in_dim(cells, cells.shape[dim] - width, cells.shape[dim], axis=dim)
        cells = jnp.concatenate(
            [
                lax.ppermute(tail, axis, [(i, (i + 1) % count) for i in range(ends)]),
                cells,
                lax.ppermute(head, axis, [((i + 1) % count, i) for i in range(ends)]),
            ],
            axis=dim,
        )
    return cells


def passed_along(block, axis, distance):
    devices = range(lax.axis_size(axis))
    route = [(i - distance, i) for i in devices if i - distance in devices]
    return lax.ppermute(block, axis, route)


def body(volume, frac, shift, angle_index, depth_weights, measured):
    depth_len, tile_len, height = volume.shape
    measured_all, frac_all, shift_all, index_all = (measured, frac, shift, angle_index)
    extended = with_halo(volume, (("tile", 1),), HALO)
    table_rows = depth_weights.shape[0]
    picker = (index_all[0][:, None] == jnp.arange(table_rows, dtype=jnp.int32)[None, :]).astype(
        jnp.float32
    )
    weights = jnp.dot(picker, depth_weights, precision=lax.Precision.HIGHEST)
    angles = weights.shape[0]
    columns = jnp.arange(tile_len, dtype=jnp.int32) + HALO + shift_all[0]

    def warp_local(image, part):
        lower = jnp.take(image, columns, axis=1)
        upper = jnp.take(image, columns + 1, axis=1)
        return (1.0 - part)[None] * lower + part[None] * upper

    warped, pullback = jax.vjp(warp_local, extended, frac_all[0])
    flat_warp = warped.reshape(depth_len, tile_len * height)
    observed = measured_all[0].reshape(angles, tile_len * height)
    partial_proj = jnp.dot(weights, flat_warp, precision=lax.Precision.HIGHEST)
    projected = lax.psum(partial_proj, "slab")
    residual = projected - observed
    spread = jnp.dot(weights.T, residual, precision=lax.Precision.HIGHEST)
    grad_image, grad_frac = pullback(spread.reshape(depth_len, tile_len, height))
    fields = [grad_frac]
    stacked = jnp.stack(fields)
    field = lax.psum(stacked, "slab")
    for sweep in range(ITS):
        widened = with_halo(field, (("tile", 1),), 1)
        padded = jnp.pad(widened, ((0, 0), (0, 0), (1, 1)))
        laplace = (
            padded[:, 2:, 1:-1]
            + padded[:, :-2, 1:-1]
            + padded[:, 1:-1, 2:]
            + padded[:, 1:-1, :-2]
            - 4.0 * field
        )
        field = field + DIFFUSION * laplace
    from_right = passed_along(grad_image[:, :HALO], "tile", -1)
    from_left = passed_along(grad_image[:, tile_len + HALO :], "tile", 1)
    own_grad = grad_image[:, HALO : HALO + tile_len]
    own_grad = own_grad + jnp.pad(from_left, ((0, 0), (0, tile_len - HALO), (0, 0)))
    own_grad = own_grad + jnp.pad(from_right, ((0, 0), (tile_len - HALO, 0), (0, 0)))
    image_grad = lax.psum(own_grad, "phase")
    return (image_grad, field)


def solution(mesh):
    return jax.shard_map(
        body,
        mesh=mesh,
        in_specs=(
            P("slab", "tile", None),
            P("phase", "tile", None),
            P("phase", "tile"),
            P("phase", None),
            P(None, "slab"),
            P("phase", None, "tile", None),
        ),
        out_specs=(P("slab", "tile", None), P("phase", "tile", None)),
        check_vma=False,
    )
```

profile of v0, /device:TPU:128, one launch (start us, length us, event | category | flops | bytes accessed | tf_op | source)
XLA Modules:
  0.0 296.6 jit_solution(13291034963584085045)
XLA Ops:
  7.2 1.8 fusion.29
  9.1 0.6 copy.36
  9.7 1.9 collective-permute-start
  12.2 7.9 %collective-permute-start.1 = (f32[32,16,512]{2,0,1:T(8,128)S(1)}, f32[32,16,512]{2,0,1:T(8,128)S(1)}, u32[]{:S(2)}, u32[]{:S(2)}) collective-permute-start(f32[32,16,512]{2,0,1:T(8,128)S(1)} %copy.37), channel_id=1, source_target_pairs={{1,0},{2,1},{3,2},{4,3},{5,4},{6,5},{7,6},{8,7},{9,8},{10,9},{11,1... | collective-permute-start | bytes 3145736 | tf_op jit(solution)/shard_map/ppermute | solution.py:23
  20.4 20.8 %collective-permute-done = f32[32,16,512]{2,0,1:T(8,128)S(1)} collective-permute-done((f32[32,16,512]{2,0,1:T(8,128)S(1)}, f32[32,16,512]{2,0,1:T(8,128)S(1)}, u32[]{:S(2)}, u32[]{:S(2)}) %collective-permute-start) | collective-permute-done | bytes 1048608 | tf_op jit(solution)/shard_map/ppermute | solution.py:21
  41.3 1.2 constant_dynamic-update-slice_fusion.1
  42.5 1.0 collective-permute-done.1
  43.6 1.9 copy-done.6
  45.6 2.9 gather_fusion.1
  48.4 4.2 %gather_fusion = f32[32,32,512]{2,1,0:T(8,128)} fusion(f32[32,64,512]{2,0,1:T(8,128)} %copy-done.6, s32[1024]{0:T(1024)S(1)} %get-tuple-element.38), kind=kCustom, calls=%fused_computation.clone | custom fusion | bytes 4194432 | tf_op jit(solution)/shard_map/jvp(jit(_take))/gather | solution.py:50
  52.6 2.0 fusion.6
  54.8 3.2 %fusion.34 = f32[32,16384]{1,0:T(8,128)} fusion(f32[32,32]{1,0:T(8,128)S(1)} %fusion.10, f32[32,16384]{1,0:T(8,128)S(1)} %bitcast.58), kind=kOutput, calls=%fused_computation.84 | convolution fusion | flops 201326592 | bytes 4198400 | tf_op jit(solution)/shard_map/dot_general | solution.py:56
  58.3 4.2 %copy.30 = f32[4,8,32,512]{3,1,2,0:T(8,128)} copy(f32[4,8,32,512]{3,2,1,0:T(8,128)} %bitcast.59) | data formatting | bytes 4194304
  62.4 61.4 %all-reduce.10.cloned.1.call-done = f32[32,16384]{1,0:T(8,128)} async-done(((f32[32,16384]{1,0:T(8,128)}), f32[32,16384]{1,0:T(8,128)}) %all-reduce.10.cloned.1.call-update) | async-done | bytes 2097168 | tf_op jit(solution)/shard_map/psum | solution.py:57
  123.9 3.8 %fusion.7 = f32[32,16384]{1,0:T(8,128)S(1)} fusion(f32[32,32]{1,0:T(8,128)S(1)} %fusion.10, f32[32,16384]{1,0:T(8,128)} %all-reduce.10.cloned.1.call-done, f32[32,16384]{1,0:T(8,128)} %bitcast.56), kind=kOutput, calls=%fused_computation.18 | convolution fusion | flops 201850880 | bytes 6295552 | tf_op jit(solution)/shard_map/dot_general | solution.py:59
  127.7 3.4 %fusion.3 = (f32[32,512]{1,0:T(8,128)S(1)}, f32[32,512]{1,0:T(8,128)S(1)}, f32[32,32,512]{2,1,0:T(8,128)}, f32[32,32,512]{2,1,0:T(8,128)}) fusion(f32[32,32,512]{2,1,0:T(8,128)S(1)} %gather_fusion.1, f32[4,32,8,512]{3,2,1,0:T(8,128)S(1)} %bitcast.57, pred[32]{0:T(512)(128)(4,1)S(1)} %get-tuple-element.20, f32[32,32,512]{2,1,0:T(8,128)S(1)} %copy-done.1, ...), kind=kLoop, calls=%fused_computation.11 | loop fusion | flops 4161536 | bytes 10747968 | tf_op jit(solution)/shard_map/transpose(jvp())/reduce_sum | solution.py:51
  131.1 2.5 broadcast_in_dim.16.clone
  133.5 6.1 %scatter_fusion = f32[32,64,512]{2,0,1:T(8,128)} fusion(f32[32,64,512]{2,0,1:T(8,128)} %broadcast_in_dim.16.clone, s32[32]{0:T(128)S(1)} %get-tuple-element.37, f32[32,32,512]{2,1,0:T(8,128)S(1)} %copy-done.5), kind=kCustom, calls=%fused_computation.2 | custom fusion | flops 524288 | bytes 6291584 | tf_op jit(solution)/shard_map/transpose(jvp(jit(_take)))/scatter-add | solution.py:50
  139.7 2.5 broadcast_in_dim.16.clone.1
  142.2 6.1 %scatter_fusion.1 = f32[32,64,512]{2,0,1:T(8,128)} fusion(f32[32,64,512]{2,0,1:T(8,128)} %broadcast_in_dim.16.clone.1, s32[32]{0:T(128)S(1)} %get-tuple-element.21, f32[32,32,512]{2,1,0:T(8,128)S(1)} %copy-done.4), kind=kCustom, calls=%fused_computation.3 | custom fusion | flops 524288 | bytes 6291584 | tf_op jit(solution)/shard_map/transpose(jvp(jit(_take)))/scatter-add | solution.py:49
  148.3 4.5 %add_any.16 = f32[32,64,512]{2,0,1:T(8,128)S(1)} add(f32[32,64,512]{2,0,1:T(8,128)} %scatter_fusion, f32[32,64,512]{2,0,1:T(8,128)} %scatter_fusion.1) | non-fusion elementwise | flops 1048576 | bytes 12582912 | tf_op jit(solution)/shard_map/transpose(jvp())/add_any | solution.py:49
  152.8 1.3 fusion.28
  154.1 1.0 copy-done.2
  155.1 1.9 collective-permute-start.2
  157.0 7.9 %collective-permute-start.3 = (f32[32,16,512]{2,0,1:T(8,128)S(1)}, f32[32,16,512]{2,0,1:T(8,128)S(1)}, u32[]{:S(2)}, u32[]{:S(2)}) collective-permute-start(f32[32,16,512]{2,0,1:T(8,128)S(1)} %get-tuple-element.23), channel_id=1, source_target_pairs={{1,0},{2,1},{3,2},{4,3},{5,4},{6,5},{7,6},{8,7},{9,8},{10,9},{11,1... | collective-permute-start | bytes 3145736 | tf_op jit(solution)/shard_map/ppermute | solution.py:33
  164.9 0.6 add_bitcast_fusion
  165.6 21.2 %collective-permute-done.2 = f32[32,16,512]{2,0,1:T(8,128)S(1)} collective-permute-done((f32[32,16,512]{2,0,1:T(8,128)}, f32[32,16,512]{2,0,1:T(8,128)S(1)}, u32[]{:S(2)}, u32[]{:S(2)}) %collective-permute-start.2) | collective-permute-done | bytes 1048608 | tf_op jit(solution)/shard_map/ppermute | solution.py:33
  186.8 0.8 collective-permute-done.3
  187.6 3.4 %fusion.4 = f32[32,32,512]{2,0,1:T(8,128)} fusion(f32[32,64,512]{2,0,1:T(8,128)} %copy-done.2, f32[32,16,512]{2,0,1:T(8,128)S(1)} %collective-permute-done.3, f32[32,16,512]{2,0,1:T(8,128)S(1)} %collective-permute-done.2), kind=kLoop, calls=%fused_computation.13 | loop fusion | flops 1048576 | bytes 6291456 | tf_op jit(solution)/shard_map/add | solution.py:79
  191.0 18.0 %all-reduce.14.cloned.1.call-done = f32[1,32,512]{2,1,0:T(8,128)} async-done(((f32[1,32,512]{2,1,0:T(8,128)}), f32[1,32,512]{2,1,0:T(8,128)}) %all-reduce.14.cloned.1.call-update) | async-done | bytes 65552 | tf_op jit(solution)/shard_map/psum | solution.py:63
  209.1 0.7 fusion.33
  209.8 1.9 collective-permute-start.5
  211.7 7.9 %collective-permute-start.4 = (f32[1,1,512]{2,1,0:T(1,128)S(1)}, f32[1,1,512]{2,1,0:T(1,128)S(1)}, u32[]{:S(2)}, u32[]{:S(2)}) collective-permute-start(f32[1,1,512]{2,1,0:T(1,128)S(1)} %get-tuple-element.35), channel_id=1, source_target_pairs={{1,0},{2,1},{3,2},{4,3},{5,4},{6,5},{7,6},{8,7},{9,8},{10,9},{11,1... | collective-permute-start | bytes 6152 | tf_op jit(solution)/shard_map/ppermute | solution.py:23
  219.6 1.3 collective-permute-done.4
  220.9 0.9 select_maximum_fusion.6
  221.8 1.0 fusion.25
  222.9 1.9 collective-permute-start.7
  224.8 7.9 %collective-permute-start.6 = (f32[1,1,512]{2,1,0:T(1,128)S(1)}, f32[1,1,512]{2,1,0:T(1,128)S(1)}, u32[]{:S(2)}, u32[]{:S(2)}) collective-permute-start(f32[1,1,512]{2,1,0:T(1,128)S(1)} %get-tuple-element.33), channel_id=1, source_target_pairs={{1,0},{2,1},{3,2},{4,3},{5,4},{6,5},{7,6},{8,7},{9,8},{10,9},{11,1... | collective-permute-start | bytes 6152 | tf_op jit(solution)/shard_map/ppermute | solution.py:23
  232.7 1.3 collective-permute-done.6
  234.2 1.9 collective-permute-start.9
  236.1 7.9 %collective-permute-start.8 = (f32[1,1,512]{2,1,0:T(1,128)S(1)}, f32[1,1,512]{2,1,0:T(1,128)S(1)}, u32[]{:S(2)}, u32[]{:S(2)}) collective-permute-start(f32[1,1,512]{2,1,0:T(1,128)S(1)} %get-tuple-element.31), channel_id=1, source_target_pairs={{1,0},{2,1},{3,2},{4,3},{5,4},{6,5},{7,6},{8,7},{9,8},{10,9},{11,1... | collective-permute-start | bytes 6152 | tf_op jit(solution)/shard_map/ppermute | solution.py:23
  244.1 1.3 collective-permute-done.8
  245.6 1.9 collective-permute-start.11
  247.5 7.9 %collective-permute-start.10 = (f32[1,1,512]{2,1,0:T(1,128)S(1)}, f32[1,1,512]{2,1,0:T(1,128)S(1)}, u32[]{:S(2)}, u32[]{:S(2)}) collective-permute-start(f32[1,1,512]{2,1,0:T(1,128)S(1)} %get-tuple-element.29), channel_id=1, source_target_pairs={{1,0},{2,1},{3,2},{4,3},{5,4},{6,5},{7,6},{8,7},{9,8},{10,9},{11,1... | collective-permute-start | bytes 6152 | tf_op jit(solution)/shard_map/ppermute | solution.py:23
  255.4 1.3 collective-permute-done.10
  256.8 0.7 fusion.13
  257.5 28.5 %all-reduce.12.cloned.1.call-done = f32[32,32,512]{2,0,1:T(8,128)} async-done(((f32[32,32,512]{2,0,1:T(8,128)}), f32[32,32,512]{2,0,1:T(8,128)}) %all-reduce.12.cloned.1.call-update) | async-done | bytes 2097168 | tf_op jit(solution)/shard_map/psum | solution.py:80
  286.0 4.1 %copy.27 = f32[32,32,512]{2,1,0:T(8,128)} copy(f32[32,32,512]{2,0,1:T(8,128)} %all-reduce.12.cloned.1.call-done) | data formatting | bytes 4194304
  (44 shorter events, 2.2 us)
Async XLA Ops:
  7.2 13.0 %copy-start = (f32[680,32]{0,1:T(8,128)S(1)}, f32[680,32]{0,1:T(8,128)}, u32[]{:S(2)}) copy-start(f32[680,32]{0,1:T(8,128)} %param.12) | copy-start | bytes 261124
  7.2 116.7 %all-reduce.10.cloned.1.call-start = ((), (), s32[]{:S(2)}) async-start(), calls=%async_computation | async-start | bytes 4194304 | tf_op jit(solution)/shard_map/psum | solution.py:57
  9.0 11.1 %copy-start.9 = (s32[1,32]{1,0:T(1,128)S(1)}, s32[1,32]{1,0:T(1,128)}, u32[]{:S(2)}) copy-start(s32[1,32]{1,0:T(1,128)} %param.10) | copy-start | bytes 388
  9.0 11.1 %copy-start.8 = (s32[1,32]{1,0:T(1,128)S(1)}, s32[1,32]{1,0:T(1,128)}, u32[]{:S(2)}) copy-start(s32[1,32]{1,0:T(1,128)} %param.11) | copy-start | bytes 388
  9.1 11.4 %copy-start.7 = (f32[1,32,512]{2,1,0:T(8,128)S(1)}, f32[1,32,512]{2,1,0:T(8,128)}, u32[]{:S(2)}) copy-start(f32[1,32,512]{2,1,0:T(8,128)} %param.9) | copy-start | bytes 196612
  9.7 31.5 %collective-permute-start = (f32[32,16,512]{2,0,1:T(8,128)S(1)}, f32[32,16,512]{2,0,1:T(8,128)S(1)}, u32[]{:S(2)}, u32[]{:S(2)}) collective-permute-start(f32[32,16,512]{2,0,1:T(8,128)S(1)} %copy.36), channel_id=1, source_target_pairs={{0,1},{1,2},{2,3},{3,4},{4,5},{5,6},{6,7},{7,8},{8,9},{9,10},{10,1... | collective-permute-start | bytes 3145736 | tf_op jit(solution)/shard_map/ppermute | solution.py:21
  11.6 29.7 %copy-start.3 = (f32[32,32,512]{2,1,0:T(8,128)S(1)}, f32[32,32,512]{2,1,0:T(8,128)}, u32[]{:S(2)}) copy-start(f32[32,32,512]{2,1,0:T(8,128)} %param.8) | copy-start | bytes 6291460
  12.2 31.3 %collective-permute-start.1 = (f32[32,16,512]{2,0,1:T(8,128)S(1)}, f32[32,16,512]{2,0,1:T(8,128)S(1)}, u32[]{:S(2)}, u32[]{:S(2)}) collective-permute-start(f32[32,16,512]{2,0,1:T(8,128)S(1)} %copy.37), channel_id=1, source_target_pairs={{1,0},{2,1},{3,2},{4,3},{5,4},{6,5},{7,6},{8,7},{9,8},{10,9},{11,1... | collective-permute-start | bytes 3145736 | tf_op jit(solution)/shard_map/ppermute | solution.py:23
  43.6 2.0 copy-start.6
  58.0 151.0 %all-reduce.14.cloned.1.call-start = ((), (), s32[]{:S(2)}) async-start(), calls=%async_computation.2 | async-start | bytes 131072 | tf_op jit(solution)/shard_map/psum | solution.py:63
  123.9 3.8 %copy-start.1 = (f32[32,32,512]{2,1,0:T(8,128)S(1)}, f32[32,32,512]{2,1,0:T(8,128)}, u32[]{:S(2)}) copy-start(f32[32,32,512]{2,1,0:T(8,128)} %gather_fusion) | copy-start | bytes 6291460
  131.1 2.5 copy-start.5
  139.7 2.5 copy-start.4
  152.8 2.3 copy-start.2
  155.1 31.7 %collective-permute-start.2 = (f32[32,16,512]{2,0,1:T(8,128)}, f32[32,16,512]{2,0,1:T(8,128)S(1)}, u32[]{:S(2)}, u32[]{:S(2)}) collective-permute-start(f32[32,16,512]{2,0,1:T(8,128)} %get-tuple-element.22), channel_id=1, source_target_pairs={{0,1},{1,2},{2,3},{3,4},{4,5},{5,6},{6,7},{7,8},{8,9},{9,10},{10,1... | collective-permute-start | bytes 3145736 | tf_op jit(solution)/shard_map/ppermute | solution.py:33
  157.0 30.6 %collective-permute-start.3 = (f32[32,16,512]{2,0,1:T(8,128)S(1)}, f32[32,16,512]{2,0,1:T(8,128)S(1)}, u32[]{:S(2)}, u32[]{:S(2)}) collective-permute-start(f32[32,16,512]{2,0,1:T(8,128)S(1)} %get-tuple-element.23), channel_id=1, source_target_pairs={{1,0},{2,1},{3,2},{4,3},{5,4},{6,5},{7,6},{8,7},{9,8},{10,9},{11,1... | collective-permute-start | bytes 3145736 | tf_op jit(solution)/shard_map/ppermute | solution.py:33
  165.6 120.4 %all-reduce.12.cloned.1.call-start = ((), (), s32[]{:S(2)}) async-start(), calls=%async_computation.1 | async-start | bytes 4194304 | tf_op jit(solution)/shard_map/psum | solution.py:80
  209.8 9.8 %collective-permute-start.5 = (f32[1,1,512]{2,1,0:T(1,128)S(1)}, f32[1,1,512]{2,1,0:T(1,128)S(1)}, u32[]{:S(2)}, u32[]{:S(2)}) collective-permute-start(f32[1,1,512]{2,1,0:T(1,128)S(1)} %get-tuple-element.34), channel_id=1, source_target_pairs={{0,1},{1,2},{2,3},{3,4},{4,5},{5,6},{6,7},{7,8},{8,9},{9,10},{10,1... | collective-permute-start | bytes 6152 | tf_op jit(solution)/shard_map/ppermute | solution.py:21
  211.7 9.2 %collective-permute-start.4 = (f32[1,1,512]{2,1,0:T(1,128)S(1)}, f32[1,1,512]{2,1,0:T(1,128)S(1)}, u32[]{:S(2)}, u32[]{:S(2)}) collective-permute-start(f32[1,1,512]{2,1,0:T(1,128)S(1)} %get-tuple-element.35), channel_id=1, source_target_pairs={{1,0},{2,1},{3,2},{4,3},{5,4},{6,5},{7,6},{8,7},{9,8},{10,9},{11,1... | collective-permute-start | bytes 6152 | tf_op jit(solution)/shard_map/ppermute | solution.py:23
  222.9 9.8 %collective-permute-start.7 = (f32[1,1,512]{2,1,0:T(1,128)S(1)}, f32[1,1,512]{2,1,0:T(1,128)S(1)}, u32[]{:S(2)}, u32[]{:S(2)}) collective-permute-start(f32[1,1,512]{2,1,0:T(1,128)S(1)} %get-tuple-element.32), channel_id=1, source_target_pairs={{0,1},{1,2},{2,3},{3,4},{4,5},{5,6},{6,7},{7,8},{8,9},{9,10},{10,1... | collective-permute-start | bytes 6152 | tf_op jit(solution)/shard_map/ppermute | solution.py:21
  224.8 9.2 %collective-permute-start.6 = (f32[1,1,512]{2,1,0:T(1,128)S(1)}, f32[1,1,512]{2,1,0:T(1,128)S(1)}, u32[]{:S(2)}, u32[]{:S(2)}) collective-permute-start(f32[1,1,512]{2,1,0:T(1,128)S(1)} %get-tuple-element.33), channel_id=1, source_target_pairs={{1,0},{2,1},{3,2},{4,3},{5,4},{6,5},{7,6},{8,7},{9,8},{10,9},{11,1... | collective-permute-start | bytes 6152 | tf_op jit(solution)/shard_map/ppermute | solution.py:23
  234.2 9.9 %collective-permute-start.9 = (f32[1,1,512]{2,1,0:T(1,128)S(1)}, f32[1,1,512]{2,1,0:T(1,128)S(1)}, u32[]{:S(2)}, u32[]{:S(2)}) collective-permute-start(f32[1,1,512]{2,1,0:T(1,128)S(1)} %get-tuple-element.30), channel_id=1, source_target_pairs={{0,1},{1,2},{2,3},{3,4},{4,5},{5,6},{6,7},{7,8},{8,9},{9,10},{10,1... | collective-permute-start | bytes 6152 | tf_op jit(solution)/shard_map/ppermute | solution.py:21
  236.1 9.2 %collective-permute-start.8 = (f32[1,1,512]{2,1,0:T(1,128)S(1)}, f32[1,1,512]{2,1,0:T(1,128)S(1)}, u32[]{:S(2)}, u32[]{:S(2)}) collective-permute-start(f32[1,1,512]{2,1,0:T(1,128)S(1)} %get-tuple-element.31), channel_id=1, source_target_pairs={{1,0},{2,1},{3,2},{4,3},{5,4},{6,5},{7,6},{8,7},{9,8},{10,9},{11,1... | collective-permute-start | bytes 6152 | tf_op jit(solution)/shard_map/ppermute | solution.py:23
  245.6 9.8 %collective-permute-start.11 = (f32[1,1,512]{2,1,0:T(1,128)S(1)}, f32[1,1,512]{2,1,0:T(1,128)S(1)}, u32[]{:S(2)}, u32[]{:S(2)}) collective-permute-start(f32[1,1,512]{2,1,0:T(1,128)S(1)} %get-tuple-element.28), channel_id=1, source_target_pairs={{0,1},{1,2},{2,3},{3,4},{4,5},{5,6},{6,7},{7,8},{8,9},{9,10},{10,1... | collective-permute-start | bytes 6152 | tf_op jit(solution)/shard_map/ppermute | solution.py:21
  247.5 9.2 %collective-permute-start.10 = (f32[1,1,512]{2,1,0:T(1,128)S(1)}, f32[1,1,512]{2,1,0:T(1,128)S(1)}, u32[]{:S(2)}, u32[]{:S(2)}) collective-permute-start(f32[1,1,512]{2,1,0:T(1,128)S(1)} %get-tuple-element.29), channel_id=1, source_target_pairs={{1,0},{2,1},{3,2},{4,3},{5,4},{6,5},{7,6},{8,7},{9,8},{10,9},{11,1... | collective-permute-start | bytes 6152 | tf_op jit(solution)/shard_map/ppermute | solution.py:23
Sparse Core Ops, SparseCore 0:
  58.2 65.6 all-reduce.9
  165.7 43.3 all-reduce.13
  212.2 73.6 all-reduce.11
where the time goes:
time: 301 us; the launch traced here: 297 us
  waiting for transfers between devices  157 us (52%)
  starting transfers between devices  59 us (20%)
  local copies, waits for them, and re-layouts  30 us (10%)
  other arithmetic  29.3 us (10%)
  between operations  14.1 us (5%)
  matrix products  7.28 us (2%)
    psum x1, waiting for transfers between devices, body(): projected = lax.psum(partial_proj, 'slab')  61.4 us
    ppermute x5, starting transfers between devices, with_halo(): lax.ppermute(head, axis, [((i + 1) % count, i) for i in range(ends)])  39.4 us
    psum x1, waiting for transfers between devices, body(): image_grad = lax.psum(own_grad, 'phase')  28.5 us
    ppermute x2, waiting for transfers between devices, passed_along(): return lax.ppermute(block, axis, route)  22 us
    ppermute x5, waiting for transfers between devices, with_halo(): lax.ppermute(tail, axis, [(i, (i + 1) % count) for i in range(ends)])  20.8 us
    psum x1, waiting for transfers between devices, body(): field = lax.psum(stacked, 'slab')  18 us
    unnamed x26, local copies, waits for them, and re-layouts  13.8 us
    ppermute x2, starting transfers between devices, passed_along(): return lax.ppermute(block, axis, route)  9.77 us
  transfers between devices with their start and end apart: 15, of which 11 were waited for; matrix products, arithmetic and copies ran while one was open for 5% of the time, Pallas kernels for 0%

commit v1 on v0

v1 whole, which is shorter than its diff:
```python
import jax
import jax.numpy as jnp
from jax import lax
from jax.experimental import pallas as pl
from jax.experimental.pallas import tpu as pltpu
from jax.sharding import PartitionSpec as P

HALO = 16
ITS = 4
DIFFUSION = 0.2
EDGE = 8
LANES = 128
HIGH = lax.Precision.HIGHEST
F32 = jnp.float32
VMEM = pl.BlockSpec(memory_space=pltpu.VMEM)
SMEM = pl.BlockSpec(memory_space=pltpu.SMEM)


def call(kernel, outs, in_specs, scratch=(), limit=16, flops=1 << 22, moved=1 << 22):
    return pl.pallas_call(
        kernel,
        out_shape=[jax.ShapeDtypeStruct(o, F32) for o in outs],
        in_specs=in_specs,
        out_specs=[VMEM] * len(outs),
        scratch_shapes=list(scratch),
        compiler_params=pltpu.CompilerParams(vmem_limit_bytes=limit << 20),
        cost_estimate=pl.CostEstimate(flops=flops, bytes_accessed=moved, transcendentals=0),
    )


def outer(a, b, precision=HIGH):
    return lax.dot_general(
        a, b, (((0,), (0,)), ((), ())), precision=precision, preferred_element_type=F32
    )


def project(place, index, table, volume, out):
    depth, cols, _ = volume.shape
    rows = table.shape[1]
    picker = (
        lax.broadcasted_iota(jnp.int32, (rows, index.shape[1]), 0) == index[...]
    ).astype(F32)
    flipped = jnp.dot(table[...], picker, precision=HIGH, preferred_element_type=F32)
    row = lax.broadcasted_iota(jnp.int32, (depth, LANES), 0)
    lane = lax.broadcasted_iota(jnp.int32, (depth, LANES), 1)
    shifted = outer(flipped, (lane == row + place[0] * depth).astype(F32))
    weights = outer(flipped, (lane == row).astype(F32))[:, :depth]
    for chunk in range(out.shape[0]):
        out[chunk, cols] = shifted
    for base in range(0, cols, 8):
        block = jnp.swapaxes(volume[:, base : base + 8, :], 0, 1)
        for k in range(8):
            part = jnp.dot(weights, block[k], precision=HIGH, preferred_element_type=F32)
            for chunk in range(out.shape[0]):
                out[chunk, base + k] = part[:, chunk * LANES : (chunk + 1) * LANES]


def gather_parts(parts, low, high, weights):
    cols = parts.shape[1] - 1
    half = cols // 2

    def total(k):
        return (parts[0, k] + parts[1, k]) + (parts[2, k] + parts[3, k])

    for k in range(half):
        low[k] = total(k)
        high[k] = total(half + k)
    weights[...] = total(cols)


def turn(place, measured, out):
    out[...] = jnp.swapaxes(measured[0], 0, 1)


def residual(shift, left, low, high, right, measured, frac, down, center, up, field, ext, grad):
    cols, angles, width = measured.shape
    ext[0:HALO] = left[...]
    ext[HALO : 2 * HALO] = low[...]
    ext[2 * HALO : 3 * HALO] = high[...]
    ext[3 * HALO :] = right[...]
    grad[...] = jnp.zeros_like(grad)
    for k in range(cols):
        at = k + HALO + shift[0, k]
        lower, upper = ext[at], ext[at + 1]
        part = frac[k : k + 1, :]
        rest = 1.0 - part
        resid = (rest * lower + part * upper) - measured[k]
        field[k : k + 1, :] = jnp.sum(resid * (upper - lower), axis=0, keepdims=True)
        grad[at] = grad[at] + rest * resid
        grad[at + 1] = grad[at + 1] + part * resid
    center[...] = grad[HALO : HALO + cols]
    down[0:HALO] = grad[0:HALO]
    up[0:HALO] = grad[HALO + cols :]
    down[HALO] = jnp.zeros((angles, width), F32)
    up[HALO] = jnp.zeros((angles, width), F32)
    down[HALO, 0:EDGE, :] = field[0:EDGE, :]
    up[HALO, 0:EDGE, :] = field[cols - EDGE : cols, :]


def land(center, left, right, weights, field, out, wide):
    cols = center.shape[0]
    out[0:HALO] = center[0:HALO] + left[0:HALO]
    out[HALO:cols] = center[HALO:cols] + right[0:HALO]
    out[cols] = weights[...]
    wide[0:EDGE] = left[HALO, 0:EDGE, :]
    wide[EDGE : EDGE + cols] = field[...]
    wide[EDGE + cols : cols + 2 * EDGE] = right[HALO, 0:EDGE, :]
    wide[cols + 2 * EDGE :] = jnp.zeros((wide.shape[0] - cols - 2 * EDGE, wide.shape[1]), F32)


def spread(place, own, other, wide, out):
    cols = own.shape[0] - 1
    depth = out.shape[2]
    first = place[1] == 0

    def both(k):
        a, b = own[k], other[k]
        return jnp.concatenate([jnp.where(first, a, b), jnp.where(first, b, a)], axis=0)

    weights = both(cols)
    for k in range(0, cols, 2):
        pair = jnp.concatenate([both(k), both(k + 1)], axis=1)
        value = outer(weights, pair)
        for chunk in range(out.shape[0]):
            rows = value[chunk * depth : (chunk + 1) * depth]
            out[chunk, k] = rows[:, :LANES]
            out[chunk, k + 1] = rows[:, LANES:]
    for chunk in range(out.shape[0]):
        out[chunk, cols] = wide[0:depth]
        out[chunk, cols + 1] = wide[depth:]


def finish(place, last, parts, image, field):
    chunks, rows, depth, width = parts.shape
    cols = rows - 2
    for chunk in range(chunks):
        for base in range(0, cols, 8):
            block = jnp.swapaxes(parts[chunk, base : base + 8], 0, 1)
            image[:, base : base + 8, chunk * width : (chunk + 1) * width] = block
    wide = jnp.concatenate(
        [jnp.concatenate([parts[c, cols], parts[c, cols + 1]], axis=0) for c in range(chunks)],
        axis=1,
    )[: cols + 2 * EDGE]
    height, total = wide.shape
    row = lax.broadcasted_iota(jnp.int32, wide.shape, 0)
    lane = lax.broadcasted_iota(jnp.int32, wide.shape, 1)
    outside = ((row < EDGE) & (place[2] == 0)) | ((row >= EDGE + cols) & (place[2] == last))
    for _ in range(ITS):
        after = pltpu.roll(wide, height - 1, 0)
        before = pltpu.roll(wide, 1, 0)
        right = jnp.where(lane == total - 1, 0.0, pltpu.roll(wide, total - 1, 1))
        left = jnp.where(lane == 0, 0.0, pltpu.roll(wide, 1, 1))
        laplace = after + before + right + left - 4.0 * wide
        wide = jnp.where(outside, 0.0, wide + DIFFUSION * laplace)
    field[0] = wide[EDGE : EDGE + cols]


def shifted(block, distance):
    count = lax.axis_size("tile")
    route = [(i, i + distance) for i in range(count) if 0 <= i + distance < count]
    return lax.ppermute(block, "tile", route)


def body(volume, frac, shift, angle_index, depth_weights, measured):
    depth, cols, height = volume.shape
    angles = angle_index.shape[1]
    slabs = lax.axis_size("slab")
    slab = lax.axis_index("slab")
    place = jnp.stack([slab, lax.axis_index("phase"), lax.axis_index("tile")]).astype(jnp.int32)
    half = (HALO, angles, LANES)
    edge = (HALO + 1, angles, LANES)
    (parts,) = call(
        project, [(slabs, cols + 1, angles, LANES)], [SMEM, VMEM, VMEM, VMEM]
    )(place, angle_index, depth_weights.T, volume)
    parts = lax.all_to_all(parts, "slab", 0, 0, tiled=True)
    low, high, weights = call(gather_parts, [half, half, (angles, LANES)], [VMEM])(parts)
    from_left = shifted(high, 1)
    from_right = shifted(low, -1)
    mine = pl.pallas_call(
        turn,
        out_shape=jax.ShapeDtypeStruct((cols, angles, LANES), F32),
        grid_spec=pltpu.PrefetchScalarGridSpec(
            num_scalar_prefetch=1,
            grid=(1,),
            in_specs=[pl.BlockSpec((1, angles, cols, LANES), lambda i, place: (0, 0, 0, place[0]))],
            out_specs=pl.BlockSpec((cols, angles, LANES), lambda i, place: (0, 0, 0)),
        ),
        cost_estimate=pl.CostEstimate(flops=1 << 20, bytes_accessed=1 << 20, transcendentals=0),
    )(place, measured)
    part = lax.dynamic_slice_in_dim(frac[0], slab * LANES, LANES, axis=1)
    scratch = [pltpu.VMEM((cols + 2 * HALO, angles, LANES), F32)] * 2
    down, center, up, field = call(
        residual,
        [edge, (cols, angles, LANES), edge, (cols, LANES)],
        [SMEM] + [VMEM] * 6,
        scratch,
    )(shift, from_left, low, high, from_right, mine, part)
    left = shifted(up, 1)
    right = shifted(down, -1)
    own, wide = call(
        land, [(cols + 1, angles, LANES), (2 * depth, LANES)], [VMEM] * 5
    )(center, left, right, weights, field)
    phases = lax.axis_size("phase")
    other = lax.ppermute(own, "phase", [(i, phases - 1 - i) for i in range(phases)])
    (parts,) = call(
        spread, [(slabs, cols + 2, depth, LANES)], [SMEM] + [VMEM] * 3
    )(place, own, other, wide)
    parts = lax.all_to_all(parts, "slab", 0, 0, tiled=True)

    def ending(place, parts, image, field):
        finish(place, lax.axis_size("tile") - 1, parts, image, field)

    return call(ending, [(depth, cols, height), (1, cols, height)], [SMEM, VMEM])(place, parts)


def solution(mesh):
    return jax.shard_map(
        body,
        mesh=mesh,
        in_specs=(
            P("slab", "tile", None),
            P("phase", "tile", None),
            P("phase", "tile"),
            P("phase", None),
            P(None, "slab"),
            P("phase", None, "tile", None),
        ),
        out_specs=(P("slab", "tile", None), P("phase", "tile", None)),
        check_vma=False,
    )
```

time: 301 us -> 116 us (0.39)
  the two profiles are of different devices: /device:TPU:128 before, /device:TPU:71 now
where the time goes in v1:
time: 116 us; the launch traced here: 115 us
  blocking collectives  52.2 us (45%)
  waiting for transfers between devices  27.4 us (24%)
  starting transfers between devices  18.9 us (16%)
  Pallas kernels  12 us (10%)
  local copies, waits for them, and re-layouts  4.21 us (4%)
    all_to_all x2, blocking collectives, body(): parts = lax.all_to_all(parts, 'slab', 0, 0, tiled=True)  52.2 us
    ppermute x4, waiting for transfers between devices, shifted(): return lax.ppermute(block, 'tile', route)  20.3 us
    ppermute x4, starting transfers between devices, shifted(): return lax.ppermute(block, 'tile', route)  14.3 us
    ppermute x1, waiting for transfers between devices, body(): lax.ppermute(own, 'phase', [(i, phases - 1 - i) for i in range(phases)])  7.04 us
    ppermute x1, starting transfers between devices, body(): lax.ppermute(own, 'phase', [(i, phases - 1 - i) for i in range(phases)])  4.61 us
    unnamed x16, local copies, waits for them, and re-layouts  4.21 us
    pallas_call x1, Pallas kernels, body(): call(project, [(slabs, cols + 1, angles, LANES)], [SMEM, VMEM, VMEM, VMEM])  3.05 us
    pallas_call x1, Pallas kernels, body(): pl.pallas_call(turn, out_shape=jax.ShapeDtypeStruct((cols, angles, LANES)...  2.74 us
  transfers between devices with their start and end apart: 5, of which 5 were waited for; matrix products, arithmetic and copies ran while one was open for 0% of the time, Pallas kernels for 2%

profile of v1, /device:TPU:71, one launch (start us, length us, event | category | flops | bytes accessed | tf_op | source)
XLA Modules:
  0.0 115.4 jit_solution(9851030255140043469)
XLA Ops:
  0.6 0.0 copy-start
  0.7 0.1 pad_add_fusion.place
  0.7 0.0 copy-start.4
  0.7 0.0 copy-start.1
  0.7 1.6 %copy-done.1 = f32[32,32,512]{2,1,0:T(8,128)S(1)} copy-done((f32[32,32,512]{2,1,0:T(8,128)S(1)}, f32[32,32,512]{2,1,0:T(8,128)}, u32[]{:S(2)}) %copy-start.1) | copy-done | bytes 2097176
  2.3 0.0 copy-start.3
  2.3 0.9 copy-done.3
  3.2 0.0 copy-start.6
  3.2 0.7 copy-done.6
  3.9 3.0 %shard_map.77 = f32[4,33,32,128]{3,2,1,0:T(8,128)S(1)} custom-call(s32[3]{0:T(128)S(1)} %pad_add_fusion.place, s32[1,32]{1,0:T(1,128)S(1)} %copy-done.6, f32[32,680]{1,0:T(8,128)S(1)} %bitcast.6, f32[32,32,512]{2,1,0:T(8,128)S(1)} %copy-done.1), custom_call_target="tpu_custom_call" | custom-call | flops 4194304 | bytes 4194304 | tf_op jit(solution)/shard_map/pallas_call | solution.py:172
  6.9 0.0 copy-done.4
  6.9 29.8 %all_to_all.10.parts = f32[4,33,32,128]{3,2,1,0:T(8,128)S(1)} all-to-all(f32[4,33,32,128]{3,2,1,0:T(8,128)S(1)} %shard_map.77), channel_id=1, replica_groups=mesh['phase'=2,'slab'=4,'tile'=32] {'slab'}, dimensions={0} | all-to-all | bytes 4325376 | tf_op jit(solution)/shard_map/all_to_all | solution.py:175
  36.7 0.0 copy-start.7
  36.8 0.1 shard_map.78
  36.9 8.1 %collective-permute-start = (f32[16,32,128]{2,1,0:T(8,128)S(1)}, f32[16,32,128]{2,1,0:T(8,128)S(1)}, u32[]{:S(2)}, u32[]{:S(2)}) collective-permute-start(f32[16,32,128]{2,1,0:T(8,128)S(1)} %get-tuple-element.11.high), channel_id=1, source_target_pairs={{0,1},{1,2},{2,3},{3,4},{4,5},{5,6},{6,7},{7,8},{8,9},{9,10},{10,1... | collective-permute-start | bytes 786440 | tf_op jit(solution)/shard_map/ppermute | solution.py:161
  44.9 1.9 %collective-permute-start.1 = (f32[16,32,128]{2,1,0:T(8,128)S(1)}, f32[16,32,128]{2,1,0:T(8,128)S(1)}, u32[]{:S(2)}, u32[]{:S(2)}) collective-permute-start(f32[16,32,128]{2,1,0:T(8,128)S(1)} %get-tuple-element.12.low), channel_id=1, source_target_pairs={{1,0},{2,1},{3,2},{4,3},{5,4},{6,5},{7,6},{8,7},{9,8},{10,9},{11,1... | collective-permute-start | bytes 786440 | tf_op jit(solution)/shard_map/ppermute | solution.py:161
  46.9 0.0 copy-start.5
  46.9 2.7 %shard_map.79.measured = f32[32,32,128]{2,1,0:T(8,128)} custom-call(s32[3]{0:T(128)} %copy-done.4, f32[1,32,32,512]{3,2,1,0:T(8,128)} %measured.1), custom_call_target="tpu_custom_call" | custom-call | flops 1048576 | bytes 1048576 | tf_op jit(solution)/shard_map/pallas_call | solution.py:179
  49.6 0.0 copy-done
  49.6 1.3 %collective-permute-done.left = f32[16,32,128]{2,1,0:T(8,128)S(1)} collective-permute-done((f32[16,32,128]{2,1,0:T(8,128)S(1)}, f32[16,32,128]{2,1,0:T(8,128)S(1)}, u32[]{:S(2)}, u32[]{:S(2)}) %collective-permute-start) | collective-permute-done | bytes 262176 | tf_op jit(solution)/shard_map/ppermute | solution.py:161
  50.9 8.6 %collective-permute-done.1.right = f32[16,32,128]{2,1,0:T(8,128)S(1)} collective-permute-done((f32[16,32,128]{2,1,0:T(8,128)S(1)}, f32[16,32,128]{2,1,0:T(8,128)S(1)}, u32[]{:S(2)}, u32[]{:S(2)}) %collective-permute-start.1) | collective-permute-done | bytes 262176 | tf_op jit(solution)/shard_map/ppermute | solution.py:161
  59.5 0.0 copy-done.7
  59.5 0.0 copy-start.2
  59.5 1.0 copy-done.2
  60.6 1.0 shard_map.80
  61.5 1.9 %collective-permute-start.2 = (f32[17,32,128]{2,1,0:T(8,128)S(1)}, f32[17,32,128]{2,1,0:T(8,128)S(1)}, u32[]{:S(2)}, u32[]{:S(2)}) collective-permute-start(f32[17,32,128]{2,1,0:T(8,128)S(1)} %get-tuple-element.14), channel_id=1, source_target_pairs={{0,1},{1,2},{2,3},{3,4},{4,5},{5,6},{6,7},{7,8},{8,9},{9,10},{10,1... | collective-permute-start | bytes 835592 | tf_op jit(solution)/shard_map/ppermute | solution.py:161
  63.5 2.4 %collective-permute-start.3 = (f32[17,32,128]{2,1,0:T(8,128)S(1)}, f32[17,32,128]{2,1,0:T(8,128)S(1)}, u32[]{:S(2)}, u32[]{:S(2)}) collective-permute-start(f32[17,32,128]{2,1,0:T(8,128)S(1)} %get-tuple-element.15), channel_id=1, source_target_pairs={{1,0},{2,1},{3,2},{4,3},{5,4},{6,5},{7,6},{8,7},{9,8},{10,9},{11,1... | collective-permute-start | bytes 835592 | tf_op jit(solution)/shard_map/ppermute | solution.py:161
  65.9 2.0 %collective-permute-done.2.left = f32[17,32,128]{2,1,0:T(8,128)S(1)} collective-permute-done((f32[17,32,128]{2,1,0:T(8,128)S(1)}, f32[17,32,128]{2,1,0:T(8,128)S(1)}, u32[]{:S(2)}, u32[]{:S(2)}) %collective-permute-start.2) | collective-permute-done | bytes 278560 | tf_op jit(solution)/shard_map/ppermute | solution.py:161
  67.9 8.4 %collective-permute-done.3.right = f32[17,32,128]{2,1,0:T(8,128)S(1)} collective-permute-done((f32[17,32,128]{2,1,0:T(8,128)S(1)}, f32[17,32,128]{2,1,0:T(8,128)S(1)}, u32[]{:S(2)}, u32[]{:S(2)}) %collective-permute-start.3) | collective-permute-done | bytes 278560 | tf_op jit(solution)/shard_map/ppermute | solution.py:161
  76.3 0.1 shard_map.81
  76.4 4.6 %collective-permute-start.4 = (f32[33,32,128]{2,1,0:T(8,128)S(1)}, f32[33,32,128]{2,1,0:T(8,128)S(1)}, u32[]{:S(2)}, u32[]{:S(2)}) collective-permute-start(f32[33,32,128]{2,1,0:T(8,128)S(1)} %get-tuple-element.18.own), channel_id=1, source_target_pairs={{0,128},{128,0},{1,129},{129,1},{2,130},{130,2},{3,131},{131,3},{4... | collective-permute-start | bytes 1622024 | tf_op jit(solution)/shard_map/ppermute | solution.py:204
  81.0 7.0 %collective-permute-done.4.other = f32[33,32,128]{2,1,0:T(8,128)S(1)} collective-permute-done((f32[33,32,128]{2,1,0:T(8,128)S(1)}, f32[33,32,128]{2,1,0:T(8,128)S(1)}, u32[]{:S(2)}, u32[]{:S(2)}) %collective-permute-start.4) | collective-permute-done | bytes 540704 | tf_op jit(solution)/shard_map/ppermute | solution.py:204
  88.0 0.0 copy-done.5
  88.0 2.4 %shard_map.82 = f32[4,34,32,128]{3,2,1,0:T(8,128)S(1)} custom-call(s32[3]{0:T(128)S(1)} %copy-done.5, f32[33,32,128]{2,1,0:T(8,128)S(1)} %get-tuple-element.18.own, f32[33,32,128]{2,1,0:T(8,128)S(1)} %collective-permute-done.4.other, f32[64,128]{1,0:T(8,128)S(1)} %get-tuple-element.19.wide), custom_call_target="tpu_custom_call" | custom-call | flops 4194304 | bytes 4194304 | tf_op jit(solution)/shard_map/pallas_call | solution.py:205
  90.4 22.4 %all_to_all.11.parts = f32[4,34,32,128]{3,2,1,0:T(8,128)S(1)} all-to-all(f32[4,34,32,128]{3,2,1,0:T(8,128)S(1)} %shard_map.82), channel_id=1, replica_groups=mesh['phase'=2,'slab'=4,'tile'=32] {'slab'}, dimensions={0} | all-to-all | bytes 4456448 | tf_op jit(solution)/shard_map/all_to_all | solution.py:208
  112.8 2.6 %shard_map.83 = (f32[32,32,512]{2,1,0:T(8,128)}, f32[1,32,512]{2,1,0:T(8,128)}) custom-call(s32[3]{0:T(128)S(1)} %copy-done.5, f32[4,34,32,128]{3,2,1,0:T(8,128)S(1)} %all_to_all.11.parts), custom_call_target="tpu_custom_call" | custom-call | flops 4194304 | bytes 4194304 | tf_op jit(solution)/shard_map/pallas_call | solution.py:213
  (1 shorter events, 0.0 us)
Async XLA Ops:
  0.6 49.0 %copy-start = (f32[1,32,512]{2,1,0:T(8,128)S(1)}, f32[1,32,512]{2,1,0:T(8,128)}, u32[]{:S(2)}) copy-start(f32[1,32,512]{2,1,0:T(8,128)} %param.7) | copy-start | bytes 196612
  0.7 6.2 %copy-start.4 = (s32[3]{0:T(128)}, s32[3]{0:T(128)S(1)}, u32[]{:S(2)}) copy-start(s32[3]{0:T(128)S(1)} %pad_add_fusion.place) | copy-start | bytes 40
  0.7 1.6 %copy-start.1 = (f32[32,32,512]{2,1,0:T(8,128)S(1)}, f32[32,32,512]{2,1,0:T(8,128)}, u32[]{:S(2)}) copy-start(f32[32,32,512]{2,1,0:T(8,128)} %volume.1) | copy-start | bytes 6291460
  2.3 0.9 copy-start.3
  3.2 0.7 copy-start.6
  36.7 22.8 %copy-start.7 = (s32[1,32]{1,0:T(1,128)S(1)}, s32[1,32]{1,0:T(1,128)}, u32[]{:S(2)}) copy-start(s32[1,32]{1,0:T(1,128)} %shift.1) | copy-start | bytes 388
  36.9 14.1 %collective-permute-start = (f32[16,32,128]{2,1,0:T(8,128)S(1)}, f32[16,32,128]{2,1,0:T(8,128)S(1)}, u32[]{:S(2)}, u32[]{:S(2)}) collective-permute-start(f32[16,32,128]{2,1,0:T(8,128)S(1)} %get-tuple-element.11.high), channel_id=1, source_target_pairs={{0,1},{1,2},{2,3},{3,4},{4,5},{5,6},{6,7},{7,8},{8,9},{9,10},{10,1... | collective-permute-start | bytes 786440 | tf_op jit(solution)/shard_map/ppermute | solution.py:161
  44.9 14.6 %collective-permute-start.1 = (f32[16,32,128]{2,1,0:T(8,128)S(1)}, f32[16,32,128]{2,1,0:T(8,128)S(1)}, u32[]{:S(2)}, u32[]{:S(2)}) collective-permute-start(f32[16,32,128]{2,1,0:T(8,128)S(1)} %get-tuple-element.12.low), channel_id=1, source_target_pairs={{1,0},{2,1},{3,2},{4,3},{5,4},{6,5},{7,6},{8,7},{9,8},{10,9},{11,1... | collective-permute-start | bytes 786440 | tf_op jit(solution)/shard_map/ppermute | solution.py:161
  46.9 41.1 %copy-start.5 = (s32[3]{0:T(128)S(1)}, s32[3]{0:T(128)}, u32[]{:S(2)}) copy-start(s32[3]{0:T(128)} %copy-done.4) | copy-start | bytes 40
  59.5 1.0 copy-start.2
  61.5 6.4 %collective-permute-start.2 = (f32[17,32,128]{2,1,0:T(8,128)S(1)}, f32[17,32,128]{2,1,0:T(8,128)S(1)}, u32[]{:S(2)}, u32[]{:S(2)}) collective-permute-start(f32[17,32,128]{2,1,0:T(8,128)S(1)} %get-tuple-element.14), channel_id=1, source_target_pairs={{0,1},{1,2},{2,3},{3,4},{4,5},{5,6},{6,7},{7,8},{8,9},{9,10},{10,1... | collective-permute-start | bytes 835592 | tf_op jit(solution)/shard_map/ppermute | solution.py:161
  63.5 12.8 %collective-permute-start.3 = (f32[17,32,128]{2,1,0:T(8,128)S(1)}, f32[17,32,128]{2,1,0:T(8,128)S(1)}, u32[]{:S(2)}, u32[]{:S(2)}) collective-permute-start(f32[17,32,128]{2,1,0:T(8,128)S(1)} %get-tuple-element.15), channel_id=1, source_target_pairs={{1,0},{2,1},{3,2},{4,3},{5,4},{6,5},{7,6},{8,7},{9,8},{10,9},{11,1... | collective-permute-start | bytes 835592 | tf_op jit(solution)/shard_map/ppermute | solution.py:161
  76.4 11.6 %collective-permute-start.4 = (f32[33,32,128]{2,1,0:T(8,128)S(1)}, f32[33,32,128]{2,1,0:T(8,128)S(1)}, u32[]{:S(2)}, u32[]{:S(2)}) collective-permute-start(f32[33,32,128]{2,1,0:T(8,128)S(1)} %get-tuple-element.18.own), channel_id=1, source_target_pairs={{0,128},{128,0},{1,129},{129,1},{2,130},{130,2},{3,131},{131,3},{4... | collective-permute-start | bytes 1622024 | tf_op jit(solution)/shard_map/ppermute | solution.py:204

commit v2 on v1

v2 whole, which is shorter than its diff:
```python
import jax
import jax.numpy as jnp
from jax import lax
from jax.experimental import pallas as pl
from jax.experimental.pallas import tpu as pltpu
from jax.sharding import PartitionSpec as P

HALO = 16
ITS = 4
DIFFUSION = 0.2
EDGE = 8
ALONE = 8
LANES = 128
HIGH = lax.Precision.HIGHEST
F32 = jnp.float32
VMEM = pl.BlockSpec(memory_space=pltpu.VMEM)
SMEM = pl.BlockSpec(memory_space=pltpu.SMEM)


def call(kernel, outs, in_specs, scratch=(), limit=16, flops=1 << 22, moved=1 << 22):
    return pl.pallas_call(
        kernel,
        out_shape=[jax.ShapeDtypeStruct(o, F32) for o in outs],
        in_specs=in_specs,
        out_specs=[VMEM] * len(outs),
        scratch_shapes=list(scratch),
        compiler_params=pltpu.CompilerParams(vmem_limit_bytes=limit << 20),
        cost_estimate=pl.CostEstimate(flops=flops, bytes_accessed=moved, transcendentals=0),
    )


def outer(a, b, precision=HIGH):
    return lax.dot_general(
        a, b, (((0,), (0,)), ((), ())), precision=precision, preferred_element_type=F32
    )


def cut(place, volume, out):
    out[0, 0 : volume.shape[1]] = jnp.swapaxes(volume[...], 0, 1)


def pick(place, index, other, table, partial, out):
    depth, rows = table.shape
    angles = index.shape[1]
    number = lax.broadcasted_iota(jnp.int32, (rows, angles), 0)
    row = lax.broadcasted_iota(jnp.int32, (depth, LANES), 0)
    lane = lax.broadcasted_iota(jnp.int32, (depth, LANES), 1)
    target = (lane == row + place[0] * depth).astype(F32)
    for k, name in enumerate((index, other)):
        picker = (number == name[...]).astype(F32)
        flipped = jnp.dot(table[...], picker, precision=HIGH, preferred_element_type=F32)
        weights = outer(flipped, target)
        for chunk in range(out.shape[0]):
            out[chunk, HALO + k] = weights


def project(parts, own, other, weights):
    slabs = parts.shape[0]
    angles = own.shape[1]

    def over(k):
        return jnp.concatenate([parts[s, k] for s in range(slabs)], axis=0)

    def total(k):
        return (parts[0, k] + parts[1, k]) + (parts[2, k] + parts[3, k])

    table = jnp.concatenate([total(HALO), total(HALO + 1)], axis=0)
    weights[...] = table
    for k in range(0, HALO, 2):
        pair = jnp.concatenate([over(k), over(k + 1)], axis=1)
        value = jnp.dot(table, pair, precision=HIGH, preferred_element_type=F32)
        own[k] = value[:angles, :LANES]
        own[k + 1] = value[:angles, LANES:]
        other[k] = value[angles:, :LANES]
        other[k + 1] = value[angles:, LANES:]


def turn(place, measured, out):
    out[...] = jnp.swapaxes(measured[0], 0, 1)


def residual(place, shift, own, partner, same, crossed, measured, frac, down, center, up, field, ext, grad):
    cols, angles, width = measured.shape
    phase = place[1]
    ext[pl.ds(HALO * (1 + phase), HALO)] = own[...]
    ext[pl.ds(HALO * (2 - phase), HALO)] = partner[...]
    ext[pl.ds(3 * HALO * (1 - phase), HALO)] = same[...]
    ext[pl.ds(3 * HALO * phase, HALO)] = crossed[...]
    grad[...] = jnp.zeros_like(grad)
    for k in range(cols):
        at = k + HALO + shift[0, k]
        lower, upper = ext[at], ext[at + 1]
        part = frac[k : k + 1, :]
        rest = 1.0 - part
        resid = (rest * lower + part * upper) - measured[k]
        field[k : k + 1, :] = jnp.sum(resid * (upper - lower), axis=0, keepdims=True)
        grad[at] = grad[at] + rest * resid
        grad[at + 1] = grad[at + 1] + part * resid
    center[...] = grad[HALO : HALO + cols]
    down[0:HALO] = grad[0:HALO]
    up[0:HALO] = grad[HALO + cols :]
    down[HALO] = jnp.zeros((angles, width), F32)
    up[HALO] = jnp.zeros((angles, width), F32)
    down[HALO, 0:EDGE, :] = field[0:EDGE, :]
    up[HALO, 0:EDGE, :] = field[cols - EDGE : cols, :]


def land(place, center, left, right, field, out, alone, shared, wide):
    cols = center.shape[0]
    out[0:HALO] = center[0:HALO] + left[0:HALO]
    out[HALO:cols] = center[HALO:cols] + right[0:HALO]
    alone[...] = out[pl.ds((cols - ALONE) * (1 - place[1]), ALONE)]
    shared[...] = out[ALONE : cols - ALONE]
    wide[0:EDGE] = left[HALO, 0:EDGE, :]
    wide[EDGE : EDGE + cols] = field[...]
    wide[EDGE + cols : cols + 2 * EDGE] = right[HALO, 0:EDGE, :]
    wide[cols + 2 * EDGE :] = jnp.zeros((wide.shape[0] - cols - 2 * EDGE, wide.shape[1]), F32)


def spread(weights, both, cols, out):
    depth = out.shape[2]
    for k in range(0, cols, 2):
        pair = jnp.concatenate([both(k), both(k + 1)], axis=1)
        value = outer(weights, pair)
        for chunk in range(out.shape[0]):
            rows = value[chunk * depth : (chunk + 1) * depth]
            out[chunk, k] = rows[:, :LANES]
            out[chunk, k + 1] = rows[:, LANES:]


def spread_alone(place, weights, own, other, out):
    base = (own.shape[0] - ALONE) * place[1]

    def both(k):
        return jnp.concatenate([own[base + k], other[k]], axis=0)

    spread(weights[...], both, ALONE, out)


def spread_shared(place, weights, own, other, wide, out):
    cols = other.shape[0]
    angles = own.shape[1]
    depth = out.shape[2]
    first = place[1] == 0

    def order(a, b):
        return jnp.concatenate([jnp.where(first, a, b), jnp.where(first, b, a)], axis=0)

    def both(k):
        return order(own[ALONE + k], other[k])

    spread(order(weights[0:angles], weights[angles:]), both, cols, out)
    for chunk in range(out.shape[0]):
        out[chunk, cols] = wide[0:depth]
        out[chunk, cols + 1] = wide[depth:]


def finish(place, last, mine, theirs, parts, image, field):
    chunks, rows, depth, width = parts.shape
    middle = rows - 2
    cols = image.shape[1]
    near = pl.multiple_of((cols - ALONE) * place[1], 8)
    far = pl.multiple_of((cols - ALONE) * (1 - place[1]), 8)
    for chunk in range(chunks):
        lanes = slice(chunk * width, (chunk + 1) * width)
        image[:, pl.ds(near, ALONE), lanes] = jnp.swapaxes(mine[chunk], 0, 1)
        image[:, pl.ds(far, ALONE), lanes] = jnp.swapaxes(theirs[chunk], 0, 1)
        for base in range(0, middle, 8):
            block = jnp.swapaxes(parts[chunk, base : base + 8], 0, 1)
            image[:, ALONE + base : ALONE + base + 8, lanes] = block
    wide = jnp.concatenate(
        [
            jnp.concatenate([parts[c, middle], parts[c, middle + 1]], axis=0)
            for c in range(chunks)
        ],
        axis=1,
    )[: cols + 2 * EDGE]
    height, total = wide.shape
    row = lax.broadcasted_iota(jnp.int32, wide.shape, 0)
    lane = lax.broadcasted_iota(jnp.int32, wide.shape, 1)
    outside = ((row < EDGE) & (place[2] == 0)) | ((row >= EDGE + cols) & (place[2] == last))
    for _ in range(ITS):
        after = pltpu.roll(wide, height - 1, 0)
        before = pltpu.roll(wide, 1, 0)
        right = jnp.where(lane == total - 1, 0.0, pltpu.roll(wide, total - 1, 1))
        left = jnp.where(lane == 0, 0.0, pltpu.roll(wide, 1, 1))
        laplace = after + before + right + left - 4.0 * wide
        wide = jnp.where(outside, 0.0, wide + DIFFUSION * laplace)
    field[0] = wide[EDGE : EDGE + cols]


def move(block, target):
    phases, tiles = lax.axis_size("phase"), lax.axis_size("tile")
    route = []
    for phase in range(phases):
        for tile in range(tiles):
            to_phase, to_tile = target(phase, tile)
            if 0 <= to_tile < tiles:
                route.append((phase * tiles + tile, to_phase * tiles + to_tile))
    return lax.ppermute(block, ("phase", "tile"), route)


def body(volume, frac, shift, angle_index, depth_weights, measured):
    depth, cols, height = volume.shape
    angles = angle_index.shape[1]
    slabs = lax.axis_size("slab")
    slab = lax.axis_index("slab")
    place = jnp.stack([slab, lax.axis_index("phase"), lax.axis_index("tile")]).astype(jnp.int32)
    half = (HALO, angles, LANES)
    edge = (HALO + 1, angles, LANES)
    message = (slabs, HALO + 2, depth, LANES)

    def partner(block):
        return move(block, lambda phase, tile: (1 - phase, tile))

    def away(phase, tile):
        return tile + 2 * phase - 1

    other_index = partner(angle_index)
    cuts = pl.pallas_call(
        cut,
        out_shape=jax.ShapeDtypeStruct(message, F32),
        grid_spec=pltpu.PrefetchScalarGridSpec(
            num_scalar_prefetch=1,
            grid=(slabs,),
            in_specs=[pl.BlockSpec((depth, HALO, LANES), lambda i, place: (0, place[1], i))],
            out_specs=pl.BlockSpec((1,) + message[1:], lambda i, place: (i, 0, 0, 0)),
        ),
        cost_estimate=pl.CostEstimate(flops=1 << 20, bytes_accessed=1 << 22, transcendentals=0),
    )(place, volume)
    message_out = pl.pallas_call(
        pick,
        out_shape=jax.ShapeDtypeStruct(message, F32),
        in_specs=[SMEM, VMEM, VMEM, VMEM, VMEM],
        out_specs=VMEM,
        input_output_aliases={4: 0},
        compiler_params=pltpu.CompilerParams(vmem_limit_bytes=16 << 20),
    )(place, angle_index, other_index, depth_weights.T, cuts)
    parts = lax.all_to_all(message_out, "slab", 0, 0, tiled=True)
    own, other, weights = call(project, [half, half, (2 * angles, LANES)], [VMEM])(parts)
    crossed = move(other, lambda phase, tile: (1 - phase, away(phase, tile)))
    same = move(own, lambda phase, tile: (phase, away(phase, tile)))
    across = partner(other)
    mine = pl.pallas_call(
        turn,
        out_shape=jax.ShapeDtypeStruct((cols, angles, LANES), F32),
        grid_spec=pltpu.PrefetchScalarGridSpec(
            num_scalar_prefetch=1,
            grid=(1,),
            in_specs=[pl.BlockSpec((1, angles, cols, LANES), lambda i, place: (0, 0, 0, place[0]))],
            out_specs=pl.BlockSpec((cols, angles, LANES), lambda i, place: (0, 0, 0)),
        ),
        cost_estimate=pl.CostEstimate(flops=1 << 20, bytes_accessed=1 << 20, transcendentals=0),
    )(place, measured)
    part = lax.dynamic_slice_in_dim(frac[0], slab * LANES, LANES, axis=1)
    scratch = [pltpu.VMEM((cols + 2 * HALO, angles, LANES), F32)] * 2
    down, center, up, field = call(
        residual,
        [edge, (cols, angles, LANES), edge, (cols, LANES)],
        [SMEM] * 2 + [VMEM] * 6,
        scratch,
    )(place, shift, own, across, same, crossed, mine, part)
    left = move(up, lambda phase, tile: (phase, tile + 1))
    right = move(down, lambda phase, tile: (phase, tile - 1))
    alone = (ALONE, angles, LANES)
    shared = (cols - 2 * ALONE, angles, LANES)
    adjoint, alone_out, shared_out, wide = call(
        land,
        [(cols, angles, LANES), alone, shared, (2 * depth, LANES)],
        [SMEM] + [VMEM] * 4,
    )(place, center, left, right, field)
    alone_in = partner(alone_out)
    shared_in = partner(shared_out)
    (first,) = call(spread_alone, [(slabs, ALONE, depth, LANES)], [SMEM] + [VMEM] * 3)(
        place, weights, adjoint, alone_in
    )
    near = lax.all_to_all(first, "slab", 0, 0, tiled=True)
    far = partner(near)
    (second,) = call(
        spread_shared, [(slabs, shared[0] + 2, depth, LANES)], [SMEM] + [VMEM] * 4
    )(place, weights, adjoint, shared_in, wide)
    middle = lax.all_to_all(second, "slab", 0, 0, tiled=True)

    def ending(place, near, far, middle, image, field):
        finish(place, lax.axis_size("tile") - 1, near, far, middle, image, field)

    return call(ending, [(depth, cols, height), (1, cols, height)], [SMEM] + [VMEM] * 3)(
        place, near, far, middle
    )


def solution(mesh):
    return jax.shard_map(
        body,
        mesh=mesh,
        in_specs=(
            P("slab", "tile", None),
            P("phase", "tile", None),
            P("phase", "tile"),
            P("phase", None),
            P(None, "slab"),
            P("phase", None, "tile", None),
        ),
        out_specs=(P("slab", "tile", None), P("phase", "tile", None)),
        check_vma=False,
    )
```

time: 116 us -> 111 us (0.957)
  blocking collectives: 52.2 us -> 19 us
  waiting for transfers between devices: 27.4 us -> 40.1 us
  starting transfers between devices: 18.9 us -> 30.1 us
  Pallas kernels: 12 us -> 18 us
  local copies, waits for them, and re-layouts: 4.21 us -> 2.34 us
    all_to_all x2 -> x1, blocking collectives: 52.2 us -> 19 us  [body(): parts = lax.all_to_all(message_out, 'slab', 0, 0, tiled=True)]
    ppermute x5 -> x9, waiting for transfers between devices: 27.4 us -> 37.7 us  [move(): return lax.ppermute(block, ('phase', 'tile'), route)]
    all_to_all x0 -> x2, starting transfers between devices: none -> 7.88 us  [the longest x1 4.41 us: body(): middle = lax.all_to_all(second, 'slab', 0, 0, tiled=True)]
    pallas_call x5 -> x7, Pallas kernels: 8.25 us -> 14.3 us  [the longest x1 4.27 us: body(): pl.pallas_call(cut, out_shape=jax.ShapeDtypeStruct(message, F32), grid_sp...]
    ppermute x5 -> x9, starting transfers between devices: 18.9 us -> 22.2 us  [move(): return lax.ppermute(block, ('phase', 'tile'), route)]
    all_to_all x0 -> x2, waiting for transfers between devices: none -> 2.42 us  [the longest x1 2.41 us: body(): middle = lax.all_to_all(second, 'slab', 0, 0, tiled=True)]
    unnamed x16, local copies, waits for them, and re-layouts: 4.21 us -> 2.34 us
  transfers between devices with their start and end apart: 5 -> 11, of which waited for: 5 -> 8; matrix products, arithmetic and copies ran while one was open for 0% -> 1% of each run, Pallas kernels for 2% -> 9%
where the time goes in v2:
time: 111 us
  waiting for transfers between devices  40.1 us (36%)
  starting transfers between devices  30.1 us (27%)
  blocking collectives  19 us (17%)
  Pallas kernels  18 us (16%)
  local copies, waits for them, and re-layouts  2.34 us (2%)
    ppermute x9, waiting for transfers between devices, move(): return lax.ppermute(block, ('phase', 'tile'), route)  37.7 us
    ppermute x9, starting transfers between devices, move(): return lax.ppermute(block, ('phase', 'tile'), route)  22.2 us
    all_to_all x1, blocking collectives, body(): parts = lax.all_to_all(message_out, 'slab', 0, 0, tiled=True)  19 us
    all_to_all x1, starting transfers between devices, body(): middle = lax.all_to_all(second, 'slab', 0, 0, tiled=True)  4.41 us
    pallas_call x1, Pallas kernels, body(): pl.pallas_call(cut, out_shape=jax.ShapeDtypeStruct(message, F32), grid_sp...  4.27 us
    all_to_all x1, starting transfers between devices, body(): near = lax.all_to_all(first, 'slab', 0, 0, tiled=True)  3.47 us
    pallas_call x1, Pallas kernels, body(): pl.pallas_call(turn, out_shape=jax.ShapeDtypeStruct((cols, angles, LANES)...  2.73 us
    pallas_call x1, Pallas kernels, body(): call(ending, [(depth, cols, height), (1, cols, height)], [SMEM] + [VMEM]...  2.64 us
  transfers between devices with their start and end apart: 11, of which 8 were waited for; matrix products, arithmetic and copies ran while one was open for 1% of the time, Pallas kernels for 9%

profile of v2, /device:TPU:71, one launch (start us, length us, event | category | flops | bytes accessed | tf_op | source)
XLA Modules:
  0.0 110.9 jit_solution(12169254427528658875)
XLA Ops:
  0.6 0.0 copy-start
  0.6 1.7 %collective-permute-start = (s32[1,32]{1,0:T(1,128)}, s32[1,32]{1,0:T(1,128)S(1)}, u32[]{:S(2)}, u32[]{:S(2)}) collective-permute-start(s32[1,32]{1,0:T(1,128)} %index.1), channel_id=1, source_target_pairs={{0,128},{1,129},{2,130},{3,131},{4,132},{5,133},{6,134},{7,135},{8... | collective-permute-start | bytes 392 | tf_op jit(solution)/shard_map/ppermute | solution.py:200
  2.4 0.6 pad_add_fusion.place
  3.0 0.0 copy-start.3
  3.0 0.0 copy-start.4
  3.0 0.0 copy-start.6
  3.0 4.3 %shard_map.77.partial = f32[4,18,32,128]{3,2,1,0:T(8,128)} custom-call(s32[3]{0:T(128)} %pad_add_fusion.place, f32[32,32,512]{2,1,0:T(8,128)} %volume.1), custom_call_target="tpu_custom_call" | custom-call | flops 1048576 | bytes 4194304 | tf_op jit(solution)/shard_map/pallas_call | solution.py:220
  7.2 0.0 collective-permute-done.other
  7.2 0.0 copy-done.3
  7.2 0.0 copy-done.4
  7.3 0.0 copy-done.6
  7.3 0.0 copy-start.1
  7.3 1.3 %copy-done.1 = f32[4,18,32,128]{3,2,1,0:T(8,128)S(1)} copy-done((f32[4,18,32,128]{3,2,1,0:T(8,128)S(1)}, f32[4,18,32,128]{3,2,1,0:T(8,128)}, u32[]{:S(2)}) %copy-start.1) | copy-done | bytes 1179672
  8.5 1.6 %shard_map.78 = f32[4,18,32,128]{3,2,1,0:T(8,128)S(1)} custom-call(s32[3]{0:T(128)S(1)} %copy-done.4, s32[1,32]{1,0:T(1,128)S(1)} %copy-done.6, s32[1,32]{1,0:T(1,128)S(1)} %collective-permute-done.other, f32[32,680]{1,0:T(8,128)S(1)} %bitcast.6, f32[4,18,32,128]{3,2,1,0:T(8,128)S(1)} %copy-done.1), custom_call_target="tpu_custom_call", output_to_operand_aliasing={{}: (4, {})} | custom-call | tf_op jit(solution)/shard_map/pallas_call | solution.py:231
  10.1 19.0 %all_to_all.15.parts = f32[4,18,32,128]{3,2,1,0:T(8,128)S(1)} all-to-all(f32[4,18,32,128]{3,2,1,0:T(8,128)S(1)} %shard_map.78), channel_id=1, replica_groups=mesh['phase'=2,'slab'=4,'tile'=32] {'slab'}, dimensions={0} | all-to-all | bytes 2359296 | tf_op jit(solution)/shard_map/all_to_all | solution.py:239
  29.1 0.6 shard_map.79
  29.7 4.4 %collective-permute-start.2 = (f32[16,32,128]{2,1,0:T(8,128)S(1)}, f32[16,32,128]{2,1,0:T(8,128)S(1)}, u32[]{:S(2)}, u32[]{:S(2)}) collective-permute-start(f32[16,32,128]{2,1,0:T(8,128)S(1)} %get-tuple-element.14.own), channel_id=1, source_target_pairs={{1,0},{2,1},{3,2},{4,3},{5,4},{6,5},{7,6},{8,7},{9,8},{10,9},{11,1... | collective-permute-start | bytes 786440 | tf_op jit(solution)/shard_map/ppermute | solution.py:200
  34.1 1.9 %collective-permute-start.3 = (f32[16,32,128]{2,1,0:T(8,128)S(1)}, f32[16,32,128]{2,1,0:T(8,128)S(1)}, u32[]{:S(2)}, u32[]{:S(2)}) collective-permute-start(f32[16,32,128]{2,1,0:T(8,128)S(1)} %get-tuple-element.15), channel_id=1, source_target_pairs={{1,128},{2,129},{3,130},{4,131},{5,132},{6,133},{7,134},{8,135},{9... | collective-permute-start | bytes 786440 | tf_op jit(solution)/shard_map/ppermute | solution.py:200
  36.0 3.9 %collective-permute-start.1 = (f32[16,32,128]{2,1,0:T(8,128)S(1)}, f32[16,32,128]{2,1,0:T(8,128)S(1)}, u32[]{:S(2)}, u32[]{:S(2)}) collective-permute-start(f32[16,32,128]{2,1,0:T(8,128)S(1)} %get-tuple-element.15), channel_id=1, source_target_pairs={{0,128},{1,129},{2,130},{3,131},{4,132},{5,133},{6,134},{7,135},{8... | collective-permute-start | bytes 786440 | tf_op jit(solution)/shard_map/ppermute | solution.py:200
  40.0 0.0 copy-start.7
  40.0 2.7 %shard_map.80.measured = f32[32,32,128]{2,1,0:T(8,128)} custom-call(s32[3]{0:T(128)} %pad_add_fusion.place, f32[1,32,32,512]{3,2,1,0:T(8,128)} %measured.1), custom_call_target="tpu_custom_call" | custom-call | flops 1048576 | bytes 1048576 | tf_op jit(solution)/shard_map/pallas_call | solution.py:244
  42.7 0.0 copy-done
  42.7 0.0 collective-permute-done.2.same
  42.7 0.9 collective-permute-done.3.crossed
  43.6 5.6 %collective-permute-done.1.partner = f32[16,32,128]{2,1,0:T(8,128)S(1)} collective-permute-done((f32[16,32,128]{2,1,0:T(8,128)S(1)}, f32[16,32,128]{2,1,0:T(8,128)S(1)}, u32[]{:S(2)}, u32[]{:S(2)}) %collective-permute-start.1) | collective-permute-done | bytes 262176 | tf_op jit(solution)/shard_map/ppermute | solution.py:200
  49.3 0.0 copy-done.5
  49.3 0.0 copy-done.7
  49.3 0.0 copy-start.2
  49.3 1.0 copy-done.2
  50.3 1.0 shard_map.81
  51.3 8.2 %collective-permute-start.4 = (f32[17,32,128]{2,1,0:T(8,128)S(1)}, f32[17,32,128]{2,1,0:T(8,128)S(1)}, u32[]{:S(2)}, u32[]{:S(2)}) collective-permute-start(f32[17,32,128]{2,1,0:T(8,128)S(1)} %get-tuple-element.17), channel_id=1, source_target_pairs={{0,1},{1,2},{2,3},{3,4},{4,5},{5,6},{6,7},{7,8},{8,9},{9,10},{10,1... | collective-permute-start | bytes 835592 | tf_op jit(solution)/shard_map/ppermute | solution.py:200
  59.5 1.9 %collective-permute-start.5 = (f32[17,32,128]{2,1,0:T(8,128)S(1)}, f32[17,32,128]{2,1,0:T(8,128)S(1)}, u32[]{:S(2)}, u32[]{:S(2)}) collective-permute-start(f32[17,32,128]{2,1,0:T(8,128)S(1)} %get-tuple-element.18), channel_id=1, source_target_pairs={{1,0},{2,1},{3,2},{4,3},{5,4},{6,5},{7,6},{8,7},{9,8},{10,9},{11,1... | collective-permute-start | bytes 835592 | tf_op jit(solution)/shard_map/ppermute | solution.py:200
  61.4 1.6 %collective-permute-done.4.left = f32[17,32,128]{2,1,0:T(8,128)S(1)} collective-permute-done((f32[17,32,128]{2,1,0:T(8,128)S(1)}, f32[17,32,128]{2,1,0:T(8,128)S(1)}, u32[]{:S(2)}, u32[]{:S(2)}) %collective-permute-start.4) | collective-permute-done | bytes 278560 | tf_op jit(solution)/shard_map/ppermute | solution.py:200
  63.1 10.8 %collective-permute-done.5.right = f32[17,32,128]{2,1,0:T(8,128)S(1)} collective-permute-done((f32[17,32,128]{2,1,0:T(8,128)S(1)}, f32[17,32,128]{2,1,0:T(8,128)S(1)}, u32[]{:S(2)}, u32[]{:S(2)}) %collective-permute-start.5) | collective-permute-done | bytes 278560 | tf_op jit(solution)/shard_map/ppermute | solution.py:200
  73.9 0.6 shard_map.82
  74.5 0.1 collective-permute-start.6
  74.6 5.5 %collective-permute-done.6.other = f32[8,32,128]{2,1,0:T(8,128)S(1)} collective-permute-done((f32[8,32,128]{2,1,0:T(8,128)S(1)}, f32[8,32,128]{2,1,0:T(8,128)S(1)}, u32[]{:S(2)}, u32[]{:S(2)}) %collective-permute-start.6) | collective-permute-done | bytes 131104 | tf_op jit(solution)/shard_map/ppermute | solution.py:200
  80.0 2.0 %shard_map.83 = f32[4,8,32,128]{3,2,1,0:T(8,128)} custom-call(s32[3]{0:T(128)S(1)} %copy-done.5, f32[64,128]{1,0:T(8,128)S(1)} %get-tuple-element.13.weights, f32[32,32,128]{2,1,0:T(8,128)S(1)} %get-tuple-element.20.own, f32[8,32,128]{2,1,0:T(8,128)S(1)} %collective-permute-done.6.other), custom_call_target="tpu_custom_call" | custom-call | flops 4194304 | bytes 4194304 | tf_op jit(solution)/shard_map/pallas_call | solution.py:274
  82.0 3.5 %all-to-all-start.1 = ((f32[4,8,32,128]{3,2,1,0:T(8,128)}), f32[4,8,32,128]{3,2,1,0:T(8,128)S(1)}, u32[]{:S(2)}, u32[]{:S(2)}) async-start(f32[4,8,32,128]{3,2,1,0:T(8,128)} %shard_map.83), calls=%async_computation.1 | async-start | bytes 1048576 | tf_op jit(solution)/shard_map/all_to_all | solution.py:277
  85.5 0.1 collective-permute-start.8
  85.6 5.2 %collective-permute-done.8.other = f32[16,32,128]{2,1,0:T(8,128)S(1)} collective-permute-done((f32[16,32,128]{2,1,0:T(8,128)S(1)}, f32[16,32,128]{2,1,0:T(8,128)S(1)}, u32[]{:S(2)}, u32[]{:S(2)}) %collective-permute-start.8) | collective-permute-done | bytes 262176 | tf_op jit(solution)/shard_map/ppermute | solution.py:200
  90.8 2.6 %shard_map.84 = f32[4,18,32,128]{3,2,1,0:T(8,128)} custom-call(s32[3]{0:T(128)S(1)} %copy-done.5, f32[64,128]{1,0:T(8,128)S(1)} %get-tuple-element.13.weights, f32[32,32,128]{2,1,0:T(8,128)S(1)} %get-tuple-element.20.own, f32[16,32,128]{2,1,0:T(8,128)S(1)} %collective-permute-done.8.other, f32[64,128]{1,0:T(8,128)S(1)} %get-tuple-element.23.wide), custom_call_target="tpu_custom_call" | custom-call | flops 4194304 | bytes 4194304 | tf_op jit(solution)/shard_map/pallas_call | solution.py:279
  93.4 0.0 all-to-all-done.1.near
  93.4 4.4 %all-to-all-start.2 = ((f32[4,18,32,128]{3,2,1,0:T(8,128)}), f32[4,18,32,128]{3,2,1,0:T(8,128)S(1)}, u32[]{:S(2)}, u32[]{:S(2)}) async-start(f32[4,18,32,128]{3,2,1,0:T(8,128)} %shard_map.84), calls=%async_computation.2 | async-start | bytes 2359296 | tf_op jit(solution)/shard_map/all_to_all | solution.py:282
  97.8 0.0 collective-permute-start.7
  97.8 8.0 %collective-permute-done.7.far = f32[4,8,32,128]{3,2,1,0:T(8,128)S(1)} collective-permute-done((f32[4,8,32,128]{3,2,1,0:T(8,128)S(1)}, f32[4,8,32,128]{3,2,1,0:T(8,128)S(1)}, u32[]{:S(2)}, u32[]{:S(2)}) %collective-permute-start.7) | collective-permute-done | bytes 524320 | tf_op jit(solution)/shard_map/ppermute | solution.py:200
  105.8 2.4 %all-to-all-done.2.middle = f32[4,18,32,128]{3,2,1,0:T(8,128)S(1)} async-done(((f32[4,18,32,128]{3,2,1,0:T(8,128)}), f32[4,18,32,128]{3,2,1,0:T(8,128)S(1)}, u32[]{:S(2)}, u32[]{:S(2)}) %all-to-all-start.2) | async-done | bytes 1179680 | tf_op jit(solution)/shard_map/all_to_all | solution.py:282
  108.2 2.6 %shard_map.85 = (f32[32,32,512]{2,1,0:T(8,128)}, f32[1,32,512]{2,1,0:T(8,128)}) custom-call(s32[3]{0:T(128)S(1)} %copy-done.5, f32[4,8,32,128]{3,2,1,0:T(8,128)S(1)} %all-to-all-done.1.near, f32[4,8,32,128]{3,2,1,0:T(8,128)S(1)} %collective-permute-done.7.far, f32[4,18,32,128]{3,2,1,0:T(8,128)S(1)} %all-to-all-done.2.middle), custom_call_target="tpu_custom_call" | custom-call | flops 4194304 | bytes 4194304 | tf_op jit(solution)/shard_map/pallas_call | solution.py:287
  (2 shorter events, 0.0 us)
Async XLA Ops:
  0.6 42.1 %copy-start = (f32[1,32,512]{2,1,0:T(8,128)S(1)}, f32[1,32,512]{2,1,0:T(8,128)}, u32[]{:S(2)}) copy-start(f32[1,32,512]{2,1,0:T(8,128)} %param.7) | copy-start | bytes 196612
  0.6 6.6 %collective-permute-start = (s32[1,32]{1,0:T(1,128)}, s32[1,32]{1,0:T(1,128)S(1)}, u32[]{:S(2)}, u32[]{:S(2)}) collective-permute-start(s32[1,32]{1,0:T(1,128)} %index.1), channel_id=1, source_target_pairs={{0,128},{1,129},{2,130},{3,131},{4,132},{5,133},{6,134},{7,135},{8... | collective-permute-start | bytes 392 | tf_op jit(solution)/shard_map/ppermute | solution.py:200
  3.0 4.3 %copy-start.3 = (f32[680,32]{0,1:T(8,128)S(1)}, f32[680,32]{0,1:T(8,128)}, u32[]{:S(2)}) copy-start(f32[680,32]{0,1:T(8,128)} %param.10) | copy-start | bytes 261124
  3.0 4.3 %copy-start.4 = (s32[3]{0:T(128)S(1)}, s32[3]{0:T(128)}, u32[]{:S(2)}) copy-start(s32[3]{0:T(128)} %pad_add_fusion.place) | copy-start | bytes 40
  3.0 4.3 %copy-start.6 = (s32[1,32]{1,0:T(1,128)S(1)}, s32[1,32]{1,0:T(1,128)}, u32[]{:S(2)}) copy-start(s32[1,32]{1,0:T(1,128)} %index.1) | copy-start | bytes 388
  7.3 1.3 %copy-start.1 = (f32[4,18,32,128]{3,2,1,0:T(8,128)S(1)}, f32[4,18,32,128]{3,2,1,0:T(8,128)}, u32[]{:S(2)}) copy-start(f32[4,18,32,128]{3,2,1,0:T(8,128)} %shard_map.77.partial) | copy-start | bytes 3538948
  29.7 13.0 %collective-permute-start.2 = (f32[16,32,128]{2,1,0:T(8,128)S(1)}, f32[16,32,128]{2,1,0:T(8,128)S(1)}, u32[]{:S(2)}, u32[]{:S(2)}) collective-permute-start(f32[16,32,128]{2,1,0:T(8,128)S(1)} %get-tuple-element.14.own), channel_id=1, source_target_pairs={{1,0},{2,1},{3,2},{4,3},{5,4},{6,5},{7,6},{8,7},{9,8},{10,9},{11,1... | collective-permute-start | bytes 786440 | tf_op jit(solution)/shard_map/ppermute | solution.py:200
  34.1 9.5 %collective-permute-start.3 = (f32[16,32,128]{2,1,0:T(8,128)S(1)}, f32[16,32,128]{2,1,0:T(8,128)S(1)}, u32[]{:S(2)}, u32[]{:S(2)}) collective-permute-start(f32[16,32,128]{2,1,0:T(8,128)S(1)} %get-tuple-element.15), channel_id=1, source_target_pairs={{1,128},{2,129},{3,130},{4,131},{5,132},{6,133},{7,134},{8,135},{9... | collective-permute-start | bytes 786440 | tf_op jit(solution)/shard_map/ppermute | solution.py:200
  36.0 13.2 %collective-permute-start.1 = (f32[16,32,128]{2,1,0:T(8,128)S(1)}, f32[16,32,128]{2,1,0:T(8,128)S(1)}, u32[]{:S(2)}, u32[]{:S(2)}) collective-permute-start(f32[16,32,128]{2,1,0:T(8,128)S(1)} %get-tuple-element.15), channel_id=1, source_target_pairs={{0,128},{1,129},{2,130},{3,131},{4,132},{5,133},{6,134},{7,135},{8... | collective-permute-start | bytes 786440 | tf_op jit(solution)/shard_map/ppermute | solution.py:200
  40.0 9.3 %copy-start.5 = (s32[3]{0:T(128)S(1)}, s32[3]{0:T(128)}, u32[]{:S(2)}) copy-start(s32[3]{0:T(128)} %pad_add_fusion.place) | copy-start | bytes 40
  40.0 9.3 %copy-start.7 = (s32[1,32]{1,0:T(1,128)S(1)}, s32[1,32]{1,0:T(1,128)}, u32[]{:S(2)}) copy-start(s32[1,32]{1,0:T(1,128)} %shift.1) | copy-start | bytes 388
  49.3 1.0 copy-start.2
  51.3 11.8 %collective-permute-start.4 = (f32[17,32,128]{2,1,0:T(8,128)S(1)}, f32[17,32,128]{2,1,0:T(8,128)S(1)}, u32[]{:S(2)}, u32[]{:S(2)}) collective-permute-start(f32[17,32,128]{2,1,0:T(8,128)S(1)} %get-tuple-element.17), channel_id=1, source_target_pairs={{0,1},{1,2},{2,3},{3,4},{4,5},{5,6},{6,7},{7,8},{8,9},{9,10},{10,1... | collective-permute-start | bytes 835592 | tf_op jit(solution)/shard_map/ppermute | solution.py:200
  59.5 14.4 %collective-permute-start.5 = (f32[17,32,128]{2,1,0:T(8,128)S(1)}, f32[17,32,128]{2,1,0:T(8,128)S(1)}, u32[]{:S(2)}, u32[]{:S(2)}) collective-permute-start(f32[17,32,128]{2,1,0:T(8,128)S(1)} %get-tuple-element.18), channel_id=1, source_target_pairs={{1,0},{2,1},{3,2},{4,3},{5,4},{6,5},{7,6},{8,7},{9,8},{10,9},{11,1... | collective-permute-start | bytes 835592 | tf_op jit(solution)/shard_map/ppermute | solution.py:200
  74.5 5.6 %collective-permute-start.6 = (f32[8,32,128]{2,1,0:T(8,128)S(1)}, f32[8,32,128]{2,1,0:T(8,128)S(1)}, u32[]{:S(2)}, u32[]{:S(2)}) collective-permute-start(f32[8,32,128]{2,1,0:T(8,128)S(1)} %get-tuple-element.21), channel_id=1, source_target_pairs={{0,128},{1,129},{2,130},{3,131},{4,132},{5,133},{6,134},{7,135},{8... | collective-permute-start | bytes 393224 | tf_op jit(solution)/shard_map/ppermute | solution.py:200
  82.0 11.4 %all-to-all-start.1 = ((f32[4,8,32,128]{3,2,1,0:T(8,128)}), f32[4,8,32,128]{3,2,1,0:T(8,128)S(1)}, u32[]{:S(2)}, u32[]{:S(2)}) async-start(f32[4,8,32,128]{3,2,1,0:T(8,128)} %shard_map.83), calls=%async_computation.1 | async-start | bytes 1048576 | tf_op jit(solution)/shard_map/all_to_all | solution.py:277
  85.5 5.3 %collective-permute-start.8 = (f32[16,32,128]{2,1,0:T(8,128)S(1)}, f32[16,32,128]{2,1,0:T(8,128)S(1)}, u32[]{:S(2)}, u32[]{:S(2)}) collective-permute-start(f32[16,32,128]{2,1,0:T(8,128)S(1)} %get-tuple-element.22), channel_id=1, source_target_pairs={{0,128},{1,129},{2,130},{3,131},{4,132},{5,133},{6,134},{7,135},{8... | collective-permute-start | bytes 786440 | tf_op jit(solution)/shard_map/ppermute | solution.py:200
  93.4 14.9 %all-to-all-start.2 = ((f32[4,18,32,128]{3,2,1,0:T(8,128)}), f32[4,18,32,128]{3,2,1,0:T(8,128)S(1)}, u32[]{:S(2)}, u32[]{:S(2)}) async-start(f32[4,18,32,128]{3,2,1,0:T(8,128)} %shard_map.84), calls=%async_computation.2 | async-start | bytes 2359296 | tf_op jit(solution)/shard_map/all_to_all | solution.py:282
  97.8 8.0 %collective-permute-start.7 = (f32[4,8,32,128]{3,2,1,0:T(8,128)S(1)}, f32[4,8,32,128]{3,2,1,0:T(8,128)S(1)}, u32[]{:S(2)}, u32[]{:S(2)}) collective-permute-start(f32[4,8,32,128]{3,2,1,0:T(8,128)S(1)} %all-to-all-done.1.near), channel_id=1, source_target_pairs={{0,128},{1,129},{2,130},{3,131},{4,132},{5,133},{6,134},{7,135},{8... | collective-permute-start | bytes 1572872 | tf_op jit(solution)/shard_map/ppermute | solution.py:200

commit v3 on v1

v3 whole, which is shorter than its diff:
```python
import jax
import jax.numpy as jnp
from jax import lax
from jax.experimental import pallas as pl
from jax.experimental.pallas import tpu as pltpu
from jax.sharding import PartitionSpec as P

HALO = 16
ITS = 4
DIFFUSION = 0.2
EDGE = 8
LANES = 128
ROOM = 56
HIGH = lax.Precision.HIGHEST
F32 = jnp.float32
VMEM = pl.BlockSpec(memory_space=pltpu.VMEM)
SMEM = pl.BlockSpec(memory_space=pltpu.SMEM)
ANY = pl.BlockSpec(memory_space=pltpu.HBM)


def call(kernel, outs, in_specs, scratch=(), out_specs=None, aliases=None, limit=16):
    return pl.pallas_call(
        kernel,
        out_shape=[jax.ShapeDtypeStruct(o, F32) for o in outs],
        in_specs=in_specs,
        out_specs=out_specs or [VMEM] * len(outs),
        scratch_shapes=list(scratch),
        input_output_aliases=aliases or {},
        compiler_params=pltpu.CompilerParams(vmem_limit_bytes=limit << 20),
        cost_estimate=pl.CostEstimate(flops=1 << 22, bytes_accessed=1 << 21, transcendentals=0),
    )


def outer(a, b):
    return lax.dot_general(
        a, b, (((0,), (0,)), ((), ())), precision=HIGH, preferred_element_type=F32
    )


def fetch(volume, base, block, sems):
    copies = []
    for k in range(HALO // 8):
        columns = pl.ds(pl.multiple_of(base + 8 * k, 8), 8)
        copies.append(pltpu.make_async_copy(volume.at[:, columns, :], block.at[k], sems.at[k]))
        copies[k].start()
    return copies


def apply(weights, copies, block, out):
    for k, copy in enumerate(copies):
        copy.wait()
        turned = jnp.swapaxes(block[k], 0, 1)
        for i in range(8):
            part = jnp.dot(weights, turned[i], precision=HIGH, preferred_element_type=F32)
            for chunk in range(out.shape[0]):
                out[chunk, 8 * k + i] = part[:, chunk * LANES : (chunk + 1) * LANES]


def project_first(place, index, table, volume, out, weights, block, sems):
    depth, rows = table.shape
    copies = fetch(volume, HALO * place[3], block, sems)
    picker = (
        lax.broadcasted_iota(jnp.int32, (rows, index.shape[1]), 0) == index[...]
    ).astype(F32)
    flipped = jnp.dot(table[...], picker, precision=HIGH, preferred_element_type=F32)
    row = lax.broadcasted_iota(jnp.int32, (depth, LANES), 0)
    lane = lax.broadcasted_iota(jnp.int32, (depth, LANES), 1)
    moved = outer(flipped, (lane == row + place[0] * depth).astype(F32))
    local = outer(flipped, (lane == row).astype(F32))
    weights[...] = local
    for chunk in range(out.shape[0]):
        out[chunk, HALO] = moved
    apply(local[:, :depth], copies, block, out)


def project_second(place, weights, volume, out, block, sems):
    copies = fetch(volume, HALO * (1 - place[3]), block, sems)
    apply(weights[:, : volume.shape[0]], copies, block, out)


def add_parts(parts, *outs):
    base = 0
    for out in outs:
        for k in range(out.shape[0]):
            low = parts[0, base + k] + parts[1, base + k]
            out[k] = low + (parts[2, base + k] + parts[3, base + k])
        base += out.shape[0]


def turn(place, measured, frac, out, part, block, sems):
    lanes = pl.ds(pl.multiple_of(place[0] * LANES, LANES), LANES)
    first = pltpu.make_async_copy(measured.at[0, :, :, lanes], block, sems.at[0])
    second = pltpu.make_async_copy(frac.at[0, :, lanes], part, sems.at[1])
    first.start()
    second.start()
    first.wait()
    out[...] = jnp.swapaxes(block[...], 0, 1)
    second.wait()


def residual(
    place, shift, own_o, own_e, halo_o, halo_e, measured, frac,
    out_o, out_e, center_o, center_e, field, ext, grad,
):
    odd = place[3]
    cols, angles, width = measured.shape
    at_o, at_e = HALO * (1 + odd), HALO * (2 - odd)
    edge_o, edge_e = 3 * HALO * odd, 3 * HALO * (1 - odd)
    ext[pl.ds(at_o, HALO)] = own_o[...]
    ext[pl.ds(at_e, HALO)] = own_e[...]
    ext[pl.ds(edge_o, HALO)] = halo_o[...]
    ext[pl.ds(edge_e, HALO)] = halo_e[...]
    grad[...] = jnp.zeros_like(grad)
    for k in range(cols):
        at = k + HALO + shift[0, k]
        lower, upper = ext[at], ext[at + 1]
        part = frac[k : k + 1, :]
        rest = 1.0 - part
        resid = (rest * lower + part * upper) - measured[k]
        field[k : k + 1, :] = jnp.sum(resid * (upper - lower), axis=0, keepdims=True)
        grad[at] = grad[at] + rest * resid
        grad[at + 1] = grad[at + 1] + part * resid
    center_o[...] = grad[pl.ds(at_o, HALO)]
    center_e[...] = grad[pl.ds(at_e, HALO)]
    out_o[0:HALO] = grad[pl.ds(edge_o, HALO)]
    out_e[0:HALO] = grad[pl.ds(edge_e, HALO)]
    left = field[0:EDGE, :]
    right = field[cols - EDGE : cols, :]
    for out, edge in (
        (out_o, jnp.where(odd == 1, right, left)),
        (out_e, jnp.where(odd == 1, left, right)),
    ):
        out[HALO] = jnp.zeros((angles, width), F32)
        out[HALO, 0:EDGE, :] = edge


def land_first(center, landed, weights, out):
    out[0:HALO] = center[...] + landed[0:HALO]
    out[HALO] = weights[0]


def land_second(place, center, landed, other, field, out, wide):
    out[...] = center[...] + landed[0:HALO]
    cols = field.shape[0]
    near, far = landed[HALO, 0:EDGE, :], other[HALO, 0:EDGE, :]
    odd = place[3] == 1
    wide[0:EDGE] = jnp.where(odd, far, near)
    wide[EDGE : EDGE + cols] = field[...]
    wide[EDGE + cols : cols + 2 * EDGE] = jnp.where(odd, near, far)
    wide[cols + 2 * EDGE :] = jnp.zeros((wide.shape[0] - cols - 2 * EDGE, wide.shape[1]), F32)


def spread(place, own_weights, other_weights, own, other, out):
    depth = out.shape[2]
    first = place[1] == 0

    def order(a, b):
        return jnp.concatenate([jnp.where(first, a, b), jnp.where(first, b, a)], axis=0)

    weights = order(own_weights, other_weights).T
    for k in range(0, HALO, 2):
        pair = jnp.concatenate([order(own[k], other[k]), order(own[k + 1], other[k + 1])], axis=1)
        value = jnp.dot(weights, pair, precision=HIGH, preferred_element_type=F32)
        for chunk in range(out.shape[0]):
            rows = value[chunk * depth : (chunk + 1) * depth]
            out[chunk, k] = rows[:, :LANES]
            out[chunk, k + 1] = rows[:, LANES:]


def spread_first(place, own, other, out):
    spread(place, own[HALO], other[HALO], own, other, out)


def spread_second(place, own_e, other_e, own, other, wide, out):
    depth = out.shape[2]
    spread(place, own_e[HALO], other_e[HALO], own, other, out)
    for chunk in range(out.shape[0]):
        out[chunk, HALO] = wide[0:depth]
        out[chunk, HALO + 1] = wide[depth:]


def store(parts, image, base, block, sems):
    chunks, _, _, width = parts.shape
    copies = []
    for k in range(HALO // 8):
        for chunk in range(chunks):
            block[k, :, :, chunk * width : (chunk + 1) * width] = jnp.swapaxes(
                parts[chunk, 8 * k : 8 * k + 8], 0, 1
            )
        columns = pl.ds(pl.multiple_of(base + 8 * k, 8), 8)
        copies.append(pltpu.make_async_copy(block.at[k], image.at[:, columns, :], sems.at[k]))
        copies[k].start()
    return copies


def finish_first(place, parts, image, block, sems):
    for copy in store(parts, image, HALO * (1 - place[3]), block, sems):
        copy.wait()


def finish_second(last, place, parts, partial, image, field, block, sems):
    del partial
    copies = store(parts, image, HALO * place[3], block, sems)
    cols = field.shape[1]
    wide = jnp.concatenate(
        [
            jnp.concatenate([parts[c, HALO], parts[c, HALO + 1]], axis=0)
            for c in range(parts.shape[0])
        ],
        axis=1,
    )[: cols + 2 * EDGE]
    height, total = wide.shape
    row = lax.broadcasted_iota(jnp.int32, wide.shape, 0)
    lane = lax.broadcasted_iota(jnp.int32, wide.shape, 1)
    outside = ((row < EDGE) & (place[2] == 0)) | ((row >= EDGE + cols) & (place[2] == last))
    for _ in range(ITS):
        after = pltpu.roll(wide, height - 1, 0)
        before = pltpu.roll(wide, 1, 0)
        right = jnp.where(lane == total - 1, 0.0, pltpu.roll(wide, total - 1, 1))
        left = jnp.where(lane == 0, 0.0, pltpu.roll(wide, 1, 1))
        laplace = after + before + right + left - 4.0 * wide
        wide = jnp.where(outside, 0.0, wide + DIFFUSION * laplace)
    field[0] = wide[EDGE : EDGE + cols]
    for copy in copies:
        copy.wait()


def body(volume, frac, shift, angle_index, depth_weights, measured):
    depth, cols, height = volume.shape
    angles = angle_index.shape[1]
    slabs, tiles, phases = (lax.axis_size(a) for a in ("slab", "tile", "phase"))
    tile = lax.axis_index("tile")
    place = jnp.stack(
        [lax.axis_index("slab"), lax.axis_index("phase"), tile, tile % 2]
    ).astype(jnp.int32)
    half = (HALO, angles, LANES)
    more = (HALO + 1, angles, LANES)
    halves = pltpu.VMEM((HALO // 8, depth, 8, height), F32)
    two = pltpu.SemaphoreType.DMA((2,))
    pairs_e = [(i, i ^ 1) for i in range(tiles)]
    pairs_o = [(i, ((i + 1) ^ 1) - 1) for i in range(1, tiles - 1)]

    def swap(block, pairs):
        return lax.ppermute(block, "tile", pairs)

    def partner(block):
        return lax.ppermute(block, "phase", [(i, phases - 1 - i) for i in range(phases)])

    def regroup(block):
        return lax.all_to_all(block, "slab", 0, 0, tiled=True)

    parts_o, local = call(
        project_first,
        [(slabs,) + more, (angles, LANES)],
        [SMEM, VMEM, VMEM, ANY],
        [halves, two],
        limit=ROOM,
    )(place, angle_index, depth_weights.T, volume)
    (parts_e,) = call(
        project_second, [(slabs,) + half], [SMEM, VMEM, ANY], [halves, two], limit=ROOM
    )(place, local, volume)
    parts_o = regroup(parts_o)
    parts_o, parts_e = lax.optimization_barrier((parts_o, parts_e))
    parts_e = regroup(parts_e)
    mine, part = call(
        turn,
        [(cols, angles, LANES), (cols, LANES)],
        [SMEM, ANY, ANY],
        [pltpu.VMEM((angles, cols, LANES), F32), two],
        limit=ROOM,
    )(place, measured, frac)
    parts_e, mine, part = lax.optimization_barrier((parts_e, mine, part))
    own_o, weights = call(add_parts, [half, (1, angles, LANES)], [VMEM])(parts_o)
    halo_o = swap(own_o, pairs_o)
    (own_e,) = call(add_parts, [half], [VMEM])(parts_e)
    halo_e = swap(own_e, pairs_e)
    scratch = [pltpu.VMEM((cols + 2 * HALO, angles, LANES), F32)] * 2
    out_o, out_e, center_o, center_e, field = call(
        residual,
        [more, more, half, half, (cols, LANES)],
        [SMEM] * 2 + [VMEM] * 6,
        scratch,
    )(place, shift, own_o, own_e, halo_o, halo_e, mine, part)
    landed_o = swap(out_o, pairs_o)
    landed_e = swap(out_e, pairs_e)
    (adjoint_e,) = call(land_first, [more], [VMEM] * 3)(center_e, landed_e, weights)
    other_e = partner(adjoint_e)
    adjoint_o, wide = call(land_second, [half, (2 * depth, LANES)], [SMEM] + [VMEM] * 4)(
        place, center_o, landed_o, landed_e, field
    )
    other_o = partner(adjoint_o)
    (image_e,) = call(spread_first, [(slabs, HALO, depth, LANES)], [SMEM] + [VMEM] * 2)(
        place, adjoint_e, other_e
    )
    image_e = regroup(image_e)
    (image_o,) = call(spread_second, [(slabs, HALO + 2, depth, LANES)], [SMEM] + [VMEM] * 5)(
        place, adjoint_e, other_e, adjoint_o, other_o, wide
    )
    image_o = regroup(image_o)
    (image,) = call(finish_first, [(depth, cols, height)], [SMEM, VMEM], [halves, two], [ANY])(
        place, image_e
    )

    def ending(*refs):
        finish_second(tiles - 1, *refs)

    return call(
        ending,
        [(depth, cols, height), (1, cols, height)],
        [SMEM, VMEM, ANY],
        [halves, two],
        [ANY, VMEM],
        {2: 0},
    )(place, image_o, image)


def solution(mesh):
    return jax.shard_map(
        body,
        mesh=mesh,
        in_specs=(
            P("slab", "tile", None),
            P("phase", "tile", None),
            P("phase", "tile"),
            P("phase", None),
            P(None, "slab"),
            P("phase", None, "tile", None),
        ),
        out_specs=(P("slab", "tile", None), P("phase", "tile", None)),
        check_vma=False,
    )
```

time: 116 us -> 112 us (0.966)
  the two profiles are of different devices: /device:TPU:71 before, /device:TPU:128 now
where the time goes in v3:
time: 112 us
  waiting for transfers between devices  66.3 us (59%)
  Pallas kernels  22.1 us (20%)
  starting transfers between devices  21.9 us (20%)
    all_to_all x4, waiting for transfers between devices, regroup(): return lax.all_to_all(block, 'slab', 0, 0, tiled=True)  30.9 us
    ppermute x4, waiting for transfers between devices, swap(): return lax.ppermute(block, 'tile', pairs)  20.4 us
    all_to_all x4, starting transfers between devices, regroup(): return lax.all_to_all(block, 'slab', 0, 0, tiled=True)  17.5 us
    ppermute x2, waiting for transfers between devices, partner(): lax.ppermute(block, 'phase', [(i, phases - 1 - i) for i in range(phases)])  15 us
    ppermute x4, starting transfers between devices, swap(): return lax.ppermute(block, 'tile', pairs)  4.23 us
    pallas_call x1, Pallas kernels, body(): call(project_first, [(slabs,) + more, (angles, LANES)], [SMEM, VMEM, VMEM...  4.21 us
    pallas_call x1, Pallas kernels, body(): call(project_second, [(slabs,) + half], [SMEM, VMEM, ANY], [halves, two],...  4 us
    pallas_call x1, Pallas kernels, body(): call(turn, [(cols, angles, LANES), (cols, LANES)], [SMEM, ANY, ANY], [plt...  2.76 us
  transfers between devices with their start and end apart: 10, of which 8 were waited for; matrix products, arithmetic and copies ran while one was open for 0% of the time, Pallas kernels for 10%

profile of v3, /device:TPU:128, one launch (start us, length us, event | category | flops | bytes accessed | tf_op | source)
XLA Modules:
  0.0 111.8 jit_solution(11569612507625239434)
XLA Ops:
  0.6 0.7 pad_add_fusion.place.refs_0_
  1.3 4.2 %shard_map.77 = (f32[4,17,32,128]{3,2,1,0:T(8,128)}, f32[32,128]{1,0:T(8,128)}) custom-call(s32[4]{0:T(128)} %pad_add_fusion.place.refs_0_, s32[1,32]{1,0:T(1,128)} %index.1, f32[32,680]{1,0:T(8,128)} %bitcast.5, f32[32,32,512]{2,1,0:T(8,128)} %volume.3), custom_call_target="tpu_custom_call" | custom-call | flops 4194304 | bytes 2097152 | tf_op jit(solution)/shard_map/pallas_call | solution.py:252
  5.5 4.5 %all-to-all-start = ((f32[4,17,32,128]{3,2,1,0:T(8,128)}), f32[4,17,32,128]{3,2,1,0:T(8,128)S(1)}, u32[]{:S(2)}, u32[]{:S(2)}) async-start(f32[4,17,32,128]{3,2,1,0:T(8,128)} %get-tuple-element.20), calls=%async_computation | async-start | bytes 2228224 | tf_op jit(solution)/shard_map/all_to_all | solution.py:250
  10.0 4.0 %shard_map.78 = f32[4,16,32,128]{3,2,1,0:T(8,128)} custom-call(s32[4]{0:T(128)} %pad_add_fusion.place.refs_0_, f32[32,128]{1,0:T(8,128)} %get-tuple-element.21.weights, f32[32,32,512]{2,1,0:T(8,128)} %volume.3), custom_call_target="tpu_custom_call" | custom-call | flops 4194304 | bytes 2097152 | tf_op jit(solution)/shard_map/pallas_call | solution.py:259
  14.0 11.8 %all-to-all-done.parts = f32[4,17,32,128]{3,2,1,0:T(8,128)S(1)} async-done(((f32[4,17,32,128]{3,2,1,0:T(8,128)}), f32[4,17,32,128]{3,2,1,0:T(8,128)S(1)}, u32[]{:S(2)}, u32[]{:S(2)}) %all-to-all-start) | async-done | bytes 1114144 | tf_op jit(solution)/shard_map/all_to_all | solution.py:250
  25.8 3.5 %all-to-all-start.1 = ((f32[4,16,32,128]{3,2,1,0:T(8,128)}), f32[4,16,32,128]{3,2,1,0:T(8,128)S(1)}, u32[]{:S(2)}, u32[]{:S(2)}) async-start(f32[4,16,32,128]{3,2,1,0:T(8,128)} %shard_map.78), calls=%async_computation.1 | async-start | bytes 2097152 | tf_op jit(solution)/shard_map/all_to_all | solution.py:250
  29.3 0.0 copy-start.1
  29.3 0.0 copy-start.3
  29.3 2.8 %shard_map.80 = (f32[32,32,128]{2,1,0:T(8,128)}, f32[32,128]{1,0:T(8,128)}) custom-call(s32[4]{0:T(128)} %pad_add_fusion.place.refs_0_, f32[1,32,32,512]{3,2,1,0:T(8,128)} %measured.1, f32[1,32,512]{2,1,0:T(8,128)} %frac.1), custom_call_target="tpu_custom_call" | custom-call | flops 4194304 | bytes 2097152 | tf_op jit(solution)/shard_map/pallas_call | solution.py:265
  32.1 0.0 copy-start
  32.1 0.0 copy-start.2
  32.1 0.1 shard_map.79
  32.2 2.1 %collective-permute-start = (f32[16,32,128]{2,1,0:T(8,128)S(1)}, f32[16,32,128]{2,1,0:T(8,128)S(1)}, u32[]{:S(2)}, u32[]{:S(2)}) collective-permute-start(f32[16,32,128]{2,1,0:T(8,128)S(1)} %get-tuple-element.23.own_o), channel_id=1, source_target_pairs={{1,2},{2,1},{3,4},{4,3},{5,6},{6,5},{7,8},{8,7},{9,10},{10,9},{11,... | collective-permute-start | bytes 786440 | tf_op jit(solution)/shard_map/ppermute | solution.py:244
  34.3 9.1 %all-to-all-done.1.parts = f32[4,16,32,128]{3,2,1,0:T(8,128)S(1)} async-done(((f32[4,16,32,128]{3,2,1,0:T(8,128)}), f32[4,16,32,128]{3,2,1,0:T(8,128)S(1)}, u32[]{:S(2)}, u32[]{:S(2)}) %all-to-all-start.1) | async-done | bytes 1048608 | tf_op jit(solution)/shard_map/all_to_all | solution.py:250
  43.5 0.1 shard_map.81.own_e
  43.5 0.1 collective-permute-start.1
  43.6 3.3 %collective-permute-done.halo_o = f32[16,32,128]{2,1,0:T(8,128)S(1)} collective-permute-done((f32[16,32,128]{2,1,0:T(8,128)S(1)}, f32[16,32,128]{2,1,0:T(8,128)S(1)}, u32[]{:S(2)}, u32[]{:S(2)}) %collective-permute-start) | collective-permute-done | bytes 262176 | tf_op jit(solution)/shard_map/ppermute | solution.py:244
  46.9 0.0 collective-permute-done.1.halo_e
  46.9 0.0 copy-done.1
  46.9 0.0 copy-done.3
  46.9 0.0 copy-done
  47.0 0.0 copy-done.2
  47.0 1.0 shard_map.82
  48.0 0.1 collective-permute-start.2
  48.1 1.5 %collective-permute-done.2.landed.other = f32[17,32,128]{2,1,0:T(8,128)S(1)} collective-permute-done((f32[17,32,128]{2,1,0:T(8,128)S(1)}, f32[17,32,128]{2,1,0:T(8,128)S(1)}, u32[]{:S(2)}, u32[]{:S(2)}) %collective-permute-start.2) | collective-permute-done | bytes 278560 | tf_op jit(solution)/shard_map/ppermute | solution.py:244
  49.6 0.1 collective-permute-start.3
  49.7 8.7 %collective-permute-done.3.other_e.other = f32[17,32,128]{2,1,0:T(8,128)S(1)} collective-permute-done((f32[17,32,128]{2,1,0:T(8,128)S(1)}, f32[17,32,128]{2,1,0:T(8,128)S(1)}, u32[]{:S(2)}, u32[]{:S(2)}) %collective-permute-start.3) | collective-permute-done | bytes 278560 | tf_op jit(solution)/shard_map/ppermute | solution.py:247
  58.4 2.5 %shard_map.86 = f32[4,16,32,128]{3,2,1,0:T(8,128)} custom-call(s32[4]{0:T(128)S(1)} %copy-done.1, f32[17,32,128]{2,1,0:T(8,128)S(1)} %shard_map.83.own_e.own, f32[17,32,128]{2,1,0:T(8,128)S(1)} %collective-permute-done.3.other_e.other), custom_call_target="tpu_custom_call" | custom-call | flops 4194304 | bytes 2097152 | tf_op jit(solution)/shard_map/pallas_call | solution.py:292
  61.0 4.7 %all-to-all-start.3 = ((f32[4,16,32,128]{3,2,1,0:T(8,128)}), f32[4,16,32,128]{3,2,1,0:T(8,128)S(1)}, u32[]{:S(2)}, u32[]{:S(2)}) async-start(f32[4,16,32,128]{3,2,1,0:T(8,128)} %shard_map.86), calls=%async_computation.3 | async-start | bytes 2097152 | tf_op jit(solution)/shard_map/all_to_all | solution.py:250
  65.7 1.9 %collective-permute-start.4 = (f32[17,32,128]{2,1,0:T(8,128)S(1)}, f32[17,32,128]{2,1,0:T(8,128)S(1)}, u32[]{:S(2)}, u32[]{:S(2)}) collective-permute-start(f32[17,32,128]{2,1,0:T(8,128)S(1)} %get-tuple-element.34), channel_id=1, source_target_pairs={{1,2},{2,1},{3,4},{4,3},{5,6},{6,5},{7,8},{8,7},{9,10},{10,9},{11,... | collective-permute-start | bytes 835592 | tf_op jit(solution)/shard_map/ppermute | solution.py:244
  67.6 15.5 %collective-permute-done.4.landed = f32[17,32,128]{2,1,0:T(8,128)S(1)} collective-permute-done((f32[17,32,128]{2,1,0:T(8,128)S(1)}, f32[17,32,128]{2,1,0:T(8,128)S(1)}, u32[]{:S(2)}, u32[]{:S(2)}) %collective-permute-start.4) | collective-permute-done | bytes 278560 | tf_op jit(solution)/shard_map/ppermute | solution.py:244
  83.2 0.6 shard_map.84
  83.7 0.1 collective-permute-start.5
  83.8 6.4 %collective-permute-done.5.other = f32[16,32,128]{2,1,0:T(8,128)S(1)} collective-permute-done((f32[16,32,128]{2,1,0:T(8,128)S(1)}, f32[16,32,128]{2,1,0:T(8,128)S(1)}, u32[]{:S(2)}, u32[]{:S(2)}) %collective-permute-start.5) | collective-permute-done | bytes 262176 | tf_op jit(solution)/shard_map/ppermute | solution.py:247
  90.2 2.6 %shard_map.85 = f32[4,18,32,128]{3,2,1,0:T(8,128)} custom-call(s32[4]{0:T(128)S(1)} %copy-done.1, f32[17,32,128]{2,1,0:T(8,128)S(1)} %shard_map.83.own_e.own, f32[17,32,128]{2,1,0:T(8,128)S(1)} %collective-permute-done.3.other_e.other, f32[16,32,128]{2,1,0:T(8,128)S(1)} %get-tuple-element.36.own, f32[16,32,128]{2,1,0:T(8,128)S(1)} %collective-permute-done.5.other, ...), custom_call_target="tpu_custom_call" | custom-call | flops 4194304 | bytes 2097152 | tf_op jit(solution)/shard_map/pallas_call | solution.py:296
  92.8 0.0 all-to-all-done.3.parts
  92.8 4.8 %all-to-all-start.2 = ((f32[4,18,32,128]{3,2,1,0:T(8,128)}), f32[4,18,32,128]{3,2,1,0:T(8,128)S(1)}, u32[]{:S(2)}, u32[]{:S(2)}) async-start(f32[4,18,32,128]{3,2,1,0:T(8,128)} %shard_map.85), calls=%async_computation.2 | async-start | bytes 2359296 | tf_op jit(solution)/shard_map/all_to_all | solution.py:250
  97.6 1.6 %shard_map.87.refs_2_ = f32[32,32,512]{2,1,0:T(8,128)} custom-call(s32[4]{0:T(128)S(1)} %copy-done.1, f32[4,16,32,128]{3,2,1,0:T(8,128)S(1)} %all-to-all-done.3.parts), custom_call_target="tpu_custom_call" | custom-call | flops 4194304 | bytes 2097152 | tf_op jit(solution)/shard_map/pallas_call | solution.py:300
  99.2 10.0 %all-to-all-done.2.refs_1_ = f32[4,18,32,128]{3,2,1,0:T(8,128)S(1)} async-done(((f32[4,18,32,128]{3,2,1,0:T(8,128)}), f32[4,18,32,128]{3,2,1,0:T(8,128)S(1)}, u32[]{:S(2)}, u32[]{:S(2)}) %all-to-all-start.2) | async-done | bytes 1179680 | tf_op jit(solution)/shard_map/all_to_all | solution.py:250
  109.2 2.6 %shard_map.88 = (f32[32,32,512]{2,1,0:T(8,128)}, f32[1,32,512]{2,1,0:T(8,128)}) custom-call(s32[4]{0:T(128)S(1)} %copy-done.1, f32[4,18,32,128]{3,2,1,0:T(8,128)S(1)} %all-to-all-done.2.refs_1_, f32[32,32,512]{2,1,0:T(8,128)} %shard_map.87.refs_2_), custom_call_target="tpu_custom_call", output_to_operand_aliasing={{0}: (2, {})} | custom-call | flops 4194304 | bytes 2097152 | tf_op jit(solution)/shard_map/pallas_call | solution.py:307
  (1 shorter events, 0.0 us)
Async XLA Ops:
  5.5 20.3 %all-to-all-start = ((f32[4,17,32,128]{3,2,1,0:T(8,128)}), f32[4,17,32,128]{3,2,1,0:T(8,128)S(1)}, u32[]{:S(2)}, u32[]{:S(2)}) async-start(f32[4,17,32,128]{3,2,1,0:T(8,128)} %get-tuple-element.20), calls=%async_computation | async-start | bytes 2228224 | tf_op jit(solution)/shard_map/all_to_all | solution.py:250
  25.8 17.7 %all-to-all-start.1 = ((f32[4,16,32,128]{3,2,1,0:T(8,128)}), f32[4,16,32,128]{3,2,1,0:T(8,128)S(1)}, u32[]{:S(2)}, u32[]{:S(2)}) async-start(f32[4,16,32,128]{3,2,1,0:T(8,128)} %shard_map.78), calls=%async_computation.1 | async-start | bytes 2097152 | tf_op jit(solution)/shard_map/all_to_all | solution.py:250
  29.3 17.6 %copy-start.1 = (s32[4]{0:T(128)S(1)}, s32[4]{0:T(128)}, u32[]{:S(2)}) copy-start(s32[4]{0:T(128)} %pad_add_fusion.place.refs_0_) | copy-start | bytes 52
  29.3 17.6 %copy-start.3 = (s32[1,32]{1,0:T(1,128)S(1)}, s32[1,32]{1,0:T(1,128)}, u32[]{:S(2)}) copy-start(s32[1,32]{1,0:T(1,128)} %shift.1) | copy-start | bytes 388
  32.1 14.9 %copy-start = (f32[32,32,128]{2,1,0:T(8,128)S(1)}, f32[32,32,128]{2,1,0:T(8,128)}, u32[]{:S(2)}) copy-start(f32[32,32,128]{2,1,0:T(8,128)} %get-tuple-element.28.measured) | copy-start | bytes 1572868
  32.1 14.9 %copy-start.2 = (f32[32,128]{1,0:T(8,128)S(1)}, f32[32,128]{1,0:T(8,128)}, u32[]{:S(2)}) copy-start(f32[32,128]{1,0:T(8,128)} %get-tuple-element.29.frac) | copy-start | bytes 49156
  32.2 14.8 %collective-permute-start = (f32[16,32,128]{2,1,0:T(8,128)S(1)}, f32[16,32,128]{2,1,0:T(8,128)S(1)}, u32[]{:S(2)}, u32[]{:S(2)}) collective-permute-start(f32[16,32,128]{2,1,0:T(8,128)S(1)} %get-tuple-element.23.own_o), channel_id=1, source_target_pairs={{1,2},{2,1},{3,4},{4,3},{5,6},{6,5},{7,8},{8,7},{9,10},{10,9},{11,... | collective-permute-start | bytes 786440 | tf_op jit(solution)/shard_map/ppermute | solution.py:244
  43.5 3.4 %collective-permute-start.1 = (f32[16,32,128]{2,1,0:T(8,128)S(1)}, f32[16,32,128]{2,1,0:T(8,128)S(1)}, u32[]{:S(2)}, u32[]{:S(2)}) collective-permute-start(f32[16,32,128]{2,1,0:T(8,128)S(1)} %shard_map.81.own_e), channel_id=1, source_target_pairs={{0,1},{1,0},{2,3},{3,2},{4,5},{5,4},{6,7},{7,6},{8,9},{9,8},{10,11... | collective-permute-start | bytes 786440 | tf_op jit(solution)/shard_map/ppermute | solution.py:244
  48.0 1.6 %collective-permute-start.2 = (f32[17,32,128]{2,1,0:T(8,128)S(1)}, f32[17,32,128]{2,1,0:T(8,128)S(1)}, u32[]{:S(2)}, u32[]{:S(2)}) collective-permute-start(f32[17,32,128]{2,1,0:T(8,128)S(1)} %get-tuple-element.31), channel_id=1, source_target_pairs={{0,1},{1,0},{2,3},{3,2},{4,5},{5,4},{6,7},{7,6},{8,9},{9,8},{10,11... | collective-permute-start | bytes 835592 | tf_op jit(solution)/shard_map/ppermute | solution.py:244
  49.6 8.8 %collective-permute-start.3 = (f32[17,32,128]{2,1,0:T(8,128)S(1)}, f32[17,32,128]{2,1,0:T(8,128)S(1)}, u32[]{:S(2)}, u32[]{:S(2)}) collective-permute-start(f32[17,32,128]{2,1,0:T(8,128)S(1)} %shard_map.83.own_e.own), channel_id=1, source_target_pairs={{0,128},{128,0},{1,129},{129,1},{2,130},{130,2},{3,131},{131,3},{4... | collective-permute-start | bytes 835592 | tf_op jit(solution)/shard_map/ppermute | solution.py:247
  61.0 31.8 %all-to-all-start.3 = ((f32[4,16,32,128]{3,2,1,0:T(8,128)}), f32[4,16,32,128]{3,2,1,0:T(8,128)S(1)}, u32[]{:S(2)}, u32[]{:S(2)}) async-start(f32[4,16,32,128]{3,2,1,0:T(8,128)} %shard_map.86), calls=%async_computation.3 | async-start | bytes 2097152 | tf_op jit(solution)/shard_map/all_to_all | solution.py:250
  65.7 17.4 %collective-permute-start.4 = (f32[17,32,128]{2,1,0:T(8,128)S(1)}, f32[17,32,128]{2,1,0:T(8,128)S(1)}, u32[]{:S(2)}, u32[]{:S(2)}) collective-permute-start(f32[17,32,128]{2,1,0:T(8,128)S(1)} %get-tuple-element.34), channel_id=1, source_target_pairs={{1,2},{2,1},{3,4},{4,3},{5,6},{6,5},{7,8},{8,7},{9,10},{10,9},{11,... | collective-permute-start | bytes 835592 | tf_op jit(solution)/shard_map/ppermute | solution.py:244
  83.7 6.5 %collective-permute-start.5 = (f32[16,32,128]{2,1,0:T(8,128)S(1)}, f32[16,32,128]{2,1,0:T(8,128)S(1)}, u32[]{:S(2)}, u32[]{:S(2)}) collective-permute-start(f32[16,32,128]{2,1,0:T(8,128)S(1)} %get-tuple-element.36.own), channel_id=1, source_target_pairs={{0,128},{128,0},{1,129},{129,1},{2,130},{130,2},{3,131},{131,3},{4... | collective-permute-start | bytes 786440 | tf_op jit(solution)/shard_map/ppermute | solution.py:247
  92.8 16.4 %all-to-all-start.2 = ((f32[4,18,32,128]{3,2,1,0:T(8,128)}), f32[4,18,32,128]{3,2,1,0:T(8,128)S(1)}, u32[]{:S(2)}, u32[]{:S(2)}) async-start(f32[4,18,32,128]{3,2,1,0:T(8,128)} %shard_map.85), calls=%async_computation.2 | async-start | bytes 2359296 | tf_op jit(solution)/shard_map/all_to_all | solution.py:250

commit v4 on v0

v4 whole, which is shorter than its diff:
```python
import jax
import jax.numpy as jnp
from jax import lax
from jax.experimental import pallas as pl
from jax.experimental.pallas import tpu as pltpu
from jax.sharding import PartitionSpec as P

HALO = 16
ITS = 4
DIFFUSION = 0.2
EDGE = 8
REACH = HALO + ITS
LANES = 128
ROOM = 56
HIGH = lax.Precision.HIGHEST
F32 = jnp.float32
VMEM = pl.BlockSpec(memory_space=pltpu.VMEM)
SMEM = pl.BlockSpec(memory_space=pltpu.SMEM)
ANY = pl.BlockSpec(memory_space=pltpu.HBM)


def call(kernel, outs, in_specs, scratch=(), out_specs=None, aliases=None, limit=16):
    return pl.pallas_call(
        kernel,
        out_shape=[jax.ShapeDtypeStruct(o, F32) for o in outs],
        in_specs=in_specs,
        out_specs=out_specs or [VMEM] * len(outs),
        scratch_shapes=list(scratch),
        input_output_aliases=aliases or {},
        compiler_params=pltpu.CompilerParams(vmem_limit_bytes=limit << 20),
        cost_estimate=pl.CostEstimate(flops=1 << 22, bytes_accessed=1 << 21, transcendentals=0),
    )


def outer(a, b):
    return lax.dot_general(
        a, b, (((0,), (0,)), ((), ())), precision=HIGH, preferred_element_type=F32
    )


def project(place, index, table, volume, out, rows, block, staged, sems, done):
    depth, cols, _ = volume.shape
    groups = cols // 8
    entry = pltpu.make_async_copy(table, rows, sems.at[groups])
    entry.start()
    copies = []
    for k in range(groups):
        columns = pl.ds(8 * k, 8)
        copies.append(pltpu.make_async_copy(volume.at[:, columns, :], block.at[k], sems.at[k]))
        copies[k].start()
    entry.wait()
    count = table.shape[1]
    picker = (
        lax.broadcasted_iota(jnp.int32, (count, index.shape[1]), 0) == index[...]
    ).astype(F32)
    flipped = jnp.dot(rows[...], picker, precision=HIGH, preferred_element_type=F32)
    row = lax.broadcasted_iota(jnp.int32, (depth, LANES), 0)
    lane = lax.broadcasted_iota(jnp.int32, (depth, LANES), 1)
    moved = outer(flipped, (lane == row + place[0] * depth).astype(F32))
    weights = outer(flipped, (lane == row).astype(F32))[:, :depth]
    sent = []
    for k in range(groups):
        copies[k].wait()
        turned = jnp.swapaxes(block[k], 0, 1)
        for i in range(8):
            part = jnp.dot(weights, turned[i], precision=HIGH, preferred_element_type=F32)
            for chunk in range(out.shape[0]):
                staged[k, chunk, i] = part[:, chunk * LANES : (chunk + 1) * LANES]
        size = 8
        if k == groups - 1:
            size = 9
            for chunk in range(out.shape[0]):
                staged[k, chunk, 8] = moved
        sent.append(
            pltpu.make_async_copy(
                staged.at[k, :, pl.ds(0, size)], out.at[:, pl.ds(8 * k, size)], done.at[k]
            )
        )
        sent[k].start()
    for copy in sent:
        copy.wait()


def add_parts(place, parts, own, edge_o, edge_e, weights):
    cols = own.shape[0]
    for k in range(cols):
        own[k] = (parts[0, k] + parts[1, k]) + (parts[2, k] + parts[3, k])
    weights[...] = (parts[0, cols] + parts[1, cols]) + (parts[2, cols] + parts[3, cols])
    skip = cols - REACH
    edge_o[...] = own[pl.ds(skip * place[3], REACH)]
    edge_e[...] = own[pl.ds(skip * (1 - place[3]), REACH)]


def turn(place, measured, frac, out, part, edge_o, edge_e, block, sems):
    lanes = pl.ds(pl.multiple_of(place[0] * LANES, LANES), LANES)
    first = pltpu.make_async_copy(measured.at[0, :, :, lanes], block, sems.at[0])
    second = pltpu.make_async_copy(frac.at[0, :, lanes], part, sems.at[1])
    first.start()
    second.start()
    first.wait()
    out[...] = jnp.swapaxes(block[...], 0, 1)
    second.wait()
    for edge, side in ((edge_o, place[3]), (edge_e, 1 - place[3])):
        start = pl.multiple_of(HALO * side, HALO)
        edge[0:HALO] = out[pl.ds(start, HALO)]
        edge[HALO] = jnp.zeros(edge.shape[1:], F32)
        edge[HALO, 0:HALO, :] = part[pl.ds(start, HALO), :]


def residual(
    place, shift, shift_o, shift_e, own, halo_o, halo_e, measured, measured_o, measured_e, frac,
    weights, keep, send, field, ext, seen, share, grad,
):
    odd = place[3]
    cols, angles, width = measured.shape
    ext[REACH : REACH + cols] = own[...]
    ext[pl.ds((REACH + cols) * odd, REACH)] = halo_o[...]
    ext[pl.ds((REACH + cols) * (1 - odd), REACH)] = halo_e[...]
    seen[HALO : HALO + cols] = measured[...]
    share[HALO : HALO + cols, :] = frac[...]
    for ref, side in ((measured_o, odd), (measured_e, 1 - odd)):
        start = pl.multiple_of((HALO + cols) * side, HALO)
        seen[pl.ds(start, HALO)] = ref[0:HALO]
        share[pl.ds(start, HALO), :] = ref[HALO, 0:HALO, :]
    grad[...] = jnp.zeros_like(grad)
    for k in range(cols + 2 * HALO):
        column = k - HALO
        if column < 0:
            step = jnp.where(odd == 1, shift_e[0, cols + column], shift_o[0, cols + column])
        elif column < cols:
            step = shift[0, column]
        else:
            step = jnp.where(odd == 1, shift_o[0, column - cols], shift_e[0, column - cols])
        at = jnp.clip(column + step + REACH, 0, cols + 2 * REACH - 2)
        lower, upper = ext[at], ext[at + 1]
        part = share[k : k + 1, :]
        rest = 1.0 - part
        resid = (rest * lower + part * upper) - seen[k]
        if -EDGE <= column < cols + EDGE:
            value = jnp.sum(resid * (upper - lower), axis=0, keepdims=True)
            for chunk in range(field.shape[0]):
                field[chunk, column + EDGE : column + EDGE + 1, :] = value
        lands = column + step + 2 * HALO
        grad[lands] = grad[lands] + rest * resid
        grad[lands + 1] = grad[lands + 1] + part * resid
    mine = HALO * (2 + place[1])
    theirs = HALO * (3 - place[1])
    keep[...] = grad[pl.ds(mine, HALO)]
    send[0:HALO] = grad[pl.ds(theirs, HALO)]
    send[HALO] = weights[...]


def spread(weights, own, other, out):
    depth = out.shape[2]
    slabs = out.shape[0] // 2
    table = jnp.concatenate([weights[...], other[HALO]], axis=0).T

    def both(k):
        return jnp.concatenate([own[k], other[k]], axis=0)

    for k in range(0, HALO, 2):
        pair = jnp.concatenate([both(k), both(k + 1)], axis=1)
        value = jnp.dot(table, pair, precision=HIGH, preferred_element_type=F32)
        for chunk in range(slabs):
            rows = value[chunk * depth : (chunk + 1) * depth]
            for copy in (chunk, slabs + chunk):
                out[copy, k] = rows[:, :LANES]
                out[copy, k + 1] = rows[:, LANES:]


def diffuse(last, place, parts, field):
    cols = field.shape[1]
    wide = jnp.concatenate([parts[c] for c in range(parts.shape[0])], axis=1)
    height, total = wide.shape
    row = lax.broadcasted_iota(jnp.int32, wide.shape, 0)
    lane = lax.broadcasted_iota(jnp.int32, wide.shape, 1)
    outside = ((row < EDGE) & (place[2] == 0)) | ((row >= EDGE + cols) & (place[2] == last))
    for _ in range(ITS):
        after = pltpu.roll(wide, height - 1, 0)
        before = pltpu.roll(wide, 1, 0)
        right = jnp.where(lane == total - 1, 0.0, pltpu.roll(wide, total - 1, 1))
        left = jnp.where(lane == 0, 0.0, pltpu.roll(wide, 1, 1))
        laplace = after + before + right + left - 4.0 * wide
        wide = jnp.where(outside, 0.0, wide + DIFFUSION * laplace)
    field[0] = wide[EDGE : EDGE + cols]


def finish(parts, image, block, sems):
    slabs = parts.shape[0] // 2
    copies = []
    for k in range(image.shape[1] // 8):
        phase, start = divmod(8 * k, HALO)
        for chunk in range(slabs):
            block[k, :, :, chunk * LANES : (chunk + 1) * LANES] = jnp.swapaxes(
                parts[phase * slabs + chunk, start : start + 8], 0, 1
            )
        columns = pl.ds(8 * k, 8)
        copies.append(pltpu.make_async_copy(block.at[k], image.at[:, columns, :], sems.at[k]))
        copies[k].start()
    for copy in copies:
        copy.wait()


def body(volume, frac, shift, angle_index, depth_weights, measured):
    depth, cols, height = volume.shape
    angles = angle_index.shape[1]
    slabs, tiles, phases = (lax.axis_size(a) for a in ("slab", "tile", "phase"))
    tile = lax.axis_index("tile")
    place = jnp.stack(
        [lax.axis_index("slab"), lax.axis_index("phase"), tile, tile % 2]
    ).astype(jnp.int32)
    half = (HALO, angles, LANES)
    more = (HALO + 1, angles, LANES)
    whole = (cols, angles, LANES)
    edge = (REACH, angles, LANES)
    groups = cols // 8
    blocks = pltpu.VMEM((groups, depth, 8, height), F32)
    dma = pltpu.SemaphoreType.DMA
    pairs_e = [(i, i ^ 1) for i in range(tiles)]
    pairs_o = [(i, ((i + 1) ^ 1) - 1) for i in range(1, tiles - 1)]

    def swap_o(block):
        return lax.ppermute(block, "tile", pairs_o)

    def swap_e(block):
        return lax.ppermute(block, "tile", pairs_e)

    (parts,) = call(
        project,
        [(slabs, cols + 1, angles, LANES)],
        [SMEM, VMEM, ANY, ANY],
        [
            pltpu.VMEM(depth_weights.shape[::-1], F32),
            blocks,
            pltpu.VMEM((groups, slabs, 9, angles, LANES), F32),
            dma((groups + 1,)),
            dma((groups,)),
        ],
        [ANY],
        limit=ROOM,
    )(place, angle_index, depth_weights.T, volume)
    parts = lax.all_to_all(parts, "slab", 0, 0, tiled=True)
    mine, part, edge_o, edge_e = call(
        turn,
        [whole, (cols, LANES), more, more],
        [SMEM, ANY, ANY],
        [pltpu.VMEM((angles, cols, LANES), F32), dma((2,))],
        limit=ROOM,
    )(place, measured, frac)
    measured_o, measured_e = swap_o(edge_o), swap_e(edge_e)
    shift_o, shift_e = swap_o(shift), swap_e(shift)
    parts, mine, part, measured_o, measured_e, shift_o, shift_e = lax.optimization_barrier(
        (parts, mine, part, measured_o, measured_e, shift_o, shift_e)
    )
    own, edge_o, edge_e, weights = call(
        add_parts, [whole, edge, edge, (angles, LANES)], [SMEM, VMEM]
    )(place, parts)
    halo_o, halo_e = swap_o(edge_o), swap_e(edge_e)
    keep, send, field = call(
        residual,
        [half, more, (slabs, cols + 2 * EDGE, LANES)],
        [SMEM] * 4 + [VMEM] * 8,
        [
            pltpu.VMEM((cols + 2 * REACH, angles, LANES), F32),
            pltpu.VMEM((cols + 2 * HALO, angles, LANES), F32),
            pltpu.VMEM((cols + 2 * HALO, LANES), F32),
            pltpu.VMEM((cols + 4 * HALO, angles, LANES), F32),
        ],
    )(
        place, shift, shift_o, shift_e, own, halo_o, halo_e, mine, measured_o, measured_e, part,
        weights,
    )
    other = lax.ppermute(send, "phase", [(i, phases - 1 - i) for i in range(phases)])
    field = lax.all_to_all(field, "slab", 0, 0, tiled=True)
    (parts,) = call(spread, [(phases * slabs, HALO, depth, LANES)], [VMEM] * 3)(
        weights, keep, other
    )
    parts = lax.all_to_all(parts, ("phase", "slab"), 0, 0, tiled=True)

    def steps(*refs):
        diffuse(tiles - 1, *refs)

    (field,) = call(steps, [(1, cols, height)], [SMEM, VMEM])(place, field)
    (image,) = call(
        finish, [(depth, cols, height)], [VMEM], [blocks, dma((groups,))], [ANY]
    )(parts)
    return image, field


def solution(mesh):
    return jax.shard_map(
        body,
        mesh=mesh,
        in_specs=(
            P("slab", "tile", None),
            P("phase", "tile", None),
            P("phase", "tile"),
            P("phase", None),
            P(None, "slab"),
            P("phase", None, "tile", None),
        ),
        out_specs=(P("slab", "tile", None), P("phase", "tile", None)),
        check_vma=False,
    )
```

time: 301 us -> 96.7 us (0.32); the launches traced: 297 us -> 95.8 us
  waiting for transfers between devices: 157 us -> 47.6 us
  local copies, waits for them, and re-layouts: 30 us -> 0.02 us
  other arithmetic: 29.3 us -> 0.58 us
  starting transfers between devices: 59 us -> 30.3 us
  Pallas kernels: 0 us -> 16.5 us
  between operations: 14.1 us -> 0.74 us
  matrix products: 7.28 us -> 0 us
    psum x3 -> x0, waiting for transfers between devices: 108 us -> none  [the longest x1 61.4 us: body(): projected = lax.psum(partial_proj, 'slab')]
    ppermute x12 -> x7, starting transfers between devices: 58.7 us -> 13.7 us  [the longest x3 11.3 us: swap_o(): return lax.ppermute(block, 'tile', pairs_o)]
    ppermute x12 -> x7, waiting for transfers between devices: 48.8 us -> 21.4 us  [the longest x3 18.1 us: swap_o(): return lax.ppermute(block, 'tile', pairs_o)]
    all_to_all x0 -> x3, waiting for transfers between devices: none -> 26.2 us  [the longest x1 14.6 us: body(): parts = lax.all_to_all(parts, ('phase', 'slab'), 0, 0, tiled=True)]
    all_to_all x0 -> x3, starting transfers between devices: none -> 16.6 us  [the longest x1 8.79 us: body(): parts = lax.all_to_all(parts, ('phase', 'slab'), 0, 0, tiled=True)]
    pallas_call x0 -> x7, Pallas kernels: none -> 16.5 us  [the longest x1 5.65 us: body(): call(project, [(slabs, cols + 1, angles, LANES)], [SMEM, VMEM, ANY, ANY],...]
    unnamed x26 -> x8, local copies, waits for them, and re-layouts: 13.8 us -> 0.02 us
    scatter-add x2 -> x0, other arithmetic: 12.2 us -> none  [the longest x1 6.12 us: warp_local(): upper = jnp.take(image, columns + 1, axis=1)]
  transfers between devices with their start and end apart: 15 -> 10, of which waited for: 11 -> 6; matrix products, arithmetic and copies ran while one was open for 5% -> 0% of each run, Pallas kernels for 0% -> 7%
where the time goes in v4:
time: 96.7 us; the launch traced here: 95.8 us
  waiting for transfers between devices  47.6 us (49%)
  starting transfers between devices  30.3 us (31%)
  Pallas kernels  16.5 us (17%)
    ppermute x3, waiting for transfers between devices, swap_o(): return lax.ppermute(block, 'tile', pairs_o)  18.1 us
    all_to_all x1, waiting for transfers between devices, body(): parts = lax.all_to_all(parts, ('phase', 'slab'), 0, 0, tiled=True)  14.6 us
    ppermute x3, starting transfers between devices, swap_o(): return lax.ppermute(block, 'tile', pairs_o)  11.3 us
    all_to_all x1, starting transfers between devices, body(): parts = lax.all_to_all(parts, ('phase', 'slab'), 0, 0, tiled=True)  8.79 us
    all_to_all x1, waiting for transfers between devices, body(): parts = lax.all_to_all(parts, 'slab', 0, 0, tiled=True)  8.65 us
    pallas_call x1, Pallas kernels, body(): call(project, [(slabs, cols + 1, angles, LANES)], [SMEM, VMEM, ANY, ANY],...  5.65 us
    all_to_all x1, starting transfers between devices, body(): parts = lax.all_to_all(parts, 'slab', 0, 0, tiled=True)  4.47 us
    all_to_all x1, starting transfers between devices, body(): field = lax.all_to_all(field, 'slab', 0, 0, tiled=True)  3.3 us
  transfers between devices with their start and end apart: 10, of which 6 were waited for; matrix products, arithmetic and copies ran while one was open for 0% of the time, Pallas kernels for 7%

profile of v4, /device:TPU:128, one launch (start us, length us, event | category | flops | bytes accessed | tf_op | source)
XLA Modules:
  0.0 95.8 jit_solution(7908917036877256967)
XLA Ops:
  0.6 0.6 pad_add_fusion.place.refs_0_
  1.2 5.6 %shard_map.77 = f32[4,33,32,128]{3,2,1,0:T(8,128)} custom-call(s32[4]{0:T(128)} %pad_add_fusion.place.refs_0_, s32[1,32]{1,0:T(1,128)} %index.1, f32[32,680]{1,0:T(8,128)} %bitcast.5, f32[32,32,512]{2,1,0:T(8,128)} %volume.1), custom_call_target="tpu_custom_call" | custom-call | flops 4194304 | bytes 2097152 | tf_op jit(solution)/shard_map/pallas_call | solution.py:228
  6.9 4.5 %all-to-all-start = ((f32[4,33,32,128]{3,2,1,0:T(8,128)}), f32[4,33,32,128]{3,2,1,0:T(8,128)S(1)}, u32[]{:S(2)}, u32[]{:S(2)}) async-start(f32[4,33,32,128]{3,2,1,0:T(8,128)} %shard_map.77), calls=%async_computation | async-start | bytes 4325376 | tf_op jit(solution)/shard_map/all_to_all | solution.py:242
  11.3 0.0 copy-start.3
  11.4 0.0 copy-start.1
  11.4 2.9 %shard_map.78 = (f32[32,32,128]{2,1,0:T(8,128)}, f32[32,128]{1,0:T(8,128)}, f32[17,32,128]{2,1,0:T(8,128)}, f32[17,32,128]{2,1,0:T(8,128)}) custom-call(s32[4]{0:T(128)} %pad_add_fusion.place.refs_0_, f32[1,32,32,512]{3,2,1,0:T(8,128)} %measured.1, f32[1,32,512]{2,1,0:T(8,128)} %frac.1), custom_call_target="tpu_custom_call" | custom-call | flops 4194304 | bytes 2097152 | tf_op jit(solution)/shard_map/pallas_call | solution.py:243
  14.3 0.0 copy-start
  14.3 0.0 copy-start.2
  14.3 3.0 %collective-permute-start = (f32[17,32,128]{2,1,0:T(8,128)}, f32[17,32,128]{2,1,0:T(8,128)S(1)}, u32[]{:S(2)}, u32[]{:S(2)}) collective-permute-start(f32[17,32,128]{2,1,0:T(8,128)} %get-tuple-element.22), channel_id=1, source_target_pairs={{1,2},{2,1},{3,4},{4,3},{5,6},{6,5},{7,8},{8,7},{9,10},{10,9},{11,... | collective-permute-start | bytes 835592 | tf_op jit(solution)/shard_map/ppermute | solution.py:223
  17.4 0.7 collective-permute-start.1
  18.1 0.0 copy-done.3
  18.1 6.3 %collective-permute-start.2 = (s32[1,32]{1,0:T(1,128)S(1)}, s32[1,32]{1,0:T(1,128)S(1)}, u32[]{:S(2)}, u32[]{:S(2)}) collective-permute-start(s32[1,32]{1,0:T(1,128)S(1)} %copy-done.3), channel_id=1, source_target_pairs={{1,2},{2,1},{3,4},{4,3},{5,6},{6,5},{7,8},{8,7},{9,10},{10,9},{11,... | collective-permute-start | bytes 392 | tf_op jit(solution)/shard_map/ppermute | solution.py:223
  24.4 0.1 collective-permute-start.3
  24.5 5.2 %collective-permute-done.2.shift_o = s32[1,32]{1,0:T(1,128)S(1)} collective-permute-done((s32[1,32]{1,0:T(1,128)S(1)}, s32[1,32]{1,0:T(1,128)S(1)}, u32[]{:S(2)}, u32[]{:S(2)}) %collective-permute-start.2) | collective-permute-done | bytes 160 | tf_op jit(solution)/shard_map/ppermute | solution.py:223
  29.7 0.0 collective-permute-done.3.shift_e
  29.7 0.0 collective-permute-done.measured_o
  29.7 0.0 collective-permute-done.1.measured_e
  29.7 8.7 %all-to-all-done.parts = f32[4,33,32,128]{3,2,1,0:T(8,128)S(1)} async-done(((f32[4,33,32,128]{3,2,1,0:T(8,128)}), f32[4,33,32,128]{3,2,1,0:T(8,128)S(1)}, u32[]{:S(2)}, u32[]{:S(2)}) %all-to-all-start) | async-done | bytes 2162720 | tf_op jit(solution)/shard_map/all_to_all | solution.py:242
  38.4 0.0 copy-done.1
  38.4 0.7 shard_map.79
  39.1 2.0 %collective-permute-start.4 = (f32[20,32,128]{2,1,0:T(8,128)S(1)}, f32[20,32,128]{2,1,0:T(8,128)S(1)}, u32[]{:S(2)}, u32[]{:S(2)}) collective-permute-start(f32[20,32,128]{2,1,0:T(8,128)S(1)} %get-tuple-element.29), channel_id=1, source_target_pairs={{1,2},{2,1},{3,4},{4,3},{5,6},{6,5},{7,8},{8,7},{9,10},{10,9},{11,... | collective-permute-start | bytes 983048 | tf_op jit(solution)/shard_map/ppermute | solution.py:223
  41.1 1.6 %collective-permute-start.5 = (f32[20,32,128]{2,1,0:T(8,128)S(1)}, f32[20,32,128]{2,1,0:T(8,128)S(1)}, u32[]{:S(2)}, u32[]{:S(2)}) collective-permute-start(f32[20,32,128]{2,1,0:T(8,128)S(1)} %get-tuple-element.30), channel_id=1, source_target_pairs={{0,1},{1,0},{2,3},{3,2},{4,5},{5,4},{6,7},{7,6},{8,9},{9,8},{10,11... | collective-permute-start | bytes 983048 | tf_op jit(solution)/shard_map/ppermute | solution.py:226
  42.7 12.9 %collective-permute-done.4.halo_o = f32[20,32,128]{2,1,0:T(8,128)S(1)} collective-permute-done((f32[20,32,128]{2,1,0:T(8,128)S(1)}, f32[20,32,128]{2,1,0:T(8,128)S(1)}, u32[]{:S(2)}, u32[]{:S(2)}) %collective-permute-start.4) | collective-permute-done | bytes 327712 | tf_op jit(solution)/shard_map/ppermute | solution.py:223
  55.6 0.0 collective-permute-done.5.halo_e
  55.6 0.0 copy-done
  55.6 0.0 copy-done.2
  55.6 1.9 %shard_map.80 = (f32[16,32,128]{2,1,0:T(8,128)S(1)}, f32[17,32,128]{2,1,0:T(8,128)S(1)}, f32[4,48,128]{2,1,0:T(8,128)}) custom-call(s32[4]{0:T(128)S(1)} %copy-done.1, s32[1,32]{1,0:T(1,128)S(1)} %copy-done.3, s32[1,32]{1,0:T(1,128)S(1)} %collective-permute-done.2.shift_o, s32[1,32]{1,0:T(1,128)S(1)} %collective-permute-done.3.shift_e, ...), custom_call_target="tpu_custom_call" | custom-call | flops 4194304 | bytes 2097152 | tf_op jit(solution)/shard_map/pallas_call | solution.py:259
  57.5 0.0 collective-permute-start.6
  57.5 3.3 %all-to-all-start.2 = ((f32[4,48,128]{2,1,0:T(8,128)}), f32[4,48,128]{2,1,0:T(8,128)S(1)}, u32[]{:S(2)}, u32[]{:S(2)}) async-start(f32[4,48,128]{2,1,0:T(8,128)} %get-tuple-element.37), calls=%async_computation.2 | async-start | bytes 196608 | tf_op jit(solution)/shard_map/all_to_all | solution.py:274
  60.8 3.2 %collective-permute-done.6.other = f32[17,32,128]{2,1,0:T(8,128)S(1)} collective-permute-done((f32[17,32,128]{2,1,0:T(8,128)S(1)}, f32[17,32,128]{2,1,0:T(8,128)S(1)}, u32[]{:S(2)}, u32[]{:S(2)}) %collective-permute-start.6) | collective-permute-done | bytes 278560 | tf_op jit(solution)/shard_map/ppermute | solution.py:273
  64.0 2.3 %shard_map.81 = f32[8,16,32,128]{3,2,1,0:T(8,128)} custom-call(f32[32,128]{1,0:T(8,128)S(1)} %get-tuple-element.25.weights, f32[16,32,128]{2,1,0:T(8,128)S(1)} %get-tuple-element.35.own, f32[17,32,128]{2,1,0:T(8,128)S(1)} %collective-permute-done.6.other), custom_call_target="tpu_custom_call" | custom-call | flops 4194304 | bytes 2097152 | tf_op jit(solution)/shard_map/pallas_call | solution.py:275
  66.4 3.0 %all-to-all-done.2.refs_1_ = f32[4,48,128]{2,1,0:T(8,128)S(1)} async-done(((f32[4,48,128]{2,1,0:T(8,128)}), f32[4,48,128]{2,1,0:T(8,128)S(1)}, u32[]{:S(2)}, u32[]{:S(2)}) %all-to-all-start.2) | async-done | bytes 98336 | tf_op jit(solution)/shard_map/all_to_all | solution.py:274
  69.3 8.8 %all-to-all-start.1 = ((f32[8,16,32,128]{3,2,1,0:T(8,128)}), f32[8,16,32,128]{3,2,1,0:T(8,128)S(1)}, u32[]{:S(2)}, u32[]{:S(2)}) async-start(f32[8,16,32,128]{3,2,1,0:T(8,128)} %shard_map.81), calls=%async_computation.1 | async-start | bytes 4194304 | tf_op jit(solution)/shard_map/all_to_all | solution.py:278
  78.1 1.6 %shard_map.83 = f32[1,32,512]{2,1,0:T(8,128)} custom-call(s32[4]{0:T(128)S(1)} %copy-done.1, f32[4,48,128]{2,1,0:T(8,128)S(1)} %all-to-all-done.2.refs_1_), custom_call_target="tpu_custom_call" | custom-call | flops 4194304 | bytes 2097152 | tf_op jit(solution)/shard_map/pallas_call | solution.py:283
  79.7 14.6 %all-to-all-done.1.parts = f32[8,16,32,128]{3,2,1,0:T(8,128)S(1)} async-done(((f32[8,16,32,128]{3,2,1,0:T(8,128)}), f32[8,16,32,128]{3,2,1,0:T(8,128)S(1)}, u32[]{:S(2)}, u32[]{:S(2)}) %all-to-all-start.1) | async-done | bytes 2097184 | tf_op jit(solution)/shard_map/all_to_all | solution.py:278
  94.3 1.4 %shard_map.82 = f32[32,32,512]{2,1,0:T(8,128)} custom-call(f32[8,16,32,128]{3,2,1,0:T(8,128)S(1)} %all-to-all-done.1.parts), custom_call_target="tpu_custom_call" | custom-call | flops 4194304 | bytes 2097152 | tf_op jit(solution)/shard_map/pallas_call | solution.py:284
Async XLA Ops:
  6.9 31.5 %all-to-all-start = ((f32[4,33,32,128]{3,2,1,0:T(8,128)}), f32[4,33,32,128]{3,2,1,0:T(8,128)S(1)}, u32[]{:S(2)}, u32[]{:S(2)}) async-start(f32[4,33,32,128]{3,2,1,0:T(8,128)} %shard_map.77), calls=%async_computation | async-start | bytes 4325376 | tf_op jit(solution)/shard_map/all_to_all | solution.py:242
  11.3 6.7 %copy-start.3 = (s32[1,32]{1,0:T(1,128)S(1)}, s32[1,32]{1,0:T(1,128)}, u32[]{:S(2)}) copy-start(s32[1,32]{1,0:T(1,128)} %shift.1) | copy-start | bytes 388
  11.4 27.0 %copy-start.1 = (s32[4]{0:T(128)S(1)}, s32[4]{0:T(128)}, u32[]{:S(2)}) copy-start(s32[4]{0:T(128)} %pad_add_fusion.place.refs_0_) | copy-start | bytes 52
  14.3 41.3 %copy-start = (f32[32,32,128]{2,1,0:T(8,128)S(1)}, f32[32,32,128]{2,1,0:T(8,128)}, u32[]{:S(2)}) copy-start(f32[32,32,128]{2,1,0:T(8,128)} %get-tuple-element.31.measured) | copy-start | bytes 1572868
  14.3 41.3 %copy-start.2 = (f32[32,128]{1,0:T(8,128)S(1)}, f32[32,128]{1,0:T(8,128)}, u32[]{:S(2)}) copy-start(f32[32,128]{1,0:T(8,128)} %get-tuple-element.34.frac) | copy-start | bytes 49156
  14.3 15.4 %collective-permute-start = (f32[17,32,128]{2,1,0:T(8,128)}, f32[17,32,128]{2,1,0:T(8,128)S(1)}, u32[]{:S(2)}, u32[]{:S(2)}) collective-permute-start(f32[17,32,128]{2,1,0:T(8,128)} %get-tuple-element.22), channel_id=1, source_target_pairs={{1,2},{2,1},{3,4},{4,3},{5,6},{6,5},{7,8},{8,7},{9,10},{10,9},{11,... | collective-permute-start | bytes 835592 | tf_op jit(solution)/shard_map/ppermute | solution.py:223
  17.4 12.3 %collective-permute-start.1 = (f32[17,32,128]{2,1,0:T(8,128)}, f32[17,32,128]{2,1,0:T(8,128)S(1)}, u32[]{:S(2)}, u32[]{:S(2)}) collective-permute-start(f32[17,32,128]{2,1,0:T(8,128)} %get-tuple-element.23), channel_id=1, source_target_pairs={{0,1},{1,0},{2,3},{3,2},{4,5},{5,4},{6,7},{7,6},{8,9},{9,8},{10,11... | collective-permute-start | bytes 835592 | tf_op jit(solution)/shard_map/ppermute | solution.py:226
  18.1 11.6 %collective-permute-start.2 = (s32[1,32]{1,0:T(1,128)S(1)}, s32[1,32]{1,0:T(1,128)S(1)}, u32[]{:S(2)}, u32[]{:S(2)}) collective-permute-start(s32[1,32]{1,0:T(1,128)S(1)} %copy-done.3), channel_id=1, source_target_pairs={{1,2},{2,1},{3,4},{4,3},{5,6},{6,5},{7,8},{8,7},{9,10},{10,9},{11,... | collective-permute-start | bytes 392 | tf_op jit(solution)/shard_map/ppermute | solution.py:223
  24.4 5.3 %collective-permute-start.3 = (s32[1,32]{1,0:T(1,128)S(1)}, s32[1,32]{1,0:T(1,128)S(1)}, u32[]{:S(2)}, u32[]{:S(2)}) collective-permute-start(s32[1,32]{1,0:T(1,128)S(1)} %copy-done.3), channel_id=1, source_target_pairs={{0,1},{1,0},{2,3},{3,2},{4,5},{5,4},{6,7},{7,6},{8,9},{9,8},{10,11... | collective-permute-start | bytes 392 | tf_op jit(solution)/shard_map/ppermute | solution.py:226
  39.1 16.5 %collective-permute-start.4 = (f32[20,32,128]{2,1,0:T(8,128)S(1)}, f32[20,32,128]{2,1,0:T(8,128)S(1)}, u32[]{:S(2)}, u32[]{:S(2)}) collective-permute-start(f32[20,32,128]{2,1,0:T(8,128)S(1)} %get-tuple-element.29), channel_id=1, source_target_pairs={{1,2},{2,1},{3,4},{4,3},{5,6},{6,5},{7,8},{8,7},{9,10},{10,9},{11,... | collective-permute-start | bytes 983048 | tf_op jit(solution)/shard_map/ppermute | solution.py:223
  41.1 14.5 %collective-permute-start.5 = (f32[20,32,128]{2,1,0:T(8,128)S(1)}, f32[20,32,128]{2,1,0:T(8,128)S(1)}, u32[]{:S(2)}, u32[]{:S(2)}) collective-permute-start(f32[20,32,128]{2,1,0:T(8,128)S(1)} %get-tuple-element.30), channel_id=1, source_target_pairs={{0,1},{1,0},{2,3},{3,2},{4,5},{5,4},{6,7},{7,6},{8,9},{9,8},{10,11... | collective-permute-start | bytes 983048 | tf_op jit(solution)/shard_map/ppermute | solution.py:226
  57.5 6.5 %collective-permute-start.6 = (f32[17,32,128]{2,1,0:T(8,128)S(1)}, f32[17,32,128]{2,1,0:T(8,128)S(1)}, u32[]{:S(2)}, u32[]{:S(2)}) collective-permute-start(f32[17,32,128]{2,1,0:T(8,128)S(1)} %get-tuple-element.36), channel_id=1, source_target_pairs={{0,128},{128,0},{1,129},{129,1},{2,130},{130,2},{3,131},{131,3},{4... | collective-permute-start | bytes 835592 | tf_op jit(solution)/shard_map/ppermute | solution.py:273
  57.5 11.9 %all-to-all-start.2 = ((f32[4,48,128]{2,1,0:T(8,128)}), f32[4,48,128]{2,1,0:T(8,128)S(1)}, u32[]{:S(2)}, u32[]{:S(2)}) async-start(f32[4,48,128]{2,1,0:T(8,128)} %get-tuple-element.37), calls=%async_computation.2 | async-start | bytes 196608 | tf_op jit(solution)/shard_map/all_to_all | solution.py:274
  69.3 25.0 %all-to-all-start.1 = ((f32[8,16,32,128]{3,2,1,0:T(8,128)}), f32[8,16,32,128]{3,2,1,0:T(8,128)S(1)}, u32[]{:S(2)}, u32[]{:S(2)}) async-start(f32[8,16,32,128]{3,2,1,0:T(8,128)} %shard_map.81), calls=%async_computation.1 | async-start | bytes 4194304 | tf_op jit(solution)/shard_map/all_to_all | solution.py:278

commit v5 on v0

v5 whole, which is shorter than its diff:
```python
import jax
import jax.numpy as jnp
from jax import lax
from jax.experimental import pallas as pl
from jax.experimental.pallas import tpu as pltpu
from jax.sharding import PartitionSpec as P

HALO = 16
ITS = 4
DIFFUSION = 0.2
EDGE = 8
SPAN = 3 * HALO
ROWS = 24
LANES = 128
ROOM = 56
HIGH = lax.Precision.HIGHEST
F32 = jnp.float32
VMEM = pl.BlockSpec(memory_space=pltpu.VMEM)
SMEM = pl.BlockSpec(memory_space=pltpu.SMEM)
ANY = pl.BlockSpec(memory_space=pltpu.HBM)


def call(kernel, outs, in_specs, scratch=(), out_specs=None, aliases=None, limit=16):
    return pl.pallas_call(
        kernel,
        out_shape=[jax.ShapeDtypeStruct(o, F32) for o in outs],
        in_specs=in_specs,
        out_specs=out_specs or [VMEM] * len(outs),
        scratch_shapes=list(scratch),
        input_output_aliases=aliases or {},
        compiler_params=pltpu.CompilerParams(vmem_limit_bytes=limit << 20),
        cost_estimate=pl.CostEstimate(flops=1 << 22, bytes_accessed=1 << 21, transcendentals=0),
    )


def outer(a, b):
    return lax.dot_general(
        a, b, (((0,), (0,)), ((), ())), precision=HIGH, preferred_element_type=F32
    )


def rim(place, volume, out, block, sem):
    cols = volume.shape[1]
    start = pl.multiple_of((cols - 8) * (1 - place[1]), 8)
    copy = pltpu.make_async_copy(volume.at[:, pl.ds(start, 8), :], block, sem.at[0])
    copy.start()
    copy.wait()
    out[...] = jnp.where(place[1] == 0, block[:, 7, :], block[:, 0, :])


def bundle(place, shift, measured, frac, whole, same, cross, sems):
    angles, cols = measured.shape[1:3]
    lanes = pl.ds(pl.multiple_of(place[0] * LANES, LANES), LANES)
    first = pltpu.make_async_copy(measured.at[0, :, :, lanes], whole.at[pl.ds(0, angles)], sems.at[0])
    second = pltpu.make_async_copy(frac.at[0, :, lanes], whole.at[angles], sems.at[1])
    first.start()
    second.start()
    for k in range(cols):
        value = jnp.full((1, LANES), shift[0, k], jnp.int32).astype(F32)
        whole[angles + 1, k : k + 1, :] = value
    first.wait()
    second.wait()
    here = pl.multiple_of(HALO * (1 - place[1]), HALO)
    there = pl.multiple_of(HALO * place[1], HALO)
    same[...] = whole[:, pl.ds(here, HALO), :]
    cross[...] = whole[:, pl.ds(there, HALO), :]


def cut(place, volume, out, block, staged, sems, done):
    copies, sent = [], []
    for k in range(HALO // 8):
        columns = pl.ds(pl.multiple_of(HALO * place[1] + 8 * k, 8), 8)
        copies.append(pltpu.make_async_copy(volume.at[:, columns, :], block.at[k], sems.at[k]))
        copies[k].start()
    for k, copy in enumerate(copies):
        copy.wait()
        turned = jnp.swapaxes(block[k], 0, 1)
        for chunk in range(out.shape[0]):
            staged[k, chunk] = turned[:, :, chunk * LANES : (chunk + 1) * LANES]
        sent.append(pltpu.make_async_copy(staged.at[k], out.at[:, pl.ds(8 * k, 8)], done.at[k]))
        sent[k].start()
    for copy in sent:
        copy.wait()


def pack(place, index, other, table, volume, beside, out, block, sem):
    depth, cols, _ = volume.shape
    start = pl.multiple_of(HALO - 8 * place[1], 8)
    copy = pltpu.make_async_copy(volume.at[:, pl.ds(start, 8), :], block, sem.at[0])
    copy.start()
    row = lax.broadcasted_iota(jnp.int32, (depth, LANES), 0)
    lane = lax.broadcasted_iota(jnp.int32, (depth, LANES), 1)
    number = lax.broadcasted_iota(jnp.int32, (table.shape[1], index.shape[1]), 0)
    slabs = out.shape[0]
    for k, name in enumerate((index, other)):
        picker = (number == name[...]).astype(F32)
        flipped = jnp.dot(table[...], picker, precision=HIGH, preferred_element_type=F32)
        weights = outer(flipped, (lane == row + place[0] * depth).astype(F32))
        for chunk in range(slabs):
            out[chunk, k] = weights
    copy.wait()
    first = place[1] == 0
    inner = jnp.where(first, block[:, 0, :], block[:, 7, :])
    low = jnp.where(first, beside[...], inner)
    high = jnp.where(first, inner, beside[...])
    for chunk in range(slabs):
        lanes = slice(chunk * LANES, (chunk + 1) * LANES)
        out[chunk, 2] = low[:, lanes]
        out[chunk, 3] = high[:, lanes]


def split(place, made, *outs):
    slabs = made.shape[0]
    for k, out in enumerate(outs):
        to = place[0] + k
        out[...] = made[jnp.where(to >= slabs, to - slabs, to)]


def arrange(place, own, other, same, cross, seen, share, steps):
    phase = place[1]
    angles = own.shape[0] - 2
    middle = pl.multiple_of(HALO * (1 - phase), HALO)
    side = pl.multiple_of(2 * HALO * phase, HALO)
    for to, inside, beyond in ((phase, own, same), (1 - phase, other, cross)):
        for ref, start in ((inside, middle), (beyond, side)):
            size = ref.shape[1]
            seen[to, pl.ds(start, size)] = jnp.swapaxes(ref[0:angles], 0, 1)
            share[to, pl.ds(start, size), :] = ref[angles]
            steps[to, pl.ds(start, size), :] = ref[angles + 1]


def core(
    place, steps, parts, a, b, c, d, seen, share, out, kept, crossed, down, down_x, up, up_x,
    ext, grad, field, canvas, beside,
):
    slabs, half, depth, width = parts.shape
    angles = seen.shape[2]
    phase = place[1]

    mine, theirs = ((a[k] + b[k]) + (c[k] + d[k]) for k in range(2))
    weights = jnp.concatenate(
        [jnp.where(phase == 0, mine, theirs), jnp.where(phase == 0, theirs, mine)], axis=0
    )
    for k, ref in enumerate((a, b, c, d)):
        source = place[0] - k
        source = jnp.where(source < 0, source + slabs, source)
        rows = pl.ds(pl.multiple_of(source * depth, depth), depth)
        beside[0, rows, :] = ref[2]
        beside[1, rows, :] = ref[3]
    nothing = jnp.zeros((2 * angles, width), F32)

    def put(columns, at):
        value = jnp.concatenate(columns, axis=1)
        value = jnp.dot(weights, value, precision=HIGH, preferred_element_type=F32)
        for k in range(len(columns)):
            ext[at[k]] = value[:, k * width : (k + 1) * width]

    for k in range(0, half, 2):
        columns = [
            jnp.concatenate([parts[s, k + i] for s in range(slabs)], axis=0) for i in range(2)
        ]
        put(columns, (k + 2, k + 3))
    put([beside[0], beside[1]], (1, half + 2))
    ext[0] = nothing
    ext[half + 3] = nothing
    grad[...] = jnp.zeros_like(grad)
    field[...] = jnp.zeros_like(field)
    outermost = jnp.where((phase == 0) & (place[2] == 0), 1, 2)
    for q in range(2):
        rows = slice(q * angles, (q + 1) * angles)
        for j in range(seen.shape[1]):
            at = j + steps[q, j] - 14

            @pl.when((at >= 1) & (at <= half + 1))
            def _(q=q, j=j, at=at, rows=rows):
                lower, upper = ext[at, rows, :], ext[at + 1, rows, :]
                part = share[q, j : j + 1, :]
                rest = 1.0 - part
                resid = (rest * lower + part * upper) - seen[q, j]
                value = jnp.sum(resid * (upper - lower), axis=0, keepdims=True)
                field[q, j : j + 1, :] = jnp.where(at >= outermost, value, 0.0)
                grad[at, rows, :] = grad[at, rows, :] + rest * resid
                grad[at + 1, rows, :] = grad[at + 1, rows, :] + part * resid

    table = weights.T
    for k in range(0, half, 2):
        pair = jnp.concatenate([grad[k + 2], grad[k + 3]], axis=1)
        value = jnp.dot(table, pair, precision=HIGH, preferred_element_type=F32)
        for chunk in range(slabs):
            part = value[chunk * depth : (chunk + 1) * depth]
            for copy in (chunk, slabs + chunk):
                out[copy, k] = part[:, :width]
                out[copy, k + 1] = part[:, width:]
    canvas[...] = jnp.zeros_like(canvas)
    start = pl.multiple_of(HALO * phase, HALO)
    for q in range(2):
        canvas[q, pl.ds(start, seen.shape[1]), :] = field[q]
    for q, (home, left, right) in ((phase, (kept, down, up)), (1 - phase, (crossed, down_x, up_x))):
        home[...] = canvas[q, EDGE : EDGE + SPAN, :]
        left[...] = canvas[q, 0:ROWS, :]
        right[...] = canvas[q, canvas.shape[1] - ROWS :, :]


def collect(kept, crossed, left, left_x, right, right_x, out):
    total = kept[...] + crossed[...]
    out[0:ROWS, :] = total[0:ROWS] + (left[...] + left_x[...])
    out[ROWS:, :] = total[ROWS:] + (right[...] + right_x[...])


def diffuse(last, place, a, b, c, d, field, chunks):
    cols = field.shape[1]
    for k, ref in enumerate((a, b, c, d)):
        source = place[0] - k
        chunks[jnp.where(source < 0, source + 4, source)] = ref[...]
    wide = jnp.concatenate([chunks[k] for k in range(chunks.shape[0])], axis=1)
    height, total = wide.shape
    row = lax.broadcasted_iota(jnp.int32, wide.shape, 0)
    lane = lax.broadcasted_iota(jnp.int32, wide.shape, 1)
    outside = ((row < EDGE) & (place[2] == 0)) | ((row >= EDGE + cols) & (place[2] == last))
    for _ in range(ITS):
        after = pltpu.roll(wide, height - 1, 0)
        before = pltpu.roll(wide, 1, 0)
        right = jnp.where(lane == total - 1, 0.0, pltpu.roll(wide, total - 1, 1))
        left = jnp.where(lane == 0, 0.0, pltpu.roll(wide, 1, 1))
        laplace = after + before + right + left - 4.0 * wide
        wide = jnp.where(outside, 0.0, wide + DIFFUSION * laplace)
    field[0] = wide[EDGE : EDGE + cols]


def finish(parts, image, block, sems):
    slabs = parts.shape[0] // 2
    copies = []
    for k in range(image.shape[1] // 8):
        phase, start = divmod(8 * k, HALO)
        for chunk in range(slabs):
            block[k, :, :, chunk * LANES : (chunk + 1) * LANES] = jnp.swapaxes(
                parts[phase * slabs + chunk, start : start + 8], 0, 1
            )
        columns = pl.ds(8 * k, 8)
        copies.append(pltpu.make_async_copy(block.at[k], image.at[:, columns, :], sems.at[k]))
        copies[k].start()
    for copy in copies:
        copy.wait()


def move(block, target):
    phases, tiles = lax.axis_size("phase"), lax.axis_size("tile")
    route = []
    for phase in range(phases):
        for tile in range(tiles):
            to_phase, to_tile = target(phase, tile)
            if 0 <= to_tile < tiles:
                route.append((phase * tiles + tile, to_phase * tiles + to_tile))
    return lax.ppermute(block, ("phase", "tile"), route)


def body(volume, frac, shift, angle_index, depth_weights, measured):
    depth, cols, height = volume.shape
    angles = angle_index.shape[1]
    slabs, tiles, phases = (lax.axis_size(a) for a in ("slab", "tile", "phase"))
    group = phases * slabs
    place = jnp.stack(
        [lax.axis_index("slab"), lax.axis_index("phase"), lax.axis_index("tile")]
    ).astype(jnp.int32)
    octet = pltpu.VMEM((depth, 8, height), F32)
    blocks = pltpu.VMEM((cols // 8, depth, 8, height), F32)
    dma = pltpu.SemaphoreType.DMA

    def toward(phase, tile):
        return phase, tile + 1 - 2 * phase

    def across(phase, tile):
        return 1 - phase, tile - 1 + 2 * phase

    def partner(phase, tile):
        return 1 - phase, tile

    def around(block, distance):
        return lax.ppermute(block, "slab", [(i, (i + distance) % slabs) for i in range(slabs)])

    (edge,) = call(rim, [(depth, height)], [SMEM, ANY], [octet, dma((1,))], limit=ROOM)(
        place, volume
    )
    beside = move(edge, toward)
    index_other = move(angle_index, partner)
    bundles = [(angles + 2, cols, LANES)] + [(angles + 2, HALO, LANES)] * 2
    bundle_own, same, cross = call(
        bundle, bundles, [SMEM] * 2 + [ANY] * 2, [dma((2,))], limit=ROOM
    )(place, shift, measured, frac)
    bundle_other = move(bundle_own, partner)
    (parts,) = call(
        cut,
        [(slabs, HALO, depth, LANES)],
        [SMEM, ANY],
        [
            pltpu.VMEM((HALO // 8, depth, 8, height), F32),
            pltpu.VMEM((HALO // 8, slabs, 8, depth, LANES), F32),
            dma((HALO // 8,)),
            dma((HALO // 8,)),
        ],
        [ANY],
        limit=ROOM,
    )(place, volume)
    parts = lax.all_to_all(parts, "slab", 0, 0, tiled=True)
    same = move(same, toward)
    cross = move(cross, across)
    (extra,) = call(
        pack, [(slabs, 4, depth, LANES)], [SMEM, VMEM, VMEM, VMEM, ANY, VMEM], [octet, dma((1,))],
        limit=ROOM,
    )(place, angle_index, index_other, depth_weights.T, volume, beside)
    extras = call(split, [(4, depth, LANES)] * slabs, [SMEM, VMEM])(place, extra)
    extras = [extras[0]] + [around(extras[k], k) for k in range(1, slabs)]
    seen, share, steps = call(
        arrange,
        [(phases, SPAN, angles, LANES), (phases, SPAN, LANES), (phases, SPAN, LANES)],
        [SMEM] + [VMEM] * 4,
    )(place, bundle_own, bundle_other, same, cross)
    steps = steps[:, :, 0].astype(jnp.int32)
    parts, seen, share, steps, *extras = lax.optimization_barrier(
        (parts, seen, share, steps, *extras)
    )
    window, side = (SPAN, LANES), (ROWS, LANES)
    stack = (HALO + 4, 2 * angles, LANES)
    parts, kept, crossed, down, down_x, up, up_x = call(
        core,
        [(group, HALO, depth, LANES), window, window, side, side, side, side],
        [SMEM] * 2 + [VMEM] * 7,
        [
            pltpu.VMEM(stack, F32),
            pltpu.VMEM(stack, F32),
            pltpu.VMEM((phases, SPAN, LANES), F32),
            pltpu.VMEM((phases, 4 * HALO, LANES), F32),
            pltpu.VMEM((2, slabs * depth, LANES), F32),
        ],
    )(place, steps, parts, *extras, seen, share)
    parts = lax.all_to_all(parts, ("phase", "slab"), 0, 0, tiled=True)
    (field,) = call(collect, [window], [VMEM] * 6)(
        kept,
        move(crossed, partner),
        move(up, lambda phase, tile: (phase, tile + 1)),
        move(up_x, lambda phase, tile: (1 - phase, tile + 1)),
        move(down, lambda phase, tile: (phase, tile - 1)),
        move(down_x, lambda phase, tile: (1 - phase, tile - 1)),
    )
    fields = [field] + [around(field, k) for k in range(1, slabs)]

    def ending(*refs):
        diffuse(tiles - 1, *refs)

    (field,) = call(
        ending,
        [(1, cols, height)],
        [SMEM] + [VMEM] * 4,
        [pltpu.VMEM((slabs,) + window, F32)],
    )(place, *fields)
    (image,) = call(
        finish, [(depth, cols, height)], [VMEM], [blocks, dma((cols // 8,))], [ANY]
    )(parts)
    return image, field


def solution(mesh):
    return jax.shard_map(
        body,
        mesh=mesh,
        in_specs=(
            P("slab", "tile", None),
            P("phase", "tile", None),
            P("phase", "tile"),
            P("phase", None),
            P(None, "slab"),
            P("phase", None, "tile", None),
        ),
        out_specs=(P("slab", "tile", None), P("phase", "tile", None)),
        check_vma=False,
    )
```

time: 301 us -> 98.3 us (0.33); the launches traced: 297 us -> 97.1 us
  waiting for transfers between devices: 157 us -> 24.5 us
  other arithmetic: 29.3 us -> 0.77 us
  local copies, waits for them, and re-layouts: 30 us -> 2.9 us
  Pallas kernels: 0 us -> 18.8 us
  between operations: 14.1 us -> 0.83 us
  starting transfers between devices: 59 us -> 49.3 us
  matrix products: 7.28 us -> 0 us
    psum x3 -> x0, waiting for transfers between devices: 108 us -> none  [the longest x1 61.4 us: body(): projected = lax.psum(partial_proj, 'slab')]
    ppermute x12 -> x16, waiting for transfers between devices: 48.8 us -> 24.5 us  [the longest x10 18.5 us: move(): return lax.ppermute(block, ('phase', 'tile'), route)]
    pallas_call x0 -> x10, Pallas kernels: none -> 18.8 us  [the longest x1 3.55 us: body(): call(core, [(group, HALO, depth, LANES), window, window, side, side, side...]
    ppermute x12 -> x16, starting transfers between devices: 58.7 us -> 40.8 us  [the longest x10 29.9 us: move(): return lax.ppermute(block, ('phase', 'tile'), route)]
    scatter-add x2 -> x0, other arithmetic: 12.2 us -> none  [the longest x1 6.12 us: warp_local(): upper = jnp.take(image, columns + 1, axis=1)]
    unnamed x26 -> x14, local copies, waits for them, and re-layouts: 13.8 us -> 2.9 us
    all_to_all x0 -> x2, starting transfers between devices: none -> 8.42 us  [the longest x1 4.48 us: body(): parts = lax.all_to_all(parts, 'slab', 0, 0, tiled=True)]
    dot_general x3 -> x0, matrix products: 7.28 us -> none  [the longest x1 3.83 us: body(): spread = jnp.dot(weights.T, residual, precision=lax.Precision.HIGHEST)]
  transfers between devices with their start and end apart: 15 -> 18, of which waited for: 11 -> 8; matrix products, arithmetic and copies ran while one was open for 5% -> 0% of each run, Pallas kernels for 0% -> 11%
where the time goes in v5:
time: 98.3 us; the launch traced here: 97.1 us
  starting transfers between devices  49.3 us (50%)
  waiting for transfers between devices  24.5 us (25%)
  Pallas kernels  18.8 us (19%)
  local copies, waits for them, and re-layouts  2.9 us (3%)
    ppermute x10, starting transfers between devices, move(): return lax.ppermute(block, ('phase', 'tile'), route)  29.9 us
    ppermute x10, waiting for transfers between devices, move(): return lax.ppermute(block, ('phase', 'tile'), route)  18.5 us
    ppermute x6, starting transfers between devices, around(): lax.ppermute(block, 'slab', [(i, (i + distance) % slabs) for i in range(s...  11 us
    ppermute x6, waiting for transfers between devices, around(): lax.ppermute(block, 'slab', [(i, (i + distance) % slabs) for i in range(s...  6.06 us
    all_to_all x1, starting transfers between devices, body(): parts = lax.all_to_all(parts, 'slab', 0, 0, tiled=True)  4.48 us
    all_to_all x1, starting transfers between devices, body(): parts = lax.all_to_all(parts, ('phase', 'slab'), 0, 0, tiled=True)  3.95 us
    pallas_call x1, Pallas kernels, body(): call(core, [(group, HALO, depth, LANES), window, window, side, side, side...  3.55 us
    unnamed x14, local copies, waits for them, and re-layouts  2.9 us
  transfers between devices with their start and end apart: 18, of which 8 were waited for; matrix products, arithmetic and copies ran while one was open for 0% of the time, Pallas kernels for 11%

profile of v5, /device:TPU:128, one launch (start us, length us, event | category | flops | bytes accessed | tf_op | source)
XLA Modules:
  0.0 97.1 jit_solution(13477006613007452157)
XLA Ops:
  0.6 0.7 pad_add_fusion.place.refs_0_
  1.3 2.8 %shard_map.77 = f32[4,16,32,128]{3,2,1,0:T(8,128)} custom-call(s32[3]{0:T(128)} %pad_add_fusion.place.refs_0_, f32[32,32,512]{2,1,0:T(8,128)} %volume.5), custom_call_target="tpu_custom_call" | custom-call | flops 4194304 | bytes 2097152 | tf_op jit(solution)/shard_map/pallas_call | solution.py:291
  4.1 4.5 %all-to-all-start = ((f32[4,16,32,128]{3,2,1,0:T(8,128)}), f32[4,16,32,128]{3,2,1,0:T(8,128)S(1)}, u32[]{:S(2)}, u32[]{:S(2)}) async-start(f32[4,16,32,128]{3,2,1,0:T(8,128)} %shard_map.77), calls=%async_computation | async-start | bytes 2097152 | tf_op jit(solution)/shard_map/all_to_all | solution.py:304
  8.6 2.9 %shard_map.78 = (f32[34,32,128]{2,1,0:T(8,128)}, f32[34,16,128]{2,1,0:T(8,128)}, f32[34,16,128]{2,1,0:T(8,128)}) custom-call(s32[3]{0:T(128)} %pad_add_fusion.place.refs_0_, s32[1,32]{1,0:T(1,128)} %shift.1, f32[1,32,32,512]{3,2,1,0:T(8,128)} %measured.1, f32[1,32,512]{2,1,0:T(8,128)} %frac.1), custom_call_target="tpu_custom_call" | custom-call | flops 4194304 | bytes 2097152 | tf_op jit(solution)/shard_map/pallas_call | solution.py:287
  11.5 1.1 %collective-permute-start = (f32[34,32,128]{2,1,0:T(8,128)}, f32[34,32,128]{2,1,0:T(8,128)S(1)}, u32[]{:S(2)}, u32[]{:S(2)}) collective-permute-start(f32[34,32,128]{2,1,0:T(8,128)} %get-tuple-element.27.own), channel_id=1, source_target_pairs={{0,128},{1,129},{2,130},{3,131},{4,132},{5,133},{6,134},{7,135},{8... | collective-permute-start | bytes 1671176 | tf_op jit(solution)/shard_map/ppermute | solution.py:254
  12.6 1.9 %collective-permute-start.1 = (f32[34,16,128]{2,1,0:T(8,128)}, f32[34,16,128]{2,1,0:T(8,128)S(1)}, u32[]{:S(2)}, u32[]{:S(2)}) collective-permute-start(f32[34,16,128]{2,1,0:T(8,128)} %get-tuple-element.28), channel_id=1, source_target_pairs={{0,1},{1,2},{2,3},{3,4},{4,5},{5,6},{6,7},{7,8},{8,9},{9,10},{10,1... | collective-permute-start | bytes 835592 | tf_op jit(solution)/shard_map/ppermute | solution.py:254
  14.5 3.5 %collective-permute-start.2 = (f32[34,16,128]{2,1,0:T(8,128)}, f32[34,16,128]{2,1,0:T(8,128)S(1)}, u32[]{:S(2)}, u32[]{:S(2)}) collective-permute-start(f32[34,16,128]{2,1,0:T(8,128)} %get-tuple-element.29), channel_id=1, source_target_pairs={{1,128},{2,129},{3,130},{4,131},{5,132},{6,133},{7,134},{8,135},{9... | collective-permute-start | bytes 835592 | tf_op jit(solution)/shard_map/ppermute | solution.py:254
  18.1 2.4 %shard_map.80 = f32[32,512]{1,0:T(8,128)} custom-call(s32[3]{0:T(128)} %pad_add_fusion.place.refs_0_, f32[32,32,512]{2,1,0:T(8,128)} %volume.5), custom_call_target="tpu_custom_call" | custom-call | flops 4194304 | bytes 2097152 | tf_op jit(solution)/shard_map/pallas_call | solution.py:281
  20.4 2.4 %collective-permute-start.4 = (f32[32,512]{1,0:T(8,128)}, f32[32,512]{1,0:T(8,128)S(1)}, u32[]{:S(2)}, u32[]{:S(2)}) collective-permute-start(f32[32,512]{1,0:T(8,128)} %shard_map.80), channel_id=1, source_target_pairs={{0,1},{1,2},{2,3},{3,4},{4,5},{5,6},{6,7},{7,8},{8,9},{9,10},{10,1... | collective-permute-start | bytes 196616 | tf_op jit(solution)/shard_map/ppermute | solution.py:254
  22.9 4.6 %collective-permute-start.3 = (s32[1,32]{1,0:T(1,128)S(1)}, s32[1,32]{1,0:T(1,128)S(1)}, u32[]{:S(2)}, u32[]{:S(2)}) collective-permute-start(s32[1,32]{1,0:T(1,128)S(1)} %copy-done.5), channel_id=1, source_target_pairs={{0,128},{1,129},{2,130},{3,131},{4,132},{5,133},{6,134},{7,135},{8... | collective-permute-start | bytes 392 | tf_op jit(solution)/shard_map/ppermute | solution.py:254
  27.5 8.0 %collective-permute-done.3.other = s32[1,32]{1,0:T(1,128)S(1)} collective-permute-done((s32[1,32]{1,0:T(1,128)S(1)}, s32[1,32]{1,0:T(1,128)S(1)}, u32[]{:S(2)}, u32[]{:S(2)}) %collective-permute-start.3) | collective-permute-done | bytes 160 | tf_op jit(solution)/shard_map/ppermute | solution.py:254
  35.5 1.8 %collective-permute-done.4.beside = f32[32,512]{1,0:T(8,128)S(1)} collective-permute-done((f32[32,512]{1,0:T(8,128)}, f32[32,512]{1,0:T(8,128)S(1)}, u32[]{:S(2)}, u32[]{:S(2)}) %collective-permute-start.4) | collective-permute-done | bytes 65568 | tf_op jit(solution)/shard_map/ppermute | solution.py:254
  37.3 0.6 copy-done.4
  37.9 2.8 %shard_map.81.made = f32[4,4,32,128]{3,2,1,0:T(8,128)} custom-call(s32[3]{0:T(128)} %pad_add_fusion.place.refs_0_, s32[1,32]{1,0:T(1,128)} %index.1, s32[1,32]{1,0:T(1,128)} %copy-done.6, f32[32,680]{1,0:T(8,128)} %bitcast.4, f32[32,32,512]{2,1,0:T(8,128)} %volume.5, f32[32,512]{1,0:T(8,128)} %copy-done.4), custom_call_target="tpu_custom_call" | custom-call | flops 4194304 | bytes 2097152 | tf_op jit(solution)/shard_map/pallas_call | solution.py:307
  40.7 0.9 copy-done.1
  41.6 0.6 shard_map.82
  42.2 1.8 %collective-permute-start.5 = (f32[4,32,128]{2,1,0:T(8,128)S(1)}, f32[4,32,128]{2,1,0:T(8,128)S(1)}, u32[]{:S(2)}, u32[]{:S(2)}) collective-permute-start(f32[4,32,128]{2,1,0:T(8,128)S(1)} %get-tuple-element.34), channel_id=1, source_target_pairs={{0,32},{32,64},{64,96},{96,0},{1,33},{33,65},{65,97},{97,1},{2,34}... | collective-permute-start | bytes 196616 | tf_op jit(solution)/shard_map/ppermute | solution.py:279
  44.0 2.7 %collective-permute-start.6 = (f32[4,32,128]{2,1,0:T(8,128)S(1)}, f32[4,32,128]{2,1,0:T(8,128)S(1)}, u32[]{:S(2)}, u32[]{:S(2)}) collective-permute-start(f32[4,32,128]{2,1,0:T(8,128)S(1)} %get-tuple-element.35), channel_id=1, source_target_pairs={{0,64},{32,96},{64,0},{96,32},{1,65},{33,97},{65,1},{97,33},{2,66}... | collective-permute-start | bytes 196616 | tf_op jit(solution)/shard_map/ppermute | solution.py:279
  46.7 0.0 collective-permute-done.1.same
  46.7 1.5 %collective-permute-start.7 = (f32[4,32,128]{2,1,0:T(8,128)S(1)}, f32[4,32,128]{2,1,0:T(8,128)S(1)}, u32[]{:S(2)}, u32[]{:S(2)}) collective-permute-start(f32[4,32,128]{2,1,0:T(8,128)S(1)} %get-tuple-element.36), channel_id=1, source_target_pairs={{0,96},{32,0},{64,32},{96,64},{1,97},{33,1},{65,33},{97,65},{2,98}... | collective-permute-start | bytes 196616 | tf_op jit(solution)/shard_map/ppermute | solution.py:279
  48.2 0.0 collective-permute-done.2.cross
  48.2 0.0 collective-permute-done.other
  48.2 0.8 shard_map.79
  49.0 0.1 convert_reduce_fusion.steps
  49.1 0.0 collective-permute-done.5.b
  49.1 0.7 collective-permute-done.6.c
  49.8 1.2 %collective-permute-done.7.d = f32[4,32,128]{2,1,0:T(8,128)S(1)} collective-permute-done((f32[4,32,128]{2,1,0:T(8,128)S(1)}, f32[4,32,128]{2,1,0:T(8,128)S(1)}, u32[]{:S(2)}, u32[]{:S(2)}) %collective-permute-start.7) | collective-permute-done | bytes 65568 | tf_op jit(solution)/shard_map/ppermute | solution.py:279
  51.0 0.0 all-to-all-done.parts
  51.0 3.6 %shard_map.83 = (f32[8,16,32,128]{3,2,1,0:T(8,128)S(1)}, f32[48,128]{1,0:T(8,128)S(1)}, f32[48,128]{1,0:T(8,128)S(1)}, f32[24,128]{1,0:T(8,128)S(1)}, f32[24,128...) custom-call(s32[3]{0:T(128)S(1)} %copy-done.3, s32[2,48]{1,0:T(2,128)S(1)} %convert_reduce_fusion.steps, ...), custom_call_target="tpu_custom_call" | custom-call | flops 4194304 | bytes 2097152 | tf_op jit(solution)/shard_map/pallas_call | solution.py:324
  54.5 0.0 copy-start
  54.5 1.3 %copy-done = f32[8,16,32,128]{3,2,1,0:T(8,128)} copy-done((f32[8,16,32,128]{3,2,1,0:T(8,128)}, f32[8,16,32,128]{3,2,1,0:T(8,128)S(1)}, u32[]{:S(2)}) %copy-start) | copy-done | bytes 2097176
  55.8 3.9 %all-to-all-start.1 = ((f32[8,16,32,128]{3,2,1,0:T(8,128)}), f32[8,16,32,128]{3,2,1,0:T(8,128)S(1)}, u32[]{:S(2)}, u32[]{:S(2)}) async-start(f32[8,16,32,128]{3,2,1,0:T(8,128)} %copy-done), calls=%async_computation.1 | async-start | bytes 4194304 | tf_op jit(solution)/shard_map/all_to_all | solution.py:336
  59.8 2.0 %collective-permute-start.8 = (f32[48,128]{1,0:T(8,128)S(1)}, f32[48,128]{1,0:T(8,128)S(1)}, u32[]{:S(2)}, u32[]{:S(2)}) collective-permute-start(f32[48,128]{1,0:T(8,128)S(1)} %get-tuple-element.47), channel_id=1, source_target_pairs={{0,128},{1,129},{2,130},{3,131},{4,132},{5,133},{6,134},{7,135},{8... | collective-permute-start | bytes 73736 | tf_op jit(solution)/shard_map/ppermute | solution.py:254
  61.8 1.9 %collective-permute-start.9 = (f32[24,128]{1,0:T(8,128)S(1)}, f32[24,128]{1,0:T(8,128)S(1)}, u32[]{:S(2)}, u32[]{:S(2)}) collective-permute-start(f32[24,128]{1,0:T(8,128)S(1)} %get-tuple-element.48), channel_id=1, source_target_pairs={{0,1},{1,2},{2,3},{3,4},{4,5},{5,6},{6,7},{7,8},{8,9},{9,10},{10,1... | collective-permute-start | bytes 36872 | tf_op jit(solution)/shard_map/ppermute | solution.py:254
  63.7 1.9 %collective-permute-start.10 = (f32[24,128]{1,0:T(8,128)S(1)}, f32[24,128]{1,0:T(8,128)S(1)}, u32[]{:S(2)}, u32[]{:S(2)}) collective-permute-start(f32[24,128]{1,0:T(8,128)S(1)} %get-tuple-element.49), channel_id=1, source_target_pairs={{0,129},{1,130},{2,131},{3,132},{4,133},{5,134},{6,135},{7,136},{8... | collective-permute-start | bytes 36872 | tf_op jit(solution)/shard_map/ppermute | solution.py:254
  65.7 7.9 %collective-permute-start.11 = (f32[24,128]{1,0:T(8,128)S(1)}, f32[24,128]{1,0:T(8,128)S(1)}, u32[]{:S(2)}, u32[]{:S(2)}) collective-permute-start(f32[24,128]{1,0:T(8,128)S(1)} %get-tuple-element.50), channel_id=1, source_target_pairs={{1,0},{2,1},{3,2},{4,3},{5,4},{6,5},{7,6},{8,7},{9,8},{10,9},{11,1... | collective-permute-start | bytes 36872 | tf_op jit(solution)/shard_map/ppermute | solution.py:254
  73.5 2.6 %collective-permute-start.12 = (f32[24,128]{1,0:T(8,128)S(1)}, f32[24,128]{1,0:T(8,128)S(1)}, u32[]{:S(2)}, u32[]{:S(2)}) collective-permute-start(f32[24,128]{1,0:T(8,128)S(1)} %get-tuple-element.51), channel_id=1, source_target_pairs={{1,128},{2,129},{3,130},{4,131},{5,132},{6,133},{7,134},{8,135},{9... | collective-permute-start | bytes 36872 | tf_op jit(solution)/shard_map/ppermute | solution.py:254
  76.1 8.7 %collective-permute-done.9.left = f32[24,128]{1,0:T(8,128)S(1)} collective-permute-done((f32[24,128]{1,0:T(8,128)S(1)}, f32[24,128]{1,0:T(8,128)S(1)}, u32[]{:S(2)}, u32[]{:S(2)}) %collective-permute-start.9) | collective-permute-done | bytes 12320 | tf_op jit(solution)/shard_map/ppermute | solution.py:254
  84.8 0.0 collective-permute-done.10.left_x
  84.8 0.0 collective-permute-done.8.crossed
  84.8 3.7 %collective-permute-start.15 = (f32[48,128]{1,0:T(8,128)S(1)}, f32[48,128]{1,0:T(8,128)S(1)}, u32[]{:S(2)}, u32[]{:S(2)}) collective-permute-start(f32[48,128]{1,0:T(8,128)S(1)} %shard_map.85.refs_1_), channel_id=1, source_target_pairs={{0,96},{32,0},{64,32},{96,64},{1,97},{33,1},{65,33},{97,65},{2,98}... | collective-permute-start | bytes 73736 | tf_op jit(solution)/shard_map/ppermute | solution.py:279
  88.5 0.5 collective-permute-start.14
  88.9 0.9 collective-permute-start.13
  89.8 0.1 collective-permute-done.15.refs_4_
  90.0 3.8 %collective-permute-done.14.refs_3_ = f32[48,128]{1,0:T(8,128)S(1)} collective-permute-done((f32[48,128]{1,0:T(8,128)S(1)}, f32[48,128]{1,0:T(8,128)S(1)}, u32[]{:S(2)}, u32[]{:S(2)}) %collective-permute-start.14) | collective-permute-done | bytes 24608 | tf_op jit(solution)/shard_map/ppermute | solution.py:279
  93.8 0.3 collective-permute-done.13.refs_2_
  94.1 1.6 %shard_map.86 = f32[1,32,512]{2,1,0:T(8,128)} custom-call(s32[3]{0:T(128)S(1)} %copy-done.3, f32[48,128]{1,0:T(8,128)S(1)} %shard_map.85.refs_1_, f32[48,128]{1,0:T(8,128)S(1)} %collective-permute-done.13.refs_2_, f32[48,128]{1,0:T(8,128)S(1)} %collective-permute-done.14.refs_3_, f32[48,128]{1,0:T(8,128)S(1)} %collective-permute-done.15.refs_4_), custom_call_target="tpu_custom_call" | custom-call | flops 4194304 | bytes 2097152 | tf_op jit(solution)/shard_map/pallas_call | solution.py:350
  95.7 1.4 %shard_map.84 = f32[32,32,512]{2,1,0:T(8,128)} custom-call(f32[8,16,32,128]{3,2,1,0:T(8,128)S(1)} %all-to-all-done.1.parts), custom_call_target="tpu_custom_call" | custom-call | flops 4194304 | bytes 2097152 | tf_op jit(solution)/shard_map/pallas_call | solution.py:356
  (14 shorter events, 0.0 us)
Async XLA Ops:
  4.1 46.8 %all-to-all-start = ((f32[4,16,32,128]{3,2,1,0:T(8,128)}), f32[4,16,32,128]{3,2,1,0:T(8,128)S(1)}, u32[]{:S(2)}, u32[]{:S(2)}) async-start(f32[4,16,32,128]{3,2,1,0:T(8,128)} %shard_map.77), calls=%async_computation | async-start | bytes 2097152 | tf_op jit(solution)/shard_map/all_to_all | solution.py:304
  8.6 14.3 %copy-start.5 = (s32[1,32]{1,0:T(1,128)S(1)}, s32[1,32]{1,0:T(1,128)}, u32[]{:S(2)}) copy-start(s32[1,32]{1,0:T(1,128)} %index.1) | copy-start | bytes 388
  11.5 36.7 %collective-permute-start = (f32[34,32,128]{2,1,0:T(8,128)}, f32[34,32,128]{2,1,0:T(8,128)S(1)}, u32[]{:S(2)}, u32[]{:S(2)}) collective-permute-start(f32[34,32,128]{2,1,0:T(8,128)} %get-tuple-element.27.own), channel_id=1, source_target_pairs={{0,128},{1,129},{2,130},{3,131},{4,132},{5,133},{6,134},{7,135},{8... | collective-permute-start | bytes 1671176 | tf_op jit(solution)/shard_map/ppermute | solution.py:254
  12.6 34.1 %collective-permute-start.1 = (f32[34,16,128]{2,1,0:T(8,128)}, f32[34,16,128]{2,1,0:T(8,128)S(1)}, u32[]{:S(2)}, u32[]{:S(2)}) collective-permute-start(f32[34,16,128]{2,1,0:T(8,128)} %get-tuple-element.28), channel_id=1, source_target_pairs={{0,1},{1,2},{2,3},{3,4},{4,5},{5,6},{6,7},{7,8},{8,9},{9,10},{10,1... | collective-permute-start | bytes 835592 | tf_op jit(solution)/shard_map/ppermute | solution.py:254
  14.5 26.2 %copy-start.3 = (s32[3]{0:T(128)S(1)}, s32[3]{0:T(128)}, u32[]{:S(2)}) copy-start(s32[3]{0:T(128)} %pad_add_fusion.place.refs_0_) | copy-start | bytes 40
  14.5 33.7 %copy-start.2 = (f32[34,32,128]{2,1,0:T(8,128)S(1)}, f32[34,32,128]{2,1,0:T(8,128)}, u32[]{:S(2)}) copy-start(f32[34,32,128]{2,1,0:T(8,128)} %get-tuple-element.27.own) | copy-start | bytes 1671172
  14.5 33.6 %collective-permute-start.2 = (f32[34,16,128]{2,1,0:T(8,128)}, f32[34,16,128]{2,1,0:T(8,128)S(1)}, u32[]{:S(2)}, u32[]{:S(2)}) collective-permute-start(f32[34,16,128]{2,1,0:T(8,128)} %get-tuple-element.29), channel_id=1, source_target_pairs={{1,128},{2,129},{3,130},{4,131},{5,132},{6,133},{7,134},{8,135},{9... | collective-permute-start | bytes 835592 | tf_op jit(solution)/shard_map/ppermute | solution.py:254
  20.4 16.8 %collective-permute-start.4 = (f32[32,512]{1,0:T(8,128)}, f32[32,512]{1,0:T(8,128)S(1)}, u32[]{:S(2)}, u32[]{:S(2)}) collective-permute-start(f32[32,512]{1,0:T(8,128)} %shard_map.80), channel_id=1, source_target_pairs={{0,1},{1,2},{2,3},{3,4},{4,5},{5,6},{6,7},{7,8},{8,9},{9,10},{10,1... | collective-permute-start | bytes 196616 | tf_op jit(solution)/shard_map/ppermute | solution.py:254
  22.9 12.6 %collective-permute-start.3 = (s32[1,32]{1,0:T(1,128)S(1)}, s32[1,32]{1,0:T(1,128)S(1)}, u32[]{:S(2)}, u32[]{:S(2)}) collective-permute-start(s32[1,32]{1,0:T(1,128)S(1)} %copy-done.5), channel_id=1, source_target_pairs={{0,128},{1,129},{2,130},{3,131},{4,132},{5,133},{6,134},{7,135},{8... | collective-permute-start | bytes 392 | tf_op jit(solution)/shard_map/ppermute | solution.py:254
  35.5 1.8 %copy-start.6 = (s32[1,32]{1,0:T(1,128)}, s32[1,32]{1,0:T(1,128)S(1)}, u32[]{:S(2)}) copy-start(s32[1,32]{1,0:T(1,128)S(1)} %collective-permute-done.3.other) | copy-start | bytes 388
  37.3 0.6 copy-start.4
  40.7 1.0 copy-start.1
  42.2 6.9 %collective-permute-start.5 = (f32[4,32,128]{2,1,0:T(8,128)S(1)}, f32[4,32,128]{2,1,0:T(8,128)S(1)}, u32[]{:S(2)}, u32[]{:S(2)}) collective-permute-start(f32[4,32,128]{2,1,0:T(8,128)S(1)} %get-tuple-element.34), channel_id=1, source_target_pairs={{0,32},{32,64},{64,96},{96,0},{1,33},{33,65},{65,97},{97,1},{2,34}... | collective-permute-start | bytes 196616 | tf_op jit(solution)/shard_map/ppermute | solution.py:279
  44.0 5.8 %collective-permute-start.6 = (f32[4,32,128]{2,1,0:T(8,128)S(1)}, f32[4,32,128]{2,1,0:T(8,128)S(1)}, u32[]{:S(2)}, u32[]{:S(2)}) collective-permute-start(f32[4,32,128]{2,1,0:T(8,128)S(1)} %get-tuple-element.35), channel_id=1, source_target_pairs={{0,64},{32,96},{64,0},{96,32},{1,65},{33,97},{65,1},{97,33},{2,66}... | collective-permute-start | bytes 196616 | tf_op jit(solution)/shard_map/ppermute | solution.py:279
  46.7 4.3 %collective-permute-start.7 = (f32[4,32,128]{2,1,0:T(8,128)S(1)}, f32[4,32,128]{2,1,0:T(8,128)S(1)}, u32[]{:S(2)}, u32[]{:S(2)}) collective-permute-start(f32[4,32,128]{2,1,0:T(8,128)S(1)} %get-tuple-element.36), channel_id=1, source_target_pairs={{0,96},{32,0},{64,32},{96,64},{1,97},{33,1},{65,33},{97,65},{2,98}... | collective-permute-start | bytes 196616 | tf_op jit(solution)/shard_map/ppermute | solution.py:279
  54.5 1.3 %copy-start = (f32[8,16,32,128]{3,2,1,0:T(8,128)}, f32[8,16,32,128]{3,2,1,0:T(8,128)S(1)}, u32[]{:S(2)}) copy-start(f32[8,16,32,128]{3,2,1,0:T(8,128)S(1)} %get-tuple-element.45) | copy-start | bytes 6291460
  55.8 39.8 %all-to-all-start.1 = ((f32[8,16,32,128]{3,2,1,0:T(8,128)}), f32[8,16,32,128]{3,2,1,0:T(8,128)S(1)}, u32[]{:S(2)}, u32[]{:S(2)}) async-start(f32[8,16,32,128]{3,2,1,0:T(8,128)} %copy-done), calls=%async_computation.1 | async-start | bytes 4194304 | tf_op jit(solution)/shard_map/all_to_all | solution.py:336
  59.8 25.0 %collective-permute-start.8 = (f32[48,128]{1,0:T(8,128)S(1)}, f32[48,128]{1,0:T(8,128)S(1)}, u32[]{:S(2)}, u32[]{:S(2)}) collective-permute-start(f32[48,128]{1,0:T(8,128)S(1)} %get-tuple-element.47), channel_id=1, source_target_pairs={{0,128},{1,129},{2,130},{3,131},{4,132},{5,133},{6,134},{7,135},{8... | collective-permute-start | bytes 73736 | tf_op jit(solution)/shard_map/ppermute | solution.py:254
  61.8 23.0 %collective-permute-start.9 = (f32[24,128]{1,0:T(8,128)S(1)}, f32[24,128]{1,0:T(8,128)S(1)}, u32[]{:S(2)}, u32[]{:S(2)}) collective-permute-start(f32[24,128]{1,0:T(8,128)S(1)} %get-tuple-element.48), channel_id=1, source_target_pairs={{0,1},{1,2},{2,3},{3,4},{4,5},{5,6},{6,7},{7,8},{8,9},{9,10},{10,1... | collective-permute-start | bytes 36872 | tf_op jit(solution)/shard_map/ppermute | solution.py:254
  63.7 21.0 %collective-permute-start.10 = (f32[24,128]{1,0:T(8,128)S(1)}, f32[24,128]{1,0:T(8,128)S(1)}, u32[]{:S(2)}, u32[]{:S(2)}) collective-permute-start(f32[24,128]{1,0:T(8,128)S(1)} %get-tuple-element.49), channel_id=1, source_target_pairs={{0,129},{1,130},{2,131},{3,132},{4,133},{5,134},{6,135},{7,136},{8... | collective-permute-start | bytes 36872 | tf_op jit(solution)/shard_map/ppermute | solution.py:254
  65.7 19.1 %collective-permute-start.11 = (f32[24,128]{1,0:T(8,128)S(1)}, f32[24,128]{1,0:T(8,128)S(1)}, u32[]{:S(2)}, u32[]{:S(2)}) collective-permute-start(f32[24,128]{1,0:T(8,128)S(1)} %get-tuple-element.50), channel_id=1, source_target_pairs={{1,0},{2,1},{3,2},{4,3},{5,4},{6,5},{7,6},{8,7},{9,8},{10,9},{11,1... | collective-permute-start | bytes 36872 | tf_op jit(solution)/shard_map/ppermute | solution.py:254
  73.5 11.3 %collective-permute-start.12 = (f32[24,128]{1,0:T(8,128)S(1)}, f32[24,128]{1,0:T(8,128)S(1)}, u32[]{:S(2)}, u32[]{:S(2)}) collective-permute-start(f32[24,128]{1,0:T(8,128)S(1)} %get-tuple-element.51), channel_id=1, source_target_pairs={{1,128},{2,129},{3,130},{4,131},{5,132},{6,133},{7,134},{8,135},{9... | collective-permute-start | bytes 36872 | tf_op jit(solution)/shard_map/ppermute | solution.py:254
  84.8 5.2 %collective-permute-start.15 = (f32[48,128]{1,0:T(8,128)S(1)}, f32[48,128]{1,0:T(8,128)S(1)}, u32[]{:S(2)}, u32[]{:S(2)}) collective-permute-start(f32[48,128]{1,0:T(8,128)S(1)} %shard_map.85.refs_1_), channel_id=1, source_target_pairs={{0,96},{32,0},{64,32},{96,64},{1,97},{33,1},{65,33},{97,65},{2,98}... | collective-permute-start | bytes 73736 | tf_op jit(solution)/shard_map/ppermute | solution.py:279
  88.5 5.3 %collective-permute-start.14 = (f32[48,128]{1,0:T(8,128)S(1)}, f32[48,128]{1,0:T(8,128)S(1)}, u32[]{:S(2)}, u32[]{:S(2)}) collective-permute-start(f32[48,128]{1,0:T(8,128)S(1)} %shard_map.85.refs_1_), channel_id=1, source_target_pairs={{0,64},{32,96},{64,0},{96,32},{1,65},{33,97},{65,1},{97,33},{2,66}... | collective-permute-start | bytes 73736 | tf_op jit(solution)/shard_map/ppermute | solution.py:279
  88.9 5.1 %collective-permute-start.13 = (f32[48,128]{1,0:T(8,128)S(1)}, f32[48,128]{1,0:T(8,128)S(1)}, u32[]{:S(2)}, u32[]{:S(2)}) collective-permute-start(f32[48,128]{1,0:T(8,128)S(1)} %shard_map.85.refs_1_), channel_id=1, source_target_pairs={{0,32},{32,64},{64,96},{96,0},{1,33},{33,65},{65,97},{97,1},{2,34}... | collective-permute-start | bytes 73736 | tf_op jit(solution)/shard_map/ppermute | solution.py:279

commit v6 on v5

v6 whole, which is shorter than its diff:
```python
import jax
import jax.numpy as jnp
from jax import lax
from jax.experimental import pallas as pl
from jax.experimental.pallas import tpu as pltpu
from jax.sharding import PartitionSpec as P

HALO = 16
ITS = 4
DIFFUSION = 0.2
EDGE = 8
SPAN = 3 * HALO
ROWS = 24
LANES = 128
ROOM = 56
HIGH = lax.Precision.HIGHEST
F32 = jnp.float32
VMEM = pl.BlockSpec(memory_space=pltpu.VMEM)
SMEM = pl.BlockSpec(memory_space=pltpu.SMEM)
ANY = pl.BlockSpec(memory_space=pltpu.HBM)


def call(kernel, outs, in_specs, scratch=(), out_specs=None, aliases=None, limit=16):
    return pl.pallas_call(
        kernel,
        out_shape=[jax.ShapeDtypeStruct(o, F32) for o in outs],
        in_specs=in_specs,
        out_specs=out_specs or [VMEM] * len(outs),
        scratch_shapes=list(scratch),
        input_output_aliases=aliases or {},
        compiler_params=pltpu.CompilerParams(vmem_limit_bytes=limit << 20),
        cost_estimate=pl.CostEstimate(flops=1 << 22, bytes_accessed=1 << 21, transcendentals=0),
    )


def outer(a, b):
    return lax.dot_general(
        a, b, (((0,), (0,)), ((), ())), precision=HIGH, preferred_element_type=F32
    )


def load(
    place, shift, measured, frac, volume, whole, same, cross, rim, parts, block, half, sems, done
):
    angles, cols = measured.shape[1:3]
    phase = place[1]
    copies = []

    def start(source, target):
        copies.append(pltpu.make_async_copy(source, target, sems.at[len(copies)]))
        copies[-1].start()

    columns = pl.ds(pl.multiple_of(HALO * phase, HALO), HALO)
    slabs = parts.shape[0]
    for k in range(slabs):
        start(volume.at[:, columns, pl.ds(k * LANES, LANES)], half.at[k])
    edge = pl.multiple_of((cols - 8) * (1 - phase), 8)
    start(volume.at[:, pl.ds(edge, 8), :], block)
    lanes = pl.ds(pl.multiple_of(place[0] * LANES, LANES), LANES)
    start(measured.at[0, :, :, lanes], whole.at[pl.ds(0, angles)])
    start(frac.at[0, :, lanes], whole.at[angles])
    for k in range(cols):
        whole[angles + 1, k : k + 1, :] = jnp.full((1, LANES), shift[0, k], jnp.int32).astype(F32)
    sent = []
    for k in range(slabs):
        copies[k].wait()
        sent.append(pltpu.make_async_copy(half.at[k], parts.at[k], done.at[k]))
        sent[k].start()
    for copy in copies[slabs:]:
        copy.wait()
    rim[...] = jnp.where(phase == 0, block[:, 7, :], block[:, 0, :])
    same[...] = whole[:, pl.ds(pl.multiple_of(HALO * (1 - phase), HALO), HALO), :]
    cross[...] = whole[:, columns, :]
    for copy in sent:
        copy.wait()


def pack(place, index, other, rim, table, volume, first, second, third, fourth, block, low, high, sem):
    depth, cols, _ = volume.shape
    angles = index.shape[1]
    start = pl.multiple_of(HALO - 8 * place[1], 8)
    copy = pltpu.make_async_copy(volume.at[:, pl.ds(start, 8), :], block, sem.at[0])
    copy.start()
    numbers = jnp.concatenate([index[...], other[...]], axis=1)
    count = table.shape[1]
    picker = (lax.broadcasted_iota(jnp.int32, (count, 2 * angles), 0) == numbers).astype(F32)
    flipped = jnp.dot(table[...], picker, precision=HIGH, preferred_element_type=F32)
    row = lax.broadcasted_iota(jnp.int32, (depth, LANES), 0)
    lane = lax.broadcasted_iota(jnp.int32, (depth, LANES), 1)
    weights = outer(flipped, (lane == row + place[0] * depth).astype(F32))
    left = place[1] == 0
    beside = rim[...]
    copy.wait()
    inner = jnp.where(left, block[:, 0, :], block[:, 7, :])
    low[...] = jnp.where(left, beside, inner)
    high[...] = jnp.where(left, inner, beside)
    slabs = volume.shape[2] // LANES
    for k, out in enumerate((first, second, third, fourth)):
        to = place[0] + k
        to = jnp.where(to >= slabs, to - slabs, to)
        lanes = pl.ds(pl.multiple_of(to * LANES, LANES), LANES)
        out[0] = weights[0:angles]
        out[1] = weights[angles:]
        out[2] = low[:, lanes]
        out[3] = high[:, lanes]


def arrange(place, own, other, same, cross, seen, share, steps):
    phase = place[1]
    angles = own.shape[0] - 2
    middle = pl.multiple_of(HALO * (1 - phase), HALO)
    side = pl.multiple_of(2 * HALO * phase, HALO)
    for to, inside, beyond in ((phase, own, same), (1 - phase, other, cross)):
        for ref, start in ((inside, middle), (beyond, side)):
            size = ref.shape[1]
            seen[to, pl.ds(start, size)] = jnp.swapaxes(ref[0:angles], 0, 1)
            share[to, pl.ds(start, size), :] = ref[angles]
            steps[to, pl.ds(start, size), :] = ref[angles + 1]


def core(
    place, steps, parts, a, b, c, d, seen, share, grad, weights, own, other,
    ext, field, canvas, beside,
):
    slabs, depth, half, width = parts.shape
    angles = seen.shape[2]
    phase = place[1]
    mine, theirs = ((a[k] + b[k]) + (c[k] + d[k]) for k in range(2))
    table = jnp.concatenate(
        [jnp.where(phase == 0, mine, theirs), jnp.where(phase == 0, theirs, mine)], axis=0
    )
    weights[...] = table
    for k, ref in enumerate((a, b, c, d)):
        source = place[0] - k
        source = jnp.where(source < 0, source + slabs, source)
        rows = pl.ds(pl.multiple_of(source * depth, depth), depth)
        beside[0, rows, :] = ref[2]
        beside[1, rows, :] = ref[3]
    nothing = jnp.zeros((2 * angles, width), F32)

    def put(columns, at):
        value = jnp.concatenate(columns, axis=1)
        value = jnp.dot(table, value, precision=HIGH, preferred_element_type=F32)
        for k in range(len(columns)):
            ext[at[k]] = value[:, k * width : (k + 1) * width]

    for base in range(0, half, 8):
        turned = [jnp.swapaxes(parts[s, :, base : base + 8, :], 0, 1) for s in range(slabs)]
        for k in range(0, 8, 2):
            columns = [
                jnp.concatenate([turned[s][k + i] for s in range(slabs)], axis=0)
                for i in range(2)
            ]
            put(columns, (base + k + 2, base + k + 3))
    put([beside[0], beside[1]], (1, half + 2))
    ext[0] = nothing
    ext[half + 3] = nothing
    grad[...] = jnp.zeros_like(grad)
    field[...] = jnp.zeros_like(field)
    outermost = jnp.where((phase == 0) & (place[2] == 0), 1, 2)
    for q in range(2):
        rows = slice(q * angles, (q + 1) * angles)
        for j in range(seen.shape[1]):
            at = j + steps[q, j] - 14

            @pl.when((at >= 1) & (at <= half + 1))
            def _(q=q, j=j, at=at, rows=rows):
                lower, upper = ext[at, rows, :], ext[at + 1, rows, :]
                part = share[q, j : j + 1, :]
                rest = 1.0 - part
                resid = (rest * lower + part * upper) - seen[q, j]
                value = jnp.sum(resid * (upper - lower), axis=0, keepdims=True)
                field[q, j : j + 1, :] = jnp.where(at >= outermost, value, 0.0)
                grad[at, rows, :] = grad[at, rows, :] + rest * resid
                grad[at + 1, rows, :] = grad[at + 1, rows, :] + part * resid

    canvas[...] = jnp.zeros_like(canvas)
    start = pl.multiple_of(HALO * phase, HALO)
    for q in range(2):
        canvas[q, pl.ds(start, seen.shape[1]), :] = field[q]
    own[...] = canvas[phase]
    other[...] = canvas[1 - phase]


def spread(grad, weights, out, staged, sems):
    slabs, half, depth, width = staged.shape
    table = weights[...].T
    copies = []
    for k in range(0, half, 2):
        pair = jnp.concatenate([grad[k + 2], grad[k + 3]], axis=1)
        value = jnp.dot(table, pair, precision=HIGH, preferred_element_type=F32)
        for chunk in range(slabs):
            part = value[chunk * depth : (chunk + 1) * depth]
            staged[chunk, k] = part[:, :width]
            staged[chunk, k + 1] = part[:, width:]
        if k % 4 == 2:
            columns = pl.ds(k - 2, 4)
            for to in range(2):
                target = out.at[pl.ds(to * slabs, slabs), columns]
                copies.append(
                    pltpu.make_async_copy(staged.at[:, columns], target, sems.at[len(copies)])
                )
                copies[-1].start()
    for copy in copies:
        copy.wait()


def merge(place, own, other, kept, side_o, side_e):
    total = own[...] + other[...]
    kept[...] = total[EDGE : EDGE + SPAN]
    left, right = total[0:ROWS], total[total.shape[0] - ROWS :]
    odd = place[3] == 1
    side_o[...] = jnp.where(odd, right, left)
    side_e[...] = jnp.where(odd, left, right)


def collect(place, kept, side_o, side_e, out):
    odd = place[3] == 1
    from_left = jnp.where(odd, side_e[...], side_o[...])
    from_right = jnp.where(odd, side_o[...], side_e[...])
    out[0:ROWS, :] = kept[0:ROWS] + from_left
    out[ROWS:, :] = kept[ROWS:] + from_right


def diffuse(last, place, a, b, c, d, field, chunks):
    cols = field.shape[1]
    for k, ref in enumerate((a, b, c, d)):
        source = place[0] - k
        chunks[jnp.where(source < 0, source + 4, source)] = ref[...]
    wide = jnp.concatenate([chunks[k] for k in range(chunks.shape[0])], axis=1)
    height, total = wide.shape
    row = lax.broadcasted_iota(jnp.int32, wide.shape, 0)
    lane = lax.broadcasted_iota(jnp.int32, wide.shape, 1)
    outside = ((row < EDGE) & (place[2] == 0)) | ((row >= EDGE + cols) & (place[2] == last))
    for _ in range(ITS):
        after = pltpu.roll(wide, height - 1, 0)
        before = pltpu.roll(wide, 1, 0)
        right = jnp.where(lane == total - 1, 0.0, pltpu.roll(wide, total - 1, 1))
        left = jnp.where(lane == 0, 0.0, pltpu.roll(wide, 1, 1))
        laplace = after + before + right + left - 4.0 * wide
        wide = jnp.where(outside, 0.0, wide + DIFFUSION * laplace)
    field[0] = wide[EDGE : EDGE + cols]


def finish(parts, image, block, sems):
    slabs = parts.shape[0] // 2
    copies = []
    for k in range(image.shape[1] // 8):
        phase, start = divmod(8 * k, HALO)
        for chunk in range(slabs):
            block[k, :, :, chunk * LANES : (chunk + 1) * LANES] = jnp.swapaxes(
                parts[phase * slabs + chunk, start : start + 8], 0, 1
            )
        columns = pl.ds(8 * k, 8)
        copies.append(pltpu.make_async_copy(block.at[k], image.at[:, columns, :], sems.at[k]))
        copies[k].start()
    for copy in copies:
        copy.wait()


def move(block, target):
    phases, tiles = lax.axis_size("phase"), lax.axis_size("tile")
    route = []
    for phase in range(phases):
        for tile in range(tiles):
            to_phase, to_tile = target(phase, tile)
            if 0 <= to_tile < tiles:
                route.append((phase * tiles + tile, to_phase * tiles + to_tile))
    return lax.ppermute(block, ("phase", "tile"), route)


def body(volume, frac, shift, angle_index, depth_weights, measured):
    depth, cols, height = volume.shape
    angles = angle_index.shape[1]
    slabs, tiles, phases = (lax.axis_size(a) for a in ("slab", "tile", "phase"))
    group = phases * slabs
    tile = lax.axis_index("tile")
    place = jnp.stack(
        [lax.axis_index("slab"), lax.axis_index("phase"), tile, tile % 2]
    ).astype(jnp.int32)
    octet = pltpu.VMEM((depth, 8, height), F32)
    blocks = pltpu.VMEM((cols // 8, depth, 8, height), F32)
    dma = pltpu.SemaphoreType.DMA

    def toward(phase, tile):
        return phase, tile + 1 - 2 * phase

    def across(phase, tile):
        return 1 - phase, tile - 1 + 2 * phase

    def partner(phase, tile):
        return 1 - phase, tile

    def around(block, distance):
        return lax.ppermute(block, "slab", [(i, (i + distance) % slabs) for i in range(slabs)])

    bundles = [(angles + 2, cols, LANES)] + [(angles + 2, HALO, LANES)] * 2
    message = (slabs, depth, HALO, LANES)
    bundle_own, same, cross, rim, parts = call(
        load,
        bundles + [(depth, height), message],
        [SMEM] * 2 + [ANY] * 3,
        [octet, pltpu.VMEM(message, F32), dma((slabs + 3,)), dma((slabs,))],
        [VMEM] * 4 + [ANY],
        limit=ROOM,
    )(place, shift, measured, frac, volume)
    rim = move(rim, toward)
    index_other = move(angle_index, partner)
    bundle_other = move(bundle_own, partner)
    parts, index_other = lax.optimization_barrier((parts, index_other))
    parts = lax.all_to_all(parts, "slab", 0, 0, tiled=True)
    same = move(same, toward)
    cross = move(cross, across)
    wide = pltpu.VMEM((depth, height), F32)
    extras = call(
        pack,
        [(4, depth, LANES)] * slabs,
        [SMEM] + [VMEM] * 4 + [ANY],
        [octet, wide, wide, dma((1,))],
    )(place, angle_index, index_other, rim, depth_weights.T, volume)
    extras = [extras[0]] + [around(extras[k], k) for k in range(1, slabs)]
    seen, share, steps = call(
        arrange,
        [(phases, SPAN, angles, LANES), (phases, SPAN, LANES), (phases, SPAN, LANES)],
        [SMEM] + [VMEM] * 4,
    )(place, bundle_own, bundle_other, same, cross)
    steps = steps[:, :, 0].astype(jnp.int32)
    parts, seen, share, steps, *extras = lax.optimization_barrier(
        (parts, seen, share, steps, *extras)
    )
    window, side, canvas = (SPAN, LANES), (ROWS, LANES), (4 * HALO, LANES)
    stack = (HALO + 4, 2 * angles, LANES)
    grad, weights, own, other = call(
        core,
        [stack, (2 * angles, LANES), canvas, canvas],
        [SMEM] * 2 + [VMEM] * 7,
        [
            pltpu.VMEM(stack, F32),
            pltpu.VMEM((phases, SPAN, LANES), F32),
            pltpu.VMEM((phases,) + canvas, F32),
            pltpu.VMEM((2, slabs * depth, LANES), F32),
        ],
    )(place, steps, parts, *extras, seen, share)
    (parts,) = call(
        spread,
        [(group, HALO, depth, LANES)],
        [VMEM] * 2,
        [pltpu.VMEM((slabs, HALO, depth, LANES), F32), dma((HALO // 2,))],
        [ANY],
        limit=ROOM,
    )(grad, weights)
    other = move(other, partner)
    parts, other = lax.optimization_barrier((parts, other))
    parts = lax.all_to_all(parts, ("phase", "slab"), 0, 0, tiled=True)
    kept, side_o, side_e = call(merge, [window, side, side], [SMEM] + [VMEM] * 2)(
        place, own, other
    )
    pairs_e = [(i, i ^ 1) for i in range(tiles)]
    pairs_o = [(i, ((i + 1) ^ 1) - 1) for i in range(1, tiles - 1)]
    (field,) = call(collect, [window], [SMEM] + [VMEM] * 3)(
        place, kept, lax.ppermute(side_o, "tile", pairs_o), lax.ppermute(side_e, "tile", pairs_e)
    )
    fields = [field] + [around(field, k) for k in range(1, slabs)]

    def ending(*refs):
        diffuse(tiles - 1, *refs)

    (field,) = call(
        ending,
        [(1, cols, height)],
        [SMEM] + [VMEM] * 4,
        [pltpu.VMEM((slabs,) + window, F32)],
    )(place, *fields)
    (image,) = call(
        finish, [(depth, cols, height)], [VMEM], [blocks, dma((cols // 8,))], [ANY]
    )(parts)
    return image, field


def solution(mesh):
    return jax.shard_map(
        body,
        mesh=mesh,
        in_specs=(
            P("slab", "tile", None),
            P("phase", "tile", None),
            P("phase", "tile"),
            P("phase", None),
            P(None, "slab"),
            P("phase", None, "tile", None),
        ),
        out_specs=(P("slab", "tile", None), P("phase", "tile", None)),
        check_vma=False,
    )
```

time: 98.3 us -> 88.9 us (0.904)
  starting transfers between devices: 49.3 us -> 34.3 us
  waiting for transfers between devices: 24.5 us -> 34.4 us
  Pallas kernels: 18.8 us -> 15.8 us
  local copies, waits for them, and re-layouts: 2.9 us -> 1.48 us
    ppermute x10 -> x6, starting transfers between devices: 29.9 us -> 10.3 us  [move(): return lax.ppermute(block, ('phase', 'tile'), route)]
    ppermute x0 -> x2, waiting for transfers between devices: none -> 12.9 us  [the longest x1 12.9 us: body(): lax.ppermute(side_o, 'tile', pairs_o)]
    ppermute x0 -> x2, starting transfers between devices: none -> 3.04 us  [the longest x1 2.95 us: body(): lax.ppermute(side_o, 'tile', pairs_o)]
    pallas_call x7 -> x6, Pallas kernels: 14.9 us -> 11.9 us  [the longest x1 3.86 us: body(): call(load, bundles + [(depth, height), message], [SMEM] * 2 + [ANY] * 3,...]
    ppermute x10 -> x6, waiting for transfers between devices: 18.5 us -> 16.9 us  [move(): return lax.ppermute(block, ('phase', 'tile'), route)]
    ppermute x6, waiting for transfers between devices: 6.06 us -> 4.55 us  [around(): lax.ppermute(block, 'slab', [(i, (i + distance) % slabs) for i in range(s...]
    unnamed x14, local copies, waits for them, and re-layouts: 2.9 us -> 1.48 us
    ppermute x6, starting transfers between devices: 11 us -> 12.2 us  [around(): lax.ppermute(block, 'slab', [(i, (i + distance) % slabs) for i in range(s...]
  transfers between devices with their start and end apart: 18 -> 16, of which waited for: 8 -> 7; matrix products, arithmetic and copies ran while one was open for 0% -> 1% of each run, Pallas kernels for 11% -> 13%
where the time goes in v6:
time: 88.9 us; the launch traced here: 87.4 us
  waiting for transfers between devices  34.4 us (39%)
  starting transfers between devices  34.3 us (39%)
  Pallas kernels  15.8 us (18%)
  local copies, waits for them, and re-layouts  1.48 us (2%)
    ppermute x6, waiting for transfers between devices, move(): return lax.ppermute(block, ('phase', 'tile'), route)  16.9 us
    ppermute x1, waiting for transfers between devices, body(): lax.ppermute(side_o, 'tile', pairs_o)  12.9 us
    ppermute x6, starting transfers between devices, around(): lax.ppermute(block, 'slab', [(i, (i + distance) % slabs) for i in range(s...  12.2 us
    ppermute x6, starting transfers between devices, move(): return lax.ppermute(block, ('phase', 'tile'), route)  10.3 us
    all_to_all x1, starting transfers between devices, body(): parts = lax.all_to_all(parts, 'slab', 0, 0, tiled=True)  4.61 us
    ppermute x6, waiting for transfers between devices, around(): lax.ppermute(block, 'slab', [(i, (i + distance) % slabs) for i in range(s...  4.55 us
    all_to_all x1, starting transfers between devices, body(): parts = lax.all_to_all(parts, ('phase', 'slab'), 0, 0, tiled=True)  4.08 us
    pallas_call x1, Pallas kernels, body(): call(load, bundles + [(depth, height), message], [SMEM] * 2 + [ANY] * 3,...  3.86 us
  transfers between devices with their start and end apart: 16, of which 7 were waited for; matrix products, arithmetic and copies ran while one was open for 1% of the time, Pallas kernels for 13%

profile of v6, /device:TPU:128, one launch (start us, length us, event | category | flops | bytes accessed | tf_op | source)
XLA Modules:
  0.0 87.4 jit_solution(11119505168523760671)
XLA Ops:
  0.6 1.1 %collective-permute-start = (s32[1,32]{1,0:T(1,128)}, s32[1,32]{1,0:T(1,128)S(1)}, u32[]{:S(2)}, u32[]{:S(2)}) collective-permute-start(s32[1,32]{1,0:T(1,128)} %index.1), channel_id=1, source_target_pairs={{0,128},{1,129},{2,130},{3,131},{4,132},{5,133},{6,134},{7,135},{8... | collective-permute-start | bytes 392 | tf_op jit(solution)/shard_map/ppermute | solution.py:269
  1.7 0.6 pad_add_fusion.place.refs_0_
  2.4 3.9 %shard_map.77 = (f32[34,32,128]{2,1,0:T(8,128)}, f32[34,16,128]{2,1,0:T(8,128)}, f32[34,16,128]{2,1,0:T(8,128)}, f32[32,512]{1,0:T(8,128)}, f32[4,32,16,128]{3,2,1,0:T(8,128)}) custom-call(s32[4]{0:T(128)} %pad_add_fusion.place.refs_0_, s32[1,32]{1,0:T(1,128)} %shift.1, f32[1,32,32,512]{3,2,1,0:T(8,128)} %measured.1, f32[1,32,512]{2,1,0:T(8,128)} %frac.1, ...), custom_call_target="tpu_custom_call" | custom-call | flops 4194304 | bytes 2097152 | tf_op jit(solution)/shard_map/pallas_call | solution.py:299
  6.2 0.0 copy-start
  6.2 0.0 copy-start.5
  6.2 0.0 copy-start.6
  6.3 0.0 collective-permute-done.other
  6.3 4.6 %all-to-all-start = ((f32[4,32,16,128]{3,2,1,0:T(8,128)}), f32[4,32,16,128]{3,2,1,0:T(8,128)S(1)}, u32[]{:S(2)}, u32[]{:S(2)}) async-start(f32[4,32,16,128]{3,2,1,0:T(8,128)} %get-tuple-element.34), calls=%async_computation | async-start | bytes 2097152 | tf_op jit(solution)/shard_map/all_to_all | solution.py:311
  10.9 1.0 %collective-permute-start.1 = (f32[34,32,128]{2,1,0:T(8,128)}, f32[34,32,128]{2,1,0:T(8,128)S(1)}, u32[]{:S(2)}, u32[]{:S(2)}) collective-permute-start(f32[34,32,128]{2,1,0:T(8,128)} %get-tuple-element.35.own), channel_id=1, source_target_pairs={{0,128},{1,129},{2,130},{3,131},{4,132},{5,133},{6,134},{7,135},{8... | collective-permute-start | bytes 1671176 | tf_op jit(solution)/shard_map/ppermute | solution.py:269
  11.9 1.9 %collective-permute-start.2 = (f32[34,16,128]{2,1,0:T(8,128)}, f32[34,16,128]{2,1,0:T(8,128)S(1)}, u32[]{:S(2)}, u32[]{:S(2)}) collective-permute-start(f32[34,16,128]{2,1,0:T(8,128)} %get-tuple-element.36), channel_id=1, source_target_pairs={{0,1},{1,2},{2,3},{3,4},{4,5},{5,6},{6,7},{7,8},{8,9},{9,10},{10,1... | collective-permute-start | bytes 835592 | tf_op jit(solution)/shard_map/ppermute | solution.py:269
  13.8 4.3 %collective-permute-start.3 = (f32[34,16,128]{2,1,0:T(8,128)}, f32[34,16,128]{2,1,0:T(8,128)S(1)}, u32[]{:S(2)}, u32[]{:S(2)}) collective-permute-start(f32[34,16,128]{2,1,0:T(8,128)} %get-tuple-element.37), channel_id=1, source_target_pairs={{1,128},{2,129},{3,130},{4,131},{5,132},{6,133},{7,134},{8,135},{9... | collective-permute-start | bytes 835592 | tf_op jit(solution)/shard_map/ppermute | solution.py:269
  18.1 2.0 %collective-permute-start.4 = (f32[32,512]{1,0:T(8,128)}, f32[32,512]{1,0:T(8,128)S(1)}, u32[]{:S(2)}, u32[]{:S(2)}) collective-permute-start(f32[32,512]{1,0:T(8,128)} %get-tuple-element.42), channel_id=1, source_target_pairs={{0,1},{1,2},{2,3},{3,4},{4,5},{5,6},{6,7},{7,8},{8,9},{9,10},{10,1... | collective-permute-start | bytes 196616 | tf_op jit(solution)/shard_map/ppermute | solution.py:269
  20.1 15.5 %collective-permute-done.4.rim = f32[32,512]{1,0:T(8,128)S(1)} collective-permute-done((f32[32,512]{1,0:T(8,128)}, f32[32,512]{1,0:T(8,128)S(1)}, u32[]{:S(2)}, u32[]{:S(2)}) %collective-permute-start.4) | collective-permute-done | bytes 65568 | tf_op jit(solution)/shard_map/ppermute | solution.py:269
  35.6 1.3 %shard_map.79 = (f32[4,32,128]{2,1,0:T(8,128)S(1)}, f32[4,32,128]{2,1,0:T(8,128)S(1)}, f32[4,32,128]{2,1,0:T(8,128)S(1)}, f32[4,32,128]{2,1,0:T(8,128)S(1)}) custom-call(s32[4]{0:T(128)S(1)} %copy-done.5, s32[1,32]{1,0:T(1,128)S(1)} %copy-done.6, s32[1,32]{1,0:T(1,128)S(1)} %collective-permute-done.other, f32[32,512]{1,0:T(8,128)S(1)} %collective-permute-done.4.rim, ...), custom_call_target="tpu_custom_call" | custom-call | flops 4194304 | bytes 2097152 | tf_op jit(solution)/shard_map/pallas_call | solution.py:315
  37.0 1.8 %collective-permute-start.5 = (f32[4,32,128]{2,1,0:T(8,128)S(1)}, f32[4,32,128]{2,1,0:T(8,128)S(1)}, u32[]{:S(2)}, u32[]{:S(2)}) collective-permute-start(f32[4,32,128]{2,1,0:T(8,128)S(1)} %get-tuple-element.44), channel_id=1, source_target_pairs={{0,32},{32,64},{64,96},{96,0},{1,33},{33,65},{65,97},{97,1},{2,34}... | collective-permute-start | bytes 196616 | tf_op jit(solution)/shard_map/ppermute | solution.py:295
  38.8 2.7 %collective-permute-start.6 = (f32[4,32,128]{2,1,0:T(8,128)S(1)}, f32[4,32,128]{2,1,0:T(8,128)S(1)}, u32[]{:S(2)}, u32[]{:S(2)}) collective-permute-start(f32[4,32,128]{2,1,0:T(8,128)S(1)} %get-tuple-element.45), channel_id=1, source_target_pairs={{0,64},{32,96},{64,0},{96,32},{1,65},{33,97},{65,1},{97,33},{2,66}... | collective-permute-start | bytes 196616 | tf_op jit(solution)/shard_map/ppermute | solution.py:295
  41.5 0.0 collective-permute-done.2.same
  41.5 1.5 %collective-permute-start.7 = (f32[4,32,128]{2,1,0:T(8,128)S(1)}, f32[4,32,128]{2,1,0:T(8,128)S(1)}, u32[]{:S(2)}, u32[]{:S(2)}) collective-permute-start(f32[4,32,128]{2,1,0:T(8,128)S(1)} %get-tuple-element.46), channel_id=1, source_target_pairs={{0,96},{32,0},{64,32},{96,64},{1,97},{33,1},{65,33},{97,65},{2,98}... | collective-permute-start | bytes 196616 | tf_op jit(solution)/shard_map/ppermute | solution.py:295
  42.9 0.0 collective-permute-done.3.cross
  42.9 0.0 collective-permute-done.1.other
  42.9 0.8 shard_map.78
  43.8 0.1 convert_reduce_fusion.steps
  43.9 0.0 collective-permute-done.5.b
  43.9 0.7 collective-permute-done.6.c
  44.6 1.2 %collective-permute-done.7.d = f32[4,32,128]{2,1,0:T(8,128)S(1)} collective-permute-done((f32[4,32,128]{2,1,0:T(8,128)S(1)}, f32[4,32,128]{2,1,0:T(8,128)S(1)}, u32[]{:S(2)}, u32[]{:S(2)}) %collective-permute-start.7) | collective-permute-done | bytes 65568 | tf_op jit(solution)/shard_map/ppermute | solution.py:295
  45.7 0.0 all-to-all-done.parts
  45.7 2.7 %shard_map.80 = (f32[20,64,128]{2,1,0:T(8,128)S(1)}, f32[64,128]{1,0:T(8,128)S(1)}, f32[64,128]{1,0:T(8,128)S(1)}, f32[64,128]{1,0:T(8,128)S(1)}) custom-call(s32[4]{0:T(128)S(1)} %copy-done.5, s32[2,48]{1,0:T(2,128)S(1)} %convert_reduce_fusion.steps, f32[4,32,16,128]{3,2,1,0:T(8,128)S(1)} %all-to-all-done.parts, f32[4,32,128]{2,1,0:T(8,128)S(1)} %get-tuple-element.49.a, ...), custom_call_target="tpu_custom_call" | custom-call | flops 4194304 | bytes 2097152 | tf_op jit(solution)/shard_map/pallas_call | solution.py:333
  48.4 0.8 copy-done.1
  49.3 0.6 copy-done.4
  49.9 0.0 collective-permute-start.8
  49.9 3.0 %shard_map.81 = f32[8,16,32,128]{3,2,1,0:T(8,128)} custom-call(f32[20,64,128]{2,1,0:T(8,128)} %copy-done.1, f32[64,128]{1,0:T(8,128)} %copy-done.4), custom_call_target="tpu_custom_call" | custom-call | flops 4194304 | bytes 2097152 | tf_op jit(solution)/shard_map/pallas_call | solution.py:344
  52.9 1.3 %collective-permute-done.8.other = f32[64,128]{1,0:T(8,128)S(1)} collective-permute-done((f32[64,128]{1,0:T(8,128)S(1)}, f32[64,128]{1,0:T(8,128)S(1)}, u32[]{:S(2)}, u32[]{:S(2)}) %collective-permute-start.8) | collective-permute-done | bytes 32800 | tf_op jit(solution)/shard_map/ppermute | solution.py:269
  54.2 4.1 %all-to-all-start.1 = ((f32[8,16,32,128]{3,2,1,0:T(8,128)}), f32[8,16,32,128]{3,2,1,0:T(8,128)S(1)}, u32[]{:S(2)}, u32[]{:S(2)}) async-start(f32[8,16,32,128]{3,2,1,0:T(8,128)} %shard_map.81), calls=%async_computation.1 | async-start | bytes 4194304 | tf_op jit(solution)/shard_map/all_to_all | solution.py:354
  58.3 0.5 shard_map.83
  58.8 0.1 collective-permute-start.10
  58.9 3.0 %collective-permute-start.9 = (f32[24,128]{1,0:T(8,128)S(1)}, f32[24,128]{1,0:T(8,128)S(1)}, u32[]{:S(2)}, u32[]{:S(2)}) collective-permute-start(f32[24,128]{1,0:T(8,128)S(1)} %get-tuple-element.62), channel_id=1, source_target_pairs={{1,2},{2,1},{3,4},{4,3},{5,6},{6,5},{7,8},{8,7},{9,10},{10,9},{11,... | collective-permute-start | bytes 36872 | tf_op jit(solution)/shard_map/ppermute | solution.py:361
  61.9 0.0 collective-permute-done.10.side_e
  61.9 12.9 %collective-permute-done.9.side_o = f32[24,128]{1,0:T(8,128)S(1)} collective-permute-done((f32[24,128]{1,0:T(8,128)S(1)}, f32[24,128]{1,0:T(8,128)S(1)}, u32[]{:S(2)}, u32[]{:S(2)}) %collective-permute-start.9) | collective-permute-done | bytes 12320 | tf_op jit(solution)/shard_map/ppermute | solution.py:361
  74.8 0.5 shard_map.84.refs_1_
  75.4 2.2 %collective-permute-start.11 = (f32[48,128]{1,0:T(8,128)S(1)}, f32[48,128]{1,0:T(8,128)S(1)}, u32[]{:S(2)}, u32[]{:S(2)}) collective-permute-start(f32[48,128]{1,0:T(8,128)S(1)} %shard_map.84.refs_1_), channel_id=1, source_target_pairs={{0,32},{32,64},{64,96},{96,0},{1,33},{33,65},{65,97},{97,1},{2,34}... | collective-permute-start | bytes 73736 | tf_op jit(solution)/shard_map/ppermute | solution.py:295
  77.6 3.0 %collective-permute-start.12 = (f32[48,128]{1,0:T(8,128)S(1)}, f32[48,128]{1,0:T(8,128)S(1)}, u32[]{:S(2)}, u32[]{:S(2)}) collective-permute-start(f32[48,128]{1,0:T(8,128)S(1)} %shard_map.84.refs_1_), channel_id=1, source_target_pairs={{0,64},{32,96},{64,0},{96,32},{1,65},{33,97},{65,1},{97,33},{2,66}... | collective-permute-start | bytes 73736 | tf_op jit(solution)/shard_map/ppermute | solution.py:295
  80.5 1.1 %collective-permute-start.13 = (f32[48,128]{1,0:T(8,128)S(1)}, f32[48,128]{1,0:T(8,128)S(1)}, u32[]{:S(2)}, u32[]{:S(2)}) collective-permute-start(f32[48,128]{1,0:T(8,128)S(1)} %shard_map.84.refs_1_), channel_id=1, source_target_pairs={{0,96},{32,0},{64,32},{96,64},{1,97},{33,1},{65,33},{97,65},{2,98}... | collective-permute-start | bytes 73736 | tf_op jit(solution)/shard_map/ppermute | solution.py:295
  81.7 0.0 collective-permute-done.11.refs_2_
  81.7 1.2 %collective-permute-done.12.refs_3_ = f32[48,128]{1,0:T(8,128)S(1)} collective-permute-done((f32[48,128]{1,0:T(8,128)S(1)}, f32[48,128]{1,0:T(8,128)S(1)}, u32[]{:S(2)}, u32[]{:S(2)}) %collective-permute-start.12) | collective-permute-done | bytes 24608 | tf_op jit(solution)/shard_map/ppermute | solution.py:295
  82.9 1.5 %collective-permute-done.13.refs_4_ = f32[48,128]{1,0:T(8,128)S(1)} collective-permute-done((f32[48,128]{1,0:T(8,128)S(1)}, f32[48,128]{1,0:T(8,128)S(1)}, u32[]{:S(2)}, u32[]{:S(2)}) %collective-permute-start.13) | collective-permute-done | bytes 24608 | tf_op jit(solution)/shard_map/ppermute | solution.py:295
  84.4 1.6 %shard_map.85 = f32[1,32,512]{2,1,0:T(8,128)} custom-call(s32[4]{0:T(128)S(1)} %copy-done.5, f32[48,128]{1,0:T(8,128)S(1)} %shard_map.84.refs_1_, f32[48,128]{1,0:T(8,128)S(1)} %collective-permute-done.11.refs_2_, f32[48,128]{1,0:T(8,128)S(1)} %collective-permute-done.12.refs_3_, f32[48,128]{1,0:T(8,128)S(1)} %collective-permute-done.13.refs_4_), custom_call_target="tpu_custom_call" | custom-call | flops 4194304 | bytes 2097152 | tf_op jit(solution)/shard_map/pallas_call | solution.py:368
  86.0 0.0 all-to-all-done.1.parts
  86.0 1.4 %shard_map.82 = f32[32,32,512]{2,1,0:T(8,128)} custom-call(f32[8,16,32,128]{3,2,1,0:T(8,128)S(1)} %all-to-all-done.1.parts), custom_call_target="tpu_custom_call" | custom-call | flops 4194304 | bytes 2097152 | tf_op jit(solution)/shard_map/pallas_call | solution.py:374
  (9 shorter events, 0.0 us)
Async XLA Ops:
  0.6 5.6 %collective-permute-start = (s32[1,32]{1,0:T(1,128)}, s32[1,32]{1,0:T(1,128)S(1)}, u32[]{:S(2)}, u32[]{:S(2)}) collective-permute-start(s32[1,32]{1,0:T(1,128)} %index.1), channel_id=1, source_target_pairs={{0,128},{1,129},{2,130},{3,131},{4,132},{5,133},{6,134},{7,135},{8... | collective-permute-start | bytes 392 | tf_op jit(solution)/shard_map/ppermute | solution.py:269
  2.4 33.3 %copy-start.3 = (f32[680,32]{0,1:T(8,128)S(1)}, f32[680,32]{0,1:T(8,128)}, u32[]{:S(2)}) copy-start(f32[680,32]{0,1:T(8,128)} %param.10) | copy-start | bytes 261124
  6.2 29.4 %copy-start = (f32[32,32,512]{2,1,0:T(8,128)S(1)}, f32[32,32,512]{2,1,0:T(8,128)}, u32[]{:S(2)}) copy-start(f32[32,32,512]{2,1,0:T(8,128)} %volume.3) | copy-start | bytes 6291460
  6.2 29.4 %copy-start.5 = (s32[4]{0:T(128)S(1)}, s32[4]{0:T(128)}, u32[]{:S(2)}) copy-start(s32[4]{0:T(128)} %pad_add_fusion.place.refs_0_) | copy-start | bytes 52
  6.2 29.4 %copy-start.6 = (s32[1,32]{1,0:T(1,128)S(1)}, s32[1,32]{1,0:T(1,128)}, u32[]{:S(2)}) copy-start(s32[1,32]{1,0:T(1,128)} %index.1) | copy-start | bytes 388
  6.3 39.5 %all-to-all-start = ((f32[4,32,16,128]{3,2,1,0:T(8,128)}), f32[4,32,16,128]{3,2,1,0:T(8,128)S(1)}, u32[]{:S(2)}, u32[]{:S(2)}) async-start(f32[4,32,16,128]{3,2,1,0:T(8,128)} %get-tuple-element.34), calls=%async_computation | async-start | bytes 2097152 | tf_op jit(solution)/shard_map/all_to_all | solution.py:311
  10.9 32.1 %copy-start.2 = (f32[34,32,128]{2,1,0:T(8,128)S(1)}, f32[34,32,128]{2,1,0:T(8,128)}, u32[]{:S(2)}) copy-start(f32[34,32,128]{2,1,0:T(8,128)} %get-tuple-element.35.own) | copy-start | bytes 1671172
  10.9 32.1 %collective-permute-start.1 = (f32[34,32,128]{2,1,0:T(8,128)}, f32[34,32,128]{2,1,0:T(8,128)S(1)}, u32[]{:S(2)}, u32[]{:S(2)}) collective-permute-start(f32[34,32,128]{2,1,0:T(8,128)} %get-tuple-element.35.own), channel_id=1, source_target_pairs={{0,128},{1,129},{2,130},{3,131},{4,132},{5,133},{6,134},{7,135},{8... | collective-permute-start | bytes 1671176 | tf_op jit(solution)/shard_map/ppermute | solution.py:269
  11.9 29.6 %collective-permute-start.2 = (f32[34,16,128]{2,1,0:T(8,128)}, f32[34,16,128]{2,1,0:T(8,128)S(1)}, u32[]{:S(2)}, u32[]{:S(2)}) collective-permute-start(f32[34,16,128]{2,1,0:T(8,128)} %get-tuple-element.36), channel_id=1, source_target_pairs={{0,1},{1,2},{2,3},{3,4},{4,5},{5,6},{6,7},{7,8},{8,9},{9,10},{10,1... | collective-permute-start | bytes 835592 | tf_op jit(solution)/shard_map/ppermute | solution.py:269
  13.8 29.1 %collective-permute-start.3 = (f32[34,16,128]{2,1,0:T(8,128)}, f32[34,16,128]{2,1,0:T(8,128)S(1)}, u32[]{:S(2)}, u32[]{:S(2)}) collective-permute-start(f32[34,16,128]{2,1,0:T(8,128)} %get-tuple-element.37), channel_id=1, source_target_pairs={{1,128},{2,129},{3,130},{4,131},{5,132},{6,133},{7,134},{8,135},{9... | collective-permute-start | bytes 835592 | tf_op jit(solution)/shard_map/ppermute | solution.py:269
  18.1 17.5 %collective-permute-start.4 = (f32[32,512]{1,0:T(8,128)}, f32[32,512]{1,0:T(8,128)S(1)}, u32[]{:S(2)}, u32[]{:S(2)}) collective-permute-start(f32[32,512]{1,0:T(8,128)} %get-tuple-element.42), channel_id=1, source_target_pairs={{0,1},{1,2},{2,3},{3,4},{4,5},{5,6},{6,7},{7,8},{8,9},{9,10},{10,1... | collective-permute-start | bytes 196616 | tf_op jit(solution)/shard_map/ppermute | solution.py:269
  37.0 6.9 %collective-permute-start.5 = (f32[4,32,128]{2,1,0:T(8,128)S(1)}, f32[4,32,128]{2,1,0:T(8,128)S(1)}, u32[]{:S(2)}, u32[]{:S(2)}) collective-permute-start(f32[4,32,128]{2,1,0:T(8,128)S(1)} %get-tuple-element.44), channel_id=1, source_target_pairs={{0,32},{32,64},{64,96},{96,0},{1,33},{33,65},{65,97},{97,1},{2,34}... | collective-permute-start | bytes 196616 | tf_op jit(solution)/shard_map/ppermute | solution.py:295
  38.8 5.8 %collective-permute-start.6 = (f32[4,32,128]{2,1,0:T(8,128)S(1)}, f32[4,32,128]{2,1,0:T(8,128)S(1)}, u32[]{:S(2)}, u32[]{:S(2)}) collective-permute-start(f32[4,32,128]{2,1,0:T(8,128)S(1)} %get-tuple-element.45), channel_id=1, source_target_pairs={{0,64},{32,96},{64,0},{96,32},{1,65},{33,97},{65,1},{97,33},{2,66}... | collective-permute-start | bytes 196616 | tf_op jit(solution)/shard_map/ppermute | solution.py:295
  41.5 4.3 %collective-permute-start.7 = (f32[4,32,128]{2,1,0:T(8,128)S(1)}, f32[4,32,128]{2,1,0:T(8,128)S(1)}, u32[]{:S(2)}, u32[]{:S(2)}) collective-permute-start(f32[4,32,128]{2,1,0:T(8,128)S(1)} %get-tuple-element.46), channel_id=1, source_target_pairs={{0,96},{32,0},{64,32},{96,64},{1,97},{33,1},{65,33},{97,65},{2,98}... | collective-permute-start | bytes 196616 | tf_op jit(solution)/shard_map/ppermute | solution.py:295
  48.4 0.8 copy-start.1
  49.3 0.6 copy-start.4
  49.9 4.3 %collective-permute-start.8 = (f32[64,128]{1,0:T(8,128)S(1)}, f32[64,128]{1,0:T(8,128)S(1)}, u32[]{:S(2)}, u32[]{:S(2)}) collective-permute-start(f32[64,128]{1,0:T(8,128)S(1)} %get-tuple-element.57), channel_id=1, source_target_pairs={{0,128},{1,129},{2,130},{3,131},{4,132},{5,133},{6,134},{7,135},{8... | collective-permute-start | bytes 98312 | tf_op jit(solution)/shard_map/ppermute | solution.py:269
  54.2 31.8 %all-to-all-start.1 = ((f32[8,16,32,128]{3,2,1,0:T(8,128)}), f32[8,16,32,128]{3,2,1,0:T(8,128)S(1)}, u32[]{:S(2)}, u32[]{:S(2)}) async-start(f32[8,16,32,128]{3,2,1,0:T(8,128)} %shard_map.81), calls=%async_computation.1 | async-start | bytes 4194304 | tf_op jit(solution)/shard_map/all_to_all | solution.py:354
  58.8 3.1 %collective-permute-start.10 = (f32[24,128]{1,0:T(8,128)S(1)}, f32[24,128]{1,0:T(8,128)S(1)}, u32[]{:S(2)}, u32[]{:S(2)}) collective-permute-start(f32[24,128]{1,0:T(8,128)S(1)} %get-tuple-element.63), channel_id=1, source_target_pairs={{0,1},{1,0},{2,3},{3,2},{4,5},{5,4},{6,7},{7,6},{8,9},{9,8},{10,11... | collective-permute-start | bytes 36872 | tf_op jit(solution)/shard_map/ppermute | solution.py:361
  58.9 15.9 %collective-permute-start.9 = (f32[24,128]{1,0:T(8,128)S(1)}, f32[24,128]{1,0:T(8,128)S(1)}, u32[]{:S(2)}, u32[]{:S(2)}) collective-permute-start(f32[24,128]{1,0:T(8,128)S(1)} %get-tuple-element.62), channel_id=1, source_target_pairs={{1,2},{2,1},{3,4},{4,3},{5,6},{6,5},{7,8},{8,7},{9,10},{10,9},{11,... | collective-permute-start | bytes 36872 | tf_op jit(solution)/shard_map/ppermute | solution.py:361
  75.4 6.3 %collective-permute-start.11 = (f32[48,128]{1,0:T(8,128)S(1)}, f32[48,128]{1,0:T(8,128)S(1)}, u32[]{:S(2)}, u32[]{:S(2)}) collective-permute-start(f32[48,128]{1,0:T(8,128)S(1)} %shard_map.84.refs_1_), channel_id=1, source_target_pairs={{0,32},{32,64},{64,96},{96,0},{1,33},{33,65},{65,97},{97,1},{2,34}... | collective-permute-start | bytes 73736 | tf_op jit(solution)/shard_map/ppermute | solution.py:295
  77.6 5.3 %collective-permute-start.12 = (f32[48,128]{1,0:T(8,128)S(1)}, f32[48,128]{1,0:T(8,128)S(1)}, u32[]{:S(2)}, u32[]{:S(2)}) collective-permute-start(f32[48,128]{1,0:T(8,128)S(1)} %shard_map.84.refs_1_), channel_id=1, source_target_pairs={{0,64},{32,96},{64,0},{96,32},{1,65},{33,97},{65,1},{97,33},{2,66}... | collective-permute-start | bytes 73736 | tf_op jit(solution)/shard_map/ppermute | solution.py:295
  80.5 3.8 %collective-permute-start.13 = (f32[48,128]{1,0:T(8,128)S(1)}, f32[48,128]{1,0:T(8,128)S(1)}, u32[]{:S(2)}, u32[]{:S(2)}) collective-permute-start(f32[48,128]{1,0:T(8,128)S(1)} %shard_map.84.refs_1_), channel_id=1, source_target_pairs={{0,96},{32,0},{64,32},{96,64},{1,97},{33,1},{65,33},{97,65},{2,98}... | collective-permute-start | bytes 73736 | tf_op jit(solution)/shard_map/ppermute | solution.py:295

commit v7 on v6

--- a/solution.py
+++ b/solution.py
@@ -40,7 +40,7 @@
 
 
 def load(
-    place, shift, measured, frac, volume, whole, same, cross, rim, parts, block, half, sems, done
+    place, shift, measured, frac, volume, whole, same, cross, parts, block, half, sems, done
 ):
     angles, cols = measured.shape[1:3]
     phase = place[1]
@@ -68,14 +68,17 @@
         sent[k].start()
     for copy in copies[slabs:]:
         copy.wait()
-    rim[...] = jnp.where(phase == 0, block[:, 7, :], block[:, 0, :])
-    same[...] = whole[:, pl.ds(pl.multiple_of(HALO * (1 - phase), HALO), HALO), :]
+    same[0 : angles + 2] = whole[:, pl.ds(pl.multiple_of(HALO * (1 - phase), HALO), HALO), :]
+    rim = jnp.where(phase == 0, block[:, 7, :], block[:, 0, :])
+    for k in range(same.shape[0] - angles - 2):
+        lanes = slice(k // 2 * LANES, (k // 2 + 1) * LANES)
+        same[angles + 2 + k] = rim[k % 2 * HALO : (k % 2 + 1) * HALO, lanes]
     cross[...] = whole[:, columns, :]
     for copy in sent:
         copy.wait()
 
 
-def pack(place, index, other, rim, table, volume, first, second, third, fourth, block, low, high, sem):
+def pack(place, index, other, same, table, volume, first, second, third, fourth, block, low, high, sem):
     depth, cols, _ = volume.shape
     angles = index.shape[1]
     start = pl.multiple_of(HALO - 8 * place[1], 8)
@@ -89,12 +92,15 @@
     lane = lax.broadcasted_iota(jnp.int32, (depth, LANES), 1)
     weights = outer(flipped, (lane == row + place[0] * depth).astype(F32))
     left = place[1] == 0
-    beside = rim[...]
     copy.wait()
     inner = jnp.where(left, block[:, 0, :], block[:, 7, :])
-    low[...] = jnp.where(left, beside, inner)
-    high[...] = jnp.where(left, inner, beside)
     slabs = volume.shape[2] // LANES
+    for k in range(slabs):
+        lanes = slice(k * LANES, (k + 1) * LANES)
+        row = angles + 2 + 2 * k
+        beside = jnp.concatenate([same[row], same[row + 1]], axis=0)
+        low[:, lanes] = jnp.where(left, beside, inner[:, lanes])
+        high[:, lanes] = jnp.where(left, inner[:, lanes], beside)
     for k, out in enumerate((first, second, third, fourth)):
         to = place[0] + k
         to = jnp.where(to >= slabs, to - slabs, to)
@@ -294,17 +300,17 @@
     def around(block, distance):
         return lax.ppermute(block, "slab", [(i, (i + distance) % slabs) for i in range(slabs)])
 
-    bundles = [(angles + 2, cols, LANES)] + [(angles + 2, HALO, LANES)] * 2
+    rim = depth * height // (HALO * LANES)
+    bundles = [(angles + 2 + more, size, LANES) for more, size in ((0, cols), (rim, HALO), (0, HALO))]
     message = (slabs, depth, HALO, LANES)
-    bundle_own, same, cross, rim, parts = call(
+    bundle_own, same, cross, parts = call(
         load,
-        bundles + [(depth, height), message],
+        bundles + [message],
         [SMEM] * 2 + [ANY] * 3,
         [octet, pltpu.VMEM(message, F32), dma((slabs + 3,)), dma((slabs,))],
-        [VMEM] * 4 + [ANY],
+        [VMEM] * 3 + [ANY],
         limit=ROOM,
     )(place, shift, measured, frac, volume)
-    rim = move(rim, toward)
     index_other = move(angle_index, partner)
     bundle_other = move(bundle_own, partner)
     parts, index_other = lax.optimization_barrier((parts, index_other))
@@ -317,7 +323,7 @@
         [(4, depth, LANES)] * slabs,
         [SMEM] + [VMEM] * 4 + [ANY],
         [octet, wide, wide, dma((1,))],
-    )(place, angle_index, index_other, rim, depth_weights.T, volume)
+    )(place, angle_index, index_other, same, depth_weights.T, volume)
     extras = [extras[0]] + [around(extras[k], k) for k in range(1, slabs)]
     seen, share, steps = call(
         arrange,
@@ -347,7 +353,7 @@
         [VMEM] * 2,
         [pltpu.VMEM((slabs, HALO, depth, LANES), F32), dma((HALO // 2,))],
         [ANY],
-        limit=ROOM,
+        limit=50,
     )(grad, weights)
     other = move(other, partner)
     parts, other = lax.optimization_barrier((parts, other))
@@ -365,15 +371,16 @@
     def ending(*refs):
         diffuse(tiles - 1, *refs)
 
+    (image,) = call(
+        finish, [(depth, cols, height)], [VMEM], [blocks, dma((cols // 8,))], [ANY]
+    )(parts)
+    image, *fields = lax.optimization_barrier((image, *fields))
     (field,) = call(
         ending,
         [(1, cols, height)],
         [SMEM] + [VMEM] * 4,
         [pltpu.VMEM((slabs,) + window, F32)],
     )(place, *fields)
-    (image,) = call(
-        finish, [(depth, cols, height)], [VMEM], [blocks, dma((cols // 8,))], [ANY]
-    )(parts)
     return image, field
 
 

time: 88.9 us -> 86.8 us (0.976)
  the two profiles are of different devices: /device:TPU:128 before, /device:TPU:192 now
where the time goes in v7:
time: 86.8 us; the launch traced here: 86.5 us
  waiting for transfers between devices  38.3 us (44%)
  starting transfers between devices  31.8 us (37%)
  Pallas kernels  14.8 us (17%)
    ppermute x1, waiting for transfers between devices, body(): lax.ppermute(side_o, 'tile', pairs_o)  18.9 us
    ppermute x5, waiting for transfers between devices, move(): return lax.ppermute(block, ('phase', 'tile'), route)  16.5 us
    ppermute x6, starting transfers between devices, around(): lax.ppermute(block, 'slab', [(i, (i + distance) % slabs) for i in range(s...  11.9 us
    ppermute x5, starting transfers between devices, move(): return lax.ppermute(block, ('phase', 'tile'), route)  9.33 us
    all_to_all x1, starting transfers between devices, body(): parts = lax.all_to_all(parts, 'slab', 0, 0, tiled=True)  4.61 us
    all_to_all x1, starting transfers between devices, body(): parts = lax.all_to_all(parts, ('phase', 'slab'), 0, 0, tiled=True)  3.94 us
    pallas_call x1, Pallas kernels, body(): call(load, bundles + [message], [SMEM] * 2 + [ANY] * 3, [octet, pltpu.VME...  3.86 us
    ppermute x6, waiting for transfers between devices, around(): lax.ppermute(block, 'slab', [(i, (i + distance) % slabs) for i in range(s...  2.99 us
  transfers between devices with their start and end apart: 15, of which 6 were waited for; matrix products, arithmetic and copies ran while one was open for 1% of the time, Pallas kernels for 12%

profile of v7, /device:TPU:192, one launch (start us, length us, event | category | flops | bytes accessed | tf_op | source)
XLA Modules:
  0.0 86.5 jit_solution(15072529560676421397)
XLA Ops:
  0.6 1.1 %collective-permute-start = (s32[1,32]{1,0:T(1,128)}, s32[1,32]{1,0:T(1,128)S(1)}, u32[]{:S(2)}, u32[]{:S(2)}) collective-permute-start(s32[1,32]{1,0:T(1,128)} %index.1), channel_id=1, source_target_pairs={{0,128},{1,129},{2,130},{3,131},{4,132},{5,133},{6,134},{7,135},{8... | collective-permute-start | bytes 392 | tf_op jit(solution)/shard_map/ppermute | solution.py:275
  1.7 0.7 pad_add_fusion.place.refs_0_
  2.4 3.9 %shard_map.77 = (f32[34,32,128]{2,1,0:T(8,128)}, f32[42,16,128]{2,1,0:T(8,128)}, f32[34,16,128]{2,1,0:T(8,128)}, f32[4,32,16,128]{3,2,1,0:T(8,128)}) custom-call(s32[4]{0:T(128)} %pad_add_fusion.place.refs_0_, s32[1,32]{1,0:T(1,128)} %shift.1, f32[1,32,32,512]{3,2,1,0:T(8,128)} %measured.1, f32[1,32,512]{2,1,0:T(8,128)} %frac.1, f32[32,32,512]{2,1,0:T(8,128)} %volume.3), custom_call_target="tpu_custom_call" | custom-call | flops 4194304 | bytes 2097152 | tf_op jit(solution)/shard_map/pallas_call | solution.py:306
  6.3 0.0 copy-start
  6.3 0.0 copy-start.3
  6.3 0.0 copy-start.4
  6.3 0.0 collective-permute-done.other
  6.3 4.6 %all-to-all-start = ((f32[4,32,16,128]{3,2,1,0:T(8,128)}), f32[4,32,16,128]{3,2,1,0:T(8,128)S(1)}, u32[]{:S(2)}, u32[]{:S(2)}) async-start(f32[4,32,16,128]{3,2,1,0:T(8,128)} %get-tuple-element.38), calls=%async_computation | async-start | bytes 2097152 | tf_op jit(solution)/shard_map/all_to_all | solution.py:317
  10.9 1.0 %collective-permute-start.1 = (f32[34,32,128]{2,1,0:T(8,128)}, f32[34,32,128]{2,1,0:T(8,128)S(1)}, u32[]{:S(2)}, u32[]{:S(2)}) collective-permute-start(f32[34,32,128]{2,1,0:T(8,128)} %get-tuple-element.39.own), channel_id=1, source_target_pairs={{0,128},{1,129},{2,130},{3,131},{4,132},{5,133},{6,134},{7,135},{8... | collective-permute-start | bytes 1671176 | tf_op jit(solution)/shard_map/ppermute | solution.py:275
  11.9 1.9 %collective-permute-start.2 = (f32[42,16,128]{2,1,0:T(8,128)}, f32[42,16,128]{2,1,0:T(8,128)S(1)}, u32[]{:S(2)}, u32[]{:S(2)}) collective-permute-start(f32[42,16,128]{2,1,0:T(8,128)} %get-tuple-element.40), channel_id=1, source_target_pairs={{0,1},{1,2},{2,3},{3,4},{4,5},{5,6},{6,7},{7,8},{8,9},{9,10},{10,1... | collective-permute-start | bytes 1032200 | tf_op jit(solution)/shard_map/ppermute | solution.py:275
  13.8 5.2 %collective-permute-start.3 = (f32[34,16,128]{2,1,0:T(8,128)}, f32[34,16,128]{2,1,0:T(8,128)S(1)}, u32[]{:S(2)}, u32[]{:S(2)}) collective-permute-start(f32[34,16,128]{2,1,0:T(8,128)} %get-tuple-element.41), channel_id=1, source_target_pairs={{1,128},{2,129},{3,130},{4,131},{5,132},{6,133},{7,134},{8,135},{9... | collective-permute-start | bytes 835592 | tf_op jit(solution)/shard_map/ppermute | solution.py:275
  19.1 14.1 %collective-permute-done.2.same = f32[42,16,128]{2,1,0:T(8,128)S(1)} collective-permute-done((f32[42,16,128]{2,1,0:T(8,128)}, f32[42,16,128]{2,1,0:T(8,128)S(1)}, u32[]{:S(2)}, u32[]{:S(2)}) %collective-permute-start.2) | collective-permute-done | bytes 344096 | tf_op jit(solution)/shard_map/ppermute | solution.py:275
  33.2 0.0 copy-done.2
  33.2 0.0 copy-done
  33.2 0.0 copy-done.3
  33.2 0.0 copy-done.4
  33.2 1.3 %shard_map.79 = (f32[4,32,128]{2,1,0:T(8,128)S(1)}, f32[4,32,128]{2,1,0:T(8,128)S(1)}, f32[4,32,128]{2,1,0:T(8,128)S(1)}, f32[4,32,128]{2,1,0:T(8,128)S(1)}) custom-call(s32[4]{0:T(128)S(1)} %copy-done.3, s32[1,32]{1,0:T(1,128)S(1)} %copy-done.4, s32[1,32]{1,0:T(1,128)S(1)} %collective-permute-done.other, f32[42,16,128]{2,1,0:T(8,128)S(1)} %collective-permute-done.2.same, ...), custom_call_target="tpu_custom_call" | custom-call | flops 4194304 | bytes 2097152 | tf_op jit(solution)/shard_map/pallas_call | solution.py:321
  34.5 1.5 %collective-permute-start.4 = (f32[4,32,128]{2,1,0:T(8,128)S(1)}, f32[4,32,128]{2,1,0:T(8,128)S(1)}, u32[]{:S(2)}, u32[]{:S(2)}) collective-permute-start(f32[4,32,128]{2,1,0:T(8,128)S(1)} %get-tuple-element.47), channel_id=1, source_target_pairs={{0,32},{32,64},{64,96},{96,0},{1,33},{33,65},{65,97},{97,1},{2,34}... | collective-permute-start | bytes 196616 | tf_op jit(solution)/shard_map/ppermute | solution.py:301
  36.0 2.7 %collective-permute-start.5 = (f32[4,32,128]{2,1,0:T(8,128)S(1)}, f32[4,32,128]{2,1,0:T(8,128)S(1)}, u32[]{:S(2)}, u32[]{:S(2)}) collective-permute-start(f32[4,32,128]{2,1,0:T(8,128)S(1)} %get-tuple-element.48), channel_id=1, source_target_pairs={{0,64},{32,96},{64,0},{96,32},{1,65},{33,97},{65,1},{97,33},{2,66}... | collective-permute-start | bytes 196616 | tf_op jit(solution)/shard_map/ppermute | solution.py:301
  38.7 1.5 %collective-permute-start.6 = (f32[4,32,128]{2,1,0:T(8,128)S(1)}, f32[4,32,128]{2,1,0:T(8,128)S(1)}, u32[]{:S(2)}, u32[]{:S(2)}) collective-permute-start(f32[4,32,128]{2,1,0:T(8,128)S(1)} %get-tuple-element.49), channel_id=1, source_target_pairs={{0,96},{32,0},{64,32},{96,64},{1,97},{33,1},{65,33},{97,65},{2,98}... | collective-permute-start | bytes 196616 | tf_op jit(solution)/shard_map/ppermute | solution.py:301
  40.2 0.0 collective-permute-done.3.cross
  40.2 0.0 collective-permute-done.1.other
  40.2 0.8 shard_map.78
  41.0 0.1 convert_reduce_fusion.steps
  41.1 0.0 collective-permute-done.4.b
  41.1 0.7 collective-permute-done.5.c
  41.8 1.2 %collective-permute-done.6.d = f32[4,32,128]{2,1,0:T(8,128)S(1)} collective-permute-done((f32[4,32,128]{2,1,0:T(8,128)S(1)}, f32[4,32,128]{2,1,0:T(8,128)S(1)}, u32[]{:S(2)}, u32[]{:S(2)}) %collective-permute-start.6) | collective-permute-done | bytes 65568 | tf_op jit(solution)/shard_map/ppermute | solution.py:301
  43.0 0.0 all-to-all-done.parts
  43.0 2.7 %shard_map.80 = (f32[20,64,128]{2,1,0:T(8,128)S(1)}, f32[64,128]{1,0:T(8,128)S(1)}, f32[64,128]{1,0:T(8,128)S(1)}, f32[64,128]{1,0:T(8,128)S(1)}) custom-call(s32[4]{0:T(128)S(1)} %copy-done.3, s32[2,48]{1,0:T(2,128)S(1)} %convert_reduce_fusion.steps, f32[4,32,16,128]{3,2,1,0:T(8,128)S(1)} %all-to-all-done.parts, f32[4,32,128]{2,1,0:T(8,128)S(1)} %get-tuple-element.52.a, ...), custom_call_target="tpu_custom_call" | custom-call | flops 4194304 | bytes 2097152 | tf_op jit(solution)/shard_map/pallas_call | solution.py:339
  45.7 0.1 collective-permute-start.7
  45.8 1.9 %shard_map.81 = f32[8,16,32,128]{3,2,1,0:T(8,128)} custom-call(f32[20,64,128]{2,1,0:T(8,128)S(1)} %get-tuple-element.58.grad, f32[64,128]{1,0:T(8,128)S(1)} %get-tuple-element.59.weights), custom_call_target="tpu_custom_call" | custom-call | flops 4194304 | bytes 2097152 | tf_op jit(solution)/shard_map/pallas_call | solution.py:350
  47.7 2.4 %collective-permute-done.7.other = f32[64,128]{1,0:T(8,128)S(1)} collective-permute-done((f32[64,128]{1,0:T(8,128)S(1)}, f32[64,128]{1,0:T(8,128)S(1)}, u32[]{:S(2)}, u32[]{:S(2)}) %collective-permute-start.7) | collective-permute-done | bytes 32800 | tf_op jit(solution)/shard_map/ppermute | solution.py:275
  50.1 3.9 %all-to-all-start.1 = ((f32[8,16,32,128]{3,2,1,0:T(8,128)}), f32[8,16,32,128]{3,2,1,0:T(8,128)S(1)}, u32[]{:S(2)}, u32[]{:S(2)}) async-start(f32[8,16,32,128]{3,2,1,0:T(8,128)} %shard_map.81), calls=%async_computation.1 | async-start | bytes 4194304 | tf_op jit(solution)/shard_map/all_to_all | solution.py:360
  54.0 0.5 shard_map.83
  54.6 1.9 %collective-permute-start.8 = (f32[24,128]{1,0:T(8,128)S(1)}, f32[24,128]{1,0:T(8,128)S(1)}, u32[]{:S(2)}, u32[]{:S(2)}) collective-permute-start(f32[24,128]{1,0:T(8,128)S(1)} %get-tuple-element.65), channel_id=1, source_target_pairs={{1,2},{2,1},{3,4},{4,3},{5,6},{6,5},{7,8},{8,7},{9,10},{10,9},{11,... | collective-permute-start | bytes 36872 | tf_op jit(solution)/shard_map/ppermute | solution.py:367
  56.5 0.1 collective-permute-start.9
  56.6 18.9 %collective-permute-done.8.side_o = f32[24,128]{1,0:T(8,128)S(1)} collective-permute-done((f32[24,128]{1,0:T(8,128)S(1)}, f32[24,128]{1,0:T(8,128)S(1)}, u32[]{:S(2)}, u32[]{:S(2)}) %collective-permute-start.8) | collective-permute-done | bytes 12320 | tf_op jit(solution)/shard_map/ppermute | solution.py:367
  75.5 0.0 collective-permute-done.9.side_e
  75.5 0.6 shard_map.84.refs_1_
  76.0 2.1 %collective-permute-start.10 = (f32[48,128]{1,0:T(8,128)S(1)}, f32[48,128]{1,0:T(8,128)S(1)}, u32[]{:S(2)}, u32[]{:S(2)}) collective-permute-start(f32[48,128]{1,0:T(8,128)S(1)} %shard_map.84.refs_1_), channel_id=1, source_target_pairs={{0,32},{32,64},{64,96},{96,0},{1,33},{33,65},{65,97},{97,1},{2,34}... | collective-permute-start | bytes 73736 | tf_op jit(solution)/shard_map/ppermute | solution.py:301
  78.1 3.0 %collective-permute-start.11 = (f32[48,128]{1,0:T(8,128)S(1)}, f32[48,128]{1,0:T(8,128)S(1)}, u32[]{:S(2)}, u32[]{:S(2)}) collective-permute-start(f32[48,128]{1,0:T(8,128)S(1)} %shard_map.84.refs_1_), channel_id=1, source_target_pairs={{0,64},{32,96},{64,0},{96,32},{1,65},{33,97},{65,1},{97,33},{2,66}... | collective-permute-start | bytes 73736 | tf_op jit(solution)/shard_map/ppermute | solution.py:301
  81.1 1.2 %collective-permute-start.12 = (f32[48,128]{1,0:T(8,128)S(1)}, f32[48,128]{1,0:T(8,128)S(1)}, u32[]{:S(2)}, u32[]{:S(2)}) collective-permute-start(f32[48,128]{1,0:T(8,128)S(1)} %shard_map.84.refs_1_), channel_id=1, source_target_pairs={{0,96},{32,0},{64,32},{96,64},{1,97},{33,1},{65,33},{97,65},{2,98}... | collective-permute-start | bytes 73736 | tf_op jit(solution)/shard_map/ppermute | solution.py:301
  82.3 0.0 all-to-all-done.1.parts
  82.3 1.4 %shard_map.82 = f32[32,32,512]{2,1,0:T(8,128)} custom-call(f32[8,16,32,128]{3,2,1,0:T(8,128)S(1)} %all-to-all-done.1.parts), custom_call_target="tpu_custom_call" | custom-call | flops 4194304 | bytes 2097152 | tf_op jit(solution)/shard_map/pallas_call | solution.py:374
  83.7 0.0 collective-permute-done.10.refs_2_
  83.7 0.0 collective-permute-done.11.refs_3_
  83.8 1.1 %collective-permute-done.12.refs_4_ = f32[48,128]{1,0:T(8,128)S(1)} collective-permute-done((f32[48,128]{1,0:T(8,128)S(1)}, f32[48,128]{1,0:T(8,128)S(1)}, u32[]{:S(2)}, u32[]{:S(2)}) %collective-permute-start.12) | collective-permute-done | bytes 24608 | tf_op jit(solution)/shard_map/ppermute | solution.py:301
  84.9 1.6 %shard_map.85 = f32[1,32,512]{2,1,0:T(8,128)} custom-call(s32[4]{0:T(128)S(1)} %copy-done.3, f32[48,128]{1,0:T(8,128)S(1)} %shard_map.84.refs_1_, f32[48,128]{1,0:T(8,128)S(1)} %collective-permute-done.10.refs_2_, f32[48,128]{1,0:T(8,128)S(1)} %collective-permute-done.11.refs_3_, f32[48,128]{1,0:T(8,128)S(1)} %collective-permute-done.12.refs_4_), custom_call_target="tpu_custom_call" | custom-call | flops 4194304 | bytes 2097152 | tf_op jit(solution)/shard_map/pallas_call | solution.py:378
  (3 shorter events, 0.0 us)
Async XLA Ops:
  0.6 5.7 %collective-permute-start = (s32[1,32]{1,0:T(1,128)}, s32[1,32]{1,0:T(1,128)S(1)}, u32[]{:S(2)}, u32[]{:S(2)}) collective-permute-start(s32[1,32]{1,0:T(1,128)} %index.1), channel_id=1, source_target_pairs={{0,128},{1,129},{2,130},{3,131},{4,132},{5,133},{6,134},{7,135},{8... | collective-permute-start | bytes 392 | tf_op jit(solution)/shard_map/ppermute | solution.py:275
  2.4 30.8 %copy-start.2 = (f32[680,32]{0,1:T(8,128)S(1)}, f32[680,32]{0,1:T(8,128)}, u32[]{:S(2)}) copy-start(f32[680,32]{0,1:T(8,128)} %param.10) | copy-start | bytes 261124
  6.3 26.9 %copy-start = (f32[32,32,512]{2,1,0:T(8,128)S(1)}, f32[32,32,512]{2,1,0:T(8,128)}, u32[]{:S(2)}) copy-start(f32[32,32,512]{2,1,0:T(8,128)} %volume.3) | copy-start | bytes 6291460
  6.3 26.9 %copy-start.3 = (s32[4]{0:T(128)S(1)}, s32[4]{0:T(128)}, u32[]{:S(2)}) copy-start(s32[4]{0:T(128)} %pad_add_fusion.place.refs_0_) | copy-start | bytes 52
  6.3 26.9 %copy-start.4 = (s32[1,32]{1,0:T(1,128)S(1)}, s32[1,32]{1,0:T(1,128)}, u32[]{:S(2)}) copy-start(s32[1,32]{1,0:T(1,128)} %index.1) | copy-start | bytes 388
  6.3 36.7 %all-to-all-start = ((f32[4,32,16,128]{3,2,1,0:T(8,128)}), f32[4,32,16,128]{3,2,1,0:T(8,128)S(1)}, u32[]{:S(2)}, u32[]{:S(2)}) async-start(f32[4,32,16,128]{3,2,1,0:T(8,128)} %get-tuple-element.38), calls=%async_computation | async-start | bytes 2097152 | tf_op jit(solution)/shard_map/all_to_all | solution.py:317
  10.9 29.3 %copy-start.1 = (f32[34,32,128]{2,1,0:T(8,128)S(1)}, f32[34,32,128]{2,1,0:T(8,128)}, u32[]{:S(2)}) copy-start(f32[34,32,128]{2,1,0:T(8,128)} %get-tuple-element.39.own) | copy-start | bytes 1671172
  10.9 29.3 %collective-permute-start.1 = (f32[34,32,128]{2,1,0:T(8,128)}, f32[34,32,128]{2,1,0:T(8,128)S(1)}, u32[]{:S(2)}, u32[]{:S(2)}) collective-permute-start(f32[34,32,128]{2,1,0:T(8,128)} %get-tuple-element.39.own), channel_id=1, source_target_pairs={{0,128},{1,129},{2,130},{3,131},{4,132},{5,133},{6,134},{7,135},{8... | collective-permute-start | bytes 1671176 | tf_op jit(solution)/shard_map/ppermute | solution.py:275
  11.9 21.2 %collective-permute-start.2 = (f32[42,16,128]{2,1,0:T(8,128)}, f32[42,16,128]{2,1,0:T(8,128)S(1)}, u32[]{:S(2)}, u32[]{:S(2)}) collective-permute-start(f32[42,16,128]{2,1,0:T(8,128)} %get-tuple-element.40), channel_id=1, source_target_pairs={{0,1},{1,2},{2,3},{3,4},{4,5},{5,6},{6,7},{7,8},{8,9},{9,10},{10,1... | collective-permute-start | bytes 1032200 | tf_op jit(solution)/shard_map/ppermute | solution.py:275
  13.8 26.3 %collective-permute-start.3 = (f32[34,16,128]{2,1,0:T(8,128)}, f32[34,16,128]{2,1,0:T(8,128)S(1)}, u32[]{:S(2)}, u32[]{:S(2)}) collective-permute-start(f32[34,16,128]{2,1,0:T(8,128)} %get-tuple-element.41), channel_id=1, source_target_pairs={{1,128},{2,129},{3,130},{4,131},{5,132},{6,133},{7,134},{8,135},{9... | collective-permute-start | bytes 835592 | tf_op jit(solution)/shard_map/ppermute | solution.py:275
  34.5 6.6 %collective-permute-start.4 = (f32[4,32,128]{2,1,0:T(8,128)S(1)}, f32[4,32,128]{2,1,0:T(8,128)S(1)}, u32[]{:S(2)}, u32[]{:S(2)}) collective-permute-start(f32[4,32,128]{2,1,0:T(8,128)S(1)} %get-tuple-element.47), channel_id=1, source_target_pairs={{0,32},{32,64},{64,96},{96,0},{1,33},{33,65},{65,97},{97,1},{2,34}... | collective-permute-start | bytes 196616 | tf_op jit(solution)/shard_map/ppermute | solution.py:301
  36.0 5.8 %collective-permute-start.5 = (f32[4,32,128]{2,1,0:T(8,128)S(1)}, f32[4,32,128]{2,1,0:T(8,128)S(1)}, u32[]{:S(2)}, u32[]{:S(2)}) collective-permute-start(f32[4,32,128]{2,1,0:T(8,128)S(1)} %get-tuple-element.48), channel_id=1, source_target_pairs={{0,64},{32,96},{64,0},{96,32},{1,65},{33,97},{65,1},{97,33},{2,66}... | collective-permute-start | bytes 196616 | tf_op jit(solution)/shard_map/ppermute | solution.py:301
  38.7 4.3 %collective-permute-start.6 = (f32[4,32,128]{2,1,0:T(8,128)S(1)}, f32[4,32,128]{2,1,0:T(8,128)S(1)}, u32[]{:S(2)}, u32[]{:S(2)}) collective-permute-start(f32[4,32,128]{2,1,0:T(8,128)S(1)} %get-tuple-element.49), channel_id=1, source_target_pairs={{0,96},{32,0},{64,32},{96,64},{1,97},{33,1},{65,33},{97,65},{2,98}... | collective-permute-start | bytes 196616 | tf_op jit(solution)/shard_map/ppermute | solution.py:301
  45.7 4.4 %collective-permute-start.7 = (f32[64,128]{1,0:T(8,128)S(1)}, f32[64,128]{1,0:T(8,128)S(1)}, u32[]{:S(2)}, u32[]{:S(2)}) collective-permute-start(f32[64,128]{1,0:T(8,128)S(1)} %get-tuple-element.60), channel_id=1, source_target_pairs={{0,128},{1,129},{2,130},{3,131},{4,132},{5,133},{6,134},{7,135},{8... | collective-permute-start | bytes 98312 | tf_op jit(solution)/shard_map/ppermute | solution.py:275
  50.1 32.2 %all-to-all-start.1 = ((f32[8,16,32,128]{3,2,1,0:T(8,128)}), f32[8,16,32,128]{3,2,1,0:T(8,128)S(1)}, u32[]{:S(2)}, u32[]{:S(2)}) async-start(f32[8,16,32,128]{3,2,1,0:T(8,128)} %shard_map.81), calls=%async_computation.1 | async-start | bytes 4194304 | tf_op jit(solution)/shard_map/all_to_all | solution.py:360
  54.6 20.9 %collective-permute-start.8 = (f32[24,128]{1,0:T(8,128)S(1)}, f32[24,128]{1,0:T(8,128)S(1)}, u32[]{:S(2)}, u32[]{:S(2)}) collective-permute-start(f32[24,128]{1,0:T(8,128)S(1)} %get-tuple-element.65), channel_id=1, source_target_pairs={{1,2},{2,1},{3,4},{4,3},{5,6},{6,5},{7,8},{8,7},{9,10},{10,9},{11,... | collective-permute-start | bytes 36872 | tf_op jit(solution)/shard_map/ppermute | solution.py:367
  56.5 19.0 %collective-permute-start.9 = (f32[24,128]{1,0:T(8,128)S(1)}, f32[24,128]{1,0:T(8,128)S(1)}, u32[]{:S(2)}, u32[]{:S(2)}) collective-permute-start(f32[24,128]{1,0:T(8,128)S(1)} %get-tuple-element.66), channel_id=1, source_target_pairs={{0,1},{1,0},{2,3},{3,2},{4,5},{5,4},{6,7},{7,6},{8,9},{9,8},{10,11... | collective-permute-start | bytes 36872 | tf_op jit(solution)/shard_map/ppermute | solution.py:367
  76.0 7.7 %collective-permute-start.10 = (f32[48,128]{1,0:T(8,128)S(1)}, f32[48,128]{1,0:T(8,128)S(1)}, u32[]{:S(2)}, u32[]{:S(2)}) collective-permute-start(f32[48,128]{1,0:T(8,128)S(1)} %shard_map.84.refs_1_), channel_id=1, source_target_pairs={{0,32},{32,64},{64,96},{96,0},{1,33},{33,65},{65,97},{97,1},{2,34}... | collective-permute-start | bytes 73736 | tf_op jit(solution)/shard_map/ppermute | solution.py:301
  78.1 5.6 %collective-permute-start.11 = (f32[48,128]{1,0:T(8,128)S(1)}, f32[48,128]{1,0:T(8,128)S(1)}, u32[]{:S(2)}, u32[]{:S(2)}) collective-permute-start(f32[48,128]{1,0:T(8,128)S(1)} %shard_map.84.refs_1_), channel_id=1, source_target_pairs={{0,64},{32,96},{64,0},{96,32},{1,65},{33,97},{65,1},{97,33},{2,66}... | collective-permute-start | bytes 73736 | tf_op jit(solution)/shard_map/ppermute | solution.py:301
  81.1 3.8 %collective-permute-start.12 = (f32[48,128]{1,0:T(8,128)S(1)}, f32[48,128]{1,0:T(8,128)S(1)}, u32[]{:S(2)}, u32[]{:S(2)}) collective-permute-start(f32[48,128]{1,0:T(8,128)S(1)} %shard_map.84.refs_1_), channel_id=1, source_target_pairs={{0,96},{32,0},{64,32},{96,64},{1,97},{33,1},{65,33},{97,65},{2,98}... | collective-permute-start | bytes 73736 | tf_op jit(solution)/shard_map/ppermute | solution.py:301

commit v8 on v7

--- a/solution.py
+++ b/solution.py
@@ -40,7 +40,8 @@
 
 
 def load(
-    place, shift, measured, frac, volume, whole, same, cross, parts, block, half, sems, done
+    place, shift, measured, frac, volume, whole, same, cross, first, second, third, fourth,
+    block, sems,
 ):
     angles, cols = measured.shape[1:3]
     phase = place[1]
@@ -51,9 +52,12 @@
         copies[-1].start()
 
     columns = pl.ds(pl.multiple_of(HALO * phase, HALO), HALO)
-    slabs = parts.shape[0]
-    for k in range(slabs):
-        start(volume.at[:, columns, pl.ds(k * LANES, LANES)], half.at[k])
+    shares = (first, second, third, fourth)
+    for k, share in enumerate(shares):
+        to = place[0] + k
+        to = jnp.where(to >= len(shares), to - len(shares), to)
+        part = pl.ds(pl.multiple_of(to * LANES, LANES), LANES)
+        start(volume.at[:, columns, part], share)
     edge = pl.multiple_of((cols - 8) * (1 - phase), 8)
     start(volume.at[:, pl.ds(edge, 8), :], block)
     lanes = pl.ds(pl.multiple_of(place[0] * LANES, LANES), LANES)
@@ -61,12 +65,7 @@
     start(frac.at[0, :, lanes], whole.at[angles])
     for k in range(cols):
         whole[angles + 1, k : k + 1, :] = jnp.full((1, LANES), shift[0, k], jnp.int32).astype(F32)
-    sent = []
-    for k in range(slabs):
-        copies[k].wait()
-        sent.append(pltpu.make_async_copy(half.at[k], parts.at[k], done.at[k]))
-        sent[k].start()
-    for copy in copies[slabs:]:
+    for copy in copies:
         copy.wait()
     same[0 : angles + 2] = whole[:, pl.ds(pl.multiple_of(HALO * (1 - phase), HALO), HALO), :]
     rim = jnp.where(phase == 0, block[:, 7, :], block[:, 0, :])
@@ -74,8 +73,6 @@
         lanes = slice(k // 2 * LANES, (k // 2 + 1) * LANES)
         same[angles + 2 + k] = rim[k % 2 * HALO : (k % 2 + 1) * HALO, lanes]
     cross[...] = whole[:, columns, :]
-    for copy in sent:
-        copy.wait()
 
 
 def pack(place, index, other, same, table, volume, first, second, third, fourth, block, low, high, sem):
@@ -125,8 +122,8 @@
 
 
 def core(
-    place, steps, parts, a, b, c, d, seen, share, grad, weights, own, other,
-    ext, field, canvas, beside,
+    place, steps, first, second, third, fourth, a, b, c, d, seen, share, grad, weights, own, other,
+    ext, field, canvas, beside, parts,
 ):
     slabs, depth, half, width = parts.shape
     angles = seen.shape[2]
@@ -142,6 +139,7 @@
         rows = pl.ds(pl.multiple_of(source * depth, depth), depth)
         beside[0, rows, :] = ref[2]
         beside[1, rows, :] = ref[3]
+        parts[source] = (first, second, third, fourth)[k][...]
     nothing = jnp.zeros((2 * angles, width), F32)
 
     def put(columns, at):
@@ -303,18 +301,19 @@
     rim = depth * height // (HALO * LANES)
     bundles = [(angles + 2 + more, size, LANES) for more, size in ((0, cols), (rim, HALO), (0, HALO))]
     message = (slabs, depth, HALO, LANES)
-    bundle_own, same, cross, parts = call(
+    bundle_own, same, cross, *parts = call(
         load,
-        bundles + [message],
+        bundles + [message[1:]] * slabs,
         [SMEM] * 2 + [ANY] * 3,
-        [octet, pltpu.VMEM(message, F32), dma((slabs + 3,)), dma((slabs,))],
-        [VMEM] * 3 + [ANY],
+        [octet, dma((slabs + 3,))],
         limit=ROOM,
     )(place, shift, measured, frac, volume)
     index_other = move(angle_index, partner)
+    bundle_own, same, cross, index_other, *parts = lax.optimization_barrier(
+        (bundle_own, same, cross, index_other, *parts)
+    )
     bundle_other = move(bundle_own, partner)
-    parts, index_other = lax.optimization_barrier((parts, index_other))
-    parts = lax.all_to_all(parts, "slab", 0, 0, tiled=True)
+    parts = [parts[0]] + [around(parts[k], k) for k in range(1, slabs)]
     same = move(same, toward)
     cross = move(cross, across)
     wide = pltpu.VMEM((depth, height), F32)
@@ -331,22 +330,20 @@
         [SMEM] + [VMEM] * 4,
     )(place, bundle_own, bundle_other, same, cross)
     steps = steps[:, :, 0].astype(jnp.int32)
-    parts, seen, share, steps, *extras = lax.optimization_barrier(
-        (parts, seen, share, steps, *extras)
-    )
     window, side, canvas = (SPAN, LANES), (ROWS, LANES), (4 * HALO, LANES)
     stack = (HALO + 4, 2 * angles, LANES)
     grad, weights, own, other = call(
         core,
         [stack, (2 * angles, LANES), canvas, canvas],
-        [SMEM] * 2 + [VMEM] * 7,
+        [SMEM] * 2 + [VMEM] * 10,
         [
             pltpu.VMEM(stack, F32),
             pltpu.VMEM((phases, SPAN, LANES), F32),
             pltpu.VMEM((phases,) + canvas, F32),
             pltpu.VMEM((2, slabs * depth, LANES), F32),
+            pltpu.VMEM(message, F32),
         ],
-    )(place, steps, parts, *extras, seen, share)
+    )(place, steps, *parts, *extras, seen, share)
     (parts,) = call(
         spread,
         [(group, HALO, depth, LANES)],

time: 86.8 us -> 85.4 us (0.984)
  the two profiles are of different devices: /device:TPU:192 before, /device:TPU:128 now
where the time goes in v8:
time: 85.4 us; the launch traced here: 84.6 us
  waiting for transfers between devices  35.3 us (41%)
  starting transfers between devices  33 us (39%)
  Pallas kernels  14.7 us (17%)
    ppermute x1, waiting for transfers between devices, body(): lax.ppermute(side_o, 'tile', pairs_o)  19.7 us
    ppermute x9, starting transfers between devices, around(): lax.ppermute(block, 'slab', [(i, (i + distance) % slabs) for i in range(s...  16.6 us
    ppermute x5, waiting for transfers between devices, move(): return lax.ppermute(block, ('phase', 'tile'), route)  11.7 us
    ppermute x5, starting transfers between devices, move(): return lax.ppermute(block, ('phase', 'tile'), route)  8.51 us
    ppermute x9, waiting for transfers between devices, around(): lax.ppermute(block, 'slab', [(i, (i + distance) % slabs) for i in range(s...  3.96 us
    all_to_all x1, starting transfers between devices, body(): parts = lax.all_to_all(parts, ('phase', 'slab'), 0, 0, tiled=True)  3.9 us
    ppermute x1, starting transfers between devices, body(): lax.ppermute(side_o, 'tile', pairs_o)  3.84 us
    pallas_call x1, Pallas kernels, body(): call(load, bundles + [message[1:]] * slabs, [SMEM] * 2 + [ANY] * 3, [octe...  3.78 us
  transfers between devices with their start and end apart: 17, of which 6 were waited for; matrix products, arithmetic and copies ran while one was open for 1% of the time, Pallas kernels for 12%

profile of v8, /device:TPU:128, one launch (start us, length us, event | category | flops | bytes accessed | tf_op | source)
XLA Modules:
  0.0 84.6 jit_solution(6049914578745212461)
XLA Ops:
  0.6 1.1 %collective-permute-start = (s32[1,32]{1,0:T(1,128)}, s32[1,32]{1,0:T(1,128)S(1)}, u32[]{:S(2)}, u32[]{:S(2)}) collective-permute-start(s32[1,32]{1,0:T(1,128)} %index.1), channel_id=1, source_target_pairs={{0,128},{1,129},{2,130},{3,131},{4,132},{5,133},{6,134},{7,135},{8... | collective-permute-start | bytes 392 | tf_op jit(solution)/shard_map/ppermute | solution.py:273
  1.7 0.6 pad_add_fusion.place.refs_0_
  2.4 3.8 %shard_map.77 = (f32[34,32,128]{2,1,0:T(8,128)}, f32[42,16,128]{2,1,0:T(8,128)}, f32[34,16,128]{2,1,0:T(8,128)}, f32[32,16,128]{2,1,0:T(8,128)}, f32[32,16,128]{...) custom-call(s32[4]{0:T(128)} %pad_add_fusion.place.refs_0_, s32[1,32]{1,0:T(1,128)} %shift.1, ...), custom_call_target="tpu_custom_call" | custom-call | flops 4194304 | bytes 2097152 | tf_op jit(solution)/shard_map/pallas_call | solution.py:304
  6.2 0.0 copy-start.1
  6.2 0.0 collective-permute-done.other
  6.2 1.1 %collective-permute-start.1 = (f32[34,32,128]{2,1,0:T(8,128)}, f32[34,32,128]{2,1,0:T(8,128)S(1)}, u32[]{:S(2)}, u32[]{:S(2)}) collective-permute-start(f32[34,32,128]{2,1,0:T(8,128)} %get-tuple-element.45.own), channel_id=1, source_target_pairs={{0,128},{1,129},{2,130},{3,131},{4,132},{5,133},{6,134},{7,135},{8... | collective-permute-start | bytes 1671176 | tf_op jit(solution)/shard_map/ppermute | solution.py:273
  7.3 1.9 %collective-permute-start.2 = (f32[42,16,128]{2,1,0:T(8,128)}, f32[42,16,128]{2,1,0:T(8,128)S(1)}, u32[]{:S(2)}, u32[]{:S(2)}) collective-permute-start(f32[42,16,128]{2,1,0:T(8,128)} %get-tuple-element.46), channel_id=1, source_target_pairs={{0,1},{1,2},{2,3},{3,4},{4,5},{5,6},{6,7},{7,8},{8,9},{9,10},{10,1... | collective-permute-start | bytes 1032200 | tf_op jit(solution)/shard_map/ppermute | solution.py:273
  9.2 4.3 %collective-permute-start.3 = (f32[34,16,128]{2,1,0:T(8,128)}, f32[34,16,128]{2,1,0:T(8,128)S(1)}, u32[]{:S(2)}, u32[]{:S(2)}) collective-permute-start(f32[34,16,128]{2,1,0:T(8,128)} %get-tuple-element.47), channel_id=1, source_target_pairs={{1,128},{2,129},{3,130},{4,131},{5,132},{6,133},{7,134},{8,135},{9... | collective-permute-start | bytes 835592 | tf_op jit(solution)/shard_map/ppermute | solution.py:273
  13.5 1.7 %collective-permute-start.4 = (f32[32,16,128]{2,1,0:T(8,128)}, f32[32,16,128]{2,1,0:T(8,128)S(1)}, u32[]{:S(2)}, u32[]{:S(2)}) collective-permute-start(f32[32,16,128]{2,1,0:T(8,128)} %get-tuple-element.50), channel_id=1, source_target_pairs={{0,32},{32,64},{64,96},{96,0},{1,33},{33,65},{65,97},{97,1},{2,34}... | collective-permute-start | bytes 786440 | tf_op jit(solution)/shard_map/ppermute | solution.py:299
  15.2 2.9 %collective-permute-start.5 = (f32[32,16,128]{2,1,0:T(8,128)}, f32[32,16,128]{2,1,0:T(8,128)S(1)}, u32[]{:S(2)}, u32[]{:S(2)}) collective-permute-start(f32[32,16,128]{2,1,0:T(8,128)} %get-tuple-element.51), channel_id=1, source_target_pairs={{0,64},{32,96},{64,0},{96,32},{1,65},{33,97},{65,1},{97,33},{2,66}... | collective-permute-start | bytes 786440 | tf_op jit(solution)/shard_map/ppermute | solution.py:299
  18.1 9.7 %collective-permute-done.2.same = f32[42,16,128]{2,1,0:T(8,128)S(1)} collective-permute-done((f32[42,16,128]{2,1,0:T(8,128)}, f32[42,16,128]{2,1,0:T(8,128)S(1)}, u32[]{:S(2)}, u32[]{:S(2)}) %collective-permute-start.2) | collective-permute-done | bytes 344096 | tf_op jit(solution)/shard_map/ppermute | solution.py:273
  27.7 3.0 %collective-permute-start.6 = (f32[32,16,128]{2,1,0:T(8,128)}, f32[32,16,128]{2,1,0:T(8,128)S(1)}, u32[]{:S(2)}, u32[]{:S(2)}) collective-permute-start(f32[32,16,128]{2,1,0:T(8,128)} %get-tuple-element.52), channel_id=1, source_target_pairs={{0,96},{32,0},{64,32},{96,64},{1,97},{33,1},{65,33},{97,65},{2,98}... | collective-permute-start | bytes 786440 | tf_op jit(solution)/shard_map/ppermute | solution.py:299
  30.7 0.0 copy-done.3
  30.8 1.3 %shard_map.79 = (f32[4,32,128]{2,1,0:T(8,128)S(1)}, f32[4,32,128]{2,1,0:T(8,128)S(1)}, f32[4,32,128]{2,1,0:T(8,128)S(1)}, f32[4,32,128]{2,1,0:T(8,128)S(1)}) custom-call(s32[4]{0:T(128)S(1)} %copy-done.4, s32[1,32]{1,0:T(1,128)S(1)} %copy-done.5, s32[1,32]{1,0:T(1,128)S(1)} %collective-permute-done.other, f32[42,16,128]{2,1,0:T(8,128)S(1)} %collective-permute-done.2.same, ...), custom_call_target="tpu_custom_call" | custom-call | flops 4194304 | bytes 2097152 | tf_op jit(solution)/shard_map/pallas_call | solution.py:320
  32.1 0.0 collective-permute-done.3.cross
  32.1 0.1 collective-permute-start.7
  32.2 0.0 collective-permute-done.1.other
  32.2 2.2 %collective-permute-start.8 = (f32[4,32,128]{2,1,0:T(8,128)S(1)}, f32[4,32,128]{2,1,0:T(8,128)S(1)}, u32[]{:S(2)}, u32[]{:S(2)}) collective-permute-start(f32[4,32,128]{2,1,0:T(8,128)S(1)} %get-tuple-element.56), channel_id=1, source_target_pairs={{0,64},{32,96},{64,0},{96,32},{1,65},{33,97},{65,1},{97,33},{2,66}... | collective-permute-start | bytes 196616 | tf_op jit(solution)/shard_map/ppermute | solution.py:299
  34.4 0.0 copy-done.1
  34.4 0.8 shard_map.78
  35.2 0.0 collective-permute-done.4.second
  35.2 1.1 %collective-permute-start.9 = (f32[4,32,128]{2,1,0:T(8,128)S(1)}, f32[4,32,128]{2,1,0:T(8,128)S(1)}, u32[]{:S(2)}, u32[]{:S(2)}) collective-permute-start(f32[4,32,128]{2,1,0:T(8,128)S(1)} %get-tuple-element.57), channel_id=1, source_target_pairs={{0,96},{32,0},{64,32},{96,64},{1,97},{33,1},{65,33},{97,65},{2,98}... | collective-permute-start | bytes 196616 | tf_op jit(solution)/shard_map/ppermute | solution.py:299
  36.3 0.1 convert_reduce_fusion.steps
  36.5 0.0 collective-permute-done.5.third
  36.5 0.0 collective-permute-done.6.fourth
  36.5 1.9 %collective-permute-done.7.b = f32[4,32,128]{2,1,0:T(8,128)S(1)} collective-permute-done((f32[4,32,128]{2,1,0:T(8,128)S(1)}, f32[4,32,128]{2,1,0:T(8,128)S(1)}, u32[]{:S(2)}, u32[]{:S(2)}) %collective-permute-start.7) | collective-permute-done | bytes 65568 | tf_op jit(solution)/shard_map/ppermute | solution.py:299
  38.4 0.0 collective-permute-done.8.c
  38.4 1.2 %collective-permute-done.9.d = f32[4,32,128]{2,1,0:T(8,128)S(1)} collective-permute-done((f32[4,32,128]{2,1,0:T(8,128)S(1)}, f32[4,32,128]{2,1,0:T(8,128)S(1)}, u32[]{:S(2)}, u32[]{:S(2)}) %collective-permute-start.9) | collective-permute-done | bytes 65568 | tf_op jit(solution)/shard_map/ppermute | solution.py:299
  39.6 2.8 %shard_map.80 = (f32[20,64,128]{2,1,0:T(8,128)S(1)}, f32[64,128]{1,0:T(8,128)S(1)}, f32[64,128]{1,0:T(8,128)S(1)}, f32[64,128]{1,0:T(8,128)S(1)}) custom-call(s32[4]{0:T(128)S(1)} %copy-done.4, s32[2,48]{1,0:T(2,128)S(1)} %convert_reduce_fusion.steps, f32[32,16,128]{2,1,0:T(8,128)S(1)} %copy-done.2, f32[32,16,128]{2,1,0:T(8,128)S(1)} %collective-permute-done.4.second, ...), custom_call_target="tpu_custom_call" | custom-call | flops 4194304 | bytes 2097152 | tf_op jit(solution)/shard_map/pallas_call | solution.py:335
  42.3 0.1 collective-permute-start.10
  42.4 1.9 %shard_map.81 = f32[8,16,32,128]{3,2,1,0:T(8,128)} custom-call(f32[20,64,128]{2,1,0:T(8,128)S(1)} %get-tuple-element.60.grad, f32[64,128]{1,0:T(8,128)S(1)} %get-tuple-element.61.weights), custom_call_target="tpu_custom_call" | custom-call | flops 4194304 | bytes 2097152 | tf_op jit(solution)/shard_map/pallas_call | solution.py:347
  44.3 2.0 %collective-permute-done.10.other = f32[64,128]{1,0:T(8,128)S(1)} collective-permute-done((f32[64,128]{1,0:T(8,128)S(1)}, f32[64,128]{1,0:T(8,128)S(1)}, u32[]{:S(2)}, u32[]{:S(2)}) %collective-permute-start.10) | collective-permute-done | bytes 32800 | tf_op jit(solution)/shard_map/ppermute | solution.py:273
  46.3 3.9 %all-to-all-start = ((f32[8,16,32,128]{3,2,1,0:T(8,128)}), f32[8,16,32,128]{3,2,1,0:T(8,128)S(1)}, u32[]{:S(2)}, u32[]{:S(2)}) async-start(f32[8,16,32,128]{3,2,1,0:T(8,128)} %shard_map.81), calls=%async_computation | async-start | bytes 4194304 | tf_op jit(solution)/shard_map/all_to_all | solution.py:357
  50.2 0.5 shard_map.83
  50.8 3.8 %collective-permute-start.11 = (f32[24,128]{1,0:T(8,128)S(1)}, f32[24,128]{1,0:T(8,128)S(1)}, u32[]{:S(2)}, u32[]{:S(2)}) collective-permute-start(f32[24,128]{1,0:T(8,128)S(1)} %get-tuple-element.67), channel_id=1, source_target_pairs={{1,2},{2,1},{3,4},{4,3},{5,6},{6,5},{7,8},{8,7},{9,10},{10,9},{11,... | collective-permute-start | bytes 36872 | tf_op jit(solution)/shard_map/ppermute | solution.py:364
  54.7 0.1 collective-permute-start.12
  54.8 19.7 %collective-permute-done.11.side_o = f32[24,128]{1,0:T(8,128)S(1)} collective-permute-done((f32[24,128]{1,0:T(8,128)S(1)}, f32[24,128]{1,0:T(8,128)S(1)}, u32[]{:S(2)}, u32[]{:S(2)}) %collective-permute-start.11) | collective-permute-done | bytes 12320 | tf_op jit(solution)/shard_map/ppermute | solution.py:364
  74.4 0.0 collective-permute-done.12.side_e
  74.4 0.6 shard_map.84.refs_1_
  75.0 1.5 %collective-permute-start.13 = (f32[48,128]{1,0:T(8,128)S(1)}, f32[48,128]{1,0:T(8,128)S(1)}, u32[]{:S(2)}, u32[]{:S(2)}) collective-permute-start(f32[48,128]{1,0:T(8,128)S(1)} %shard_map.84.refs_1_), channel_id=1, source_target_pairs={{0,32},{32,64},{64,96},{96,0},{1,33},{33,65},{65,97},{97,1},{2,34}... | collective-permute-start | bytes 73736 | tf_op jit(solution)/shard_map/ppermute | solution.py:299
  76.5 2.7 %collective-permute-start.14 = (f32[48,128]{1,0:T(8,128)S(1)}, f32[48,128]{1,0:T(8,128)S(1)}, u32[]{:S(2)}, u32[]{:S(2)}) collective-permute-start(f32[48,128]{1,0:T(8,128)S(1)} %shard_map.84.refs_1_), channel_id=1, source_target_pairs={{0,64},{32,96},{64,0},{96,32},{1,65},{33,97},{65,1},{97,33},{2,66}... | collective-permute-start | bytes 73736 | tf_op jit(solution)/shard_map/ppermute | solution.py:299
  79.2 1.5 %collective-permute-start.15 = (f32[48,128]{1,0:T(8,128)S(1)}, f32[48,128]{1,0:T(8,128)S(1)}, u32[]{:S(2)}, u32[]{:S(2)}) collective-permute-start(f32[48,128]{1,0:T(8,128)S(1)} %shard_map.84.refs_1_), channel_id=1, source_target_pairs={{0,96},{32,0},{64,32},{96,64},{1,97},{33,1},{65,33},{97,65},{2,98}... | collective-permute-start | bytes 73736 | tf_op jit(solution)/shard_map/ppermute | solution.py:299
  80.7 0.0 all-to-all-done.parts
  80.7 1.4 %shard_map.82 = f32[32,32,512]{2,1,0:T(8,128)} custom-call(f32[8,16,32,128]{3,2,1,0:T(8,128)S(1)} %all-to-all-done.parts), custom_call_target="tpu_custom_call" | custom-call | flops 4194304 | bytes 2097152 | tf_op jit(solution)/shard_map/pallas_call | solution.py:371
  82.1 0.0 collective-permute-done.13.refs_2_
  82.1 0.0 collective-permute-done.14.refs_3_
  82.1 0.8 %collective-permute-done.15.refs_4_ = f32[48,128]{1,0:T(8,128)S(1)} collective-permute-done((f32[48,128]{1,0:T(8,128)S(1)}, f32[48,128]{1,0:T(8,128)S(1)}, u32[]{:S(2)}, u32[]{:S(2)}) %collective-permute-start.15) | collective-permute-done | bytes 24608 | tf_op jit(solution)/shard_map/ppermute | solution.py:299
  83.0 1.6 %shard_map.85 = f32[1,32,512]{2,1,0:T(8,128)} custom-call(s32[4]{0:T(128)S(1)} %copy-done.4, f32[48,128]{1,0:T(8,128)S(1)} %shard_map.84.refs_1_, f32[48,128]{1,0:T(8,128)S(1)} %collective-permute-done.13.refs_2_, f32[48,128]{1,0:T(8,128)S(1)} %collective-permute-done.14.refs_3_, f32[48,128]{1,0:T(8,128)S(1)} %collective-permute-done.15.refs_4_), custom_call_target="tpu_custom_call" | custom-call | flops 4194304 | bytes 2097152 | tf_op jit(solution)/shard_map/pallas_call | solution.py:375
  (9 shorter events, 0.0 us)
Async XLA Ops:
  0.6 5.5 %collective-permute-start = (s32[1,32]{1,0:T(1,128)}, s32[1,32]{1,0:T(1,128)S(1)}, u32[]{:S(2)}, u32[]{:S(2)}) collective-permute-start(s32[1,32]{1,0:T(1,128)} %index.1), channel_id=1, source_target_pairs={{0,128},{1,129},{2,130},{3,131},{4,132},{5,133},{6,134},{7,135},{8... | collective-permute-start | bytes 392 | tf_op jit(solution)/shard_map/ppermute | solution.py:273
  2.4 28.4 %copy-start = (f32[32,32,512]{2,1,0:T(8,128)S(1)}, f32[32,32,512]{2,1,0:T(8,128)}, u32[]{:S(2)}) copy-start(f32[32,32,512]{2,1,0:T(8,128)} %volume.3) | copy-start | bytes 6291460
  2.4 28.4 %copy-start.3 = (f32[680,32]{0,1:T(8,128)S(1)}, f32[680,32]{0,1:T(8,128)}, u32[]{:S(2)}) copy-start(f32[680,32]{0,1:T(8,128)} %param.10) | copy-start | bytes 261124
  2.4 28.4 %copy-start.4 = (s32[4]{0:T(128)S(1)}, s32[4]{0:T(128)}, u32[]{:S(2)}) copy-start(s32[4]{0:T(128)} %pad_add_fusion.place.refs_0_) | copy-start | bytes 52
  2.4 28.4 %copy-start.5 = (s32[1,32]{1,0:T(1,128)S(1)}, s32[1,32]{1,0:T(1,128)}, u32[]{:S(2)}) copy-start(s32[1,32]{1,0:T(1,128)} %index.1) | copy-start | bytes 388
  6.2 28.2 %copy-start.1 = (f32[34,32,128]{2,1,0:T(8,128)S(1)}, f32[34,32,128]{2,1,0:T(8,128)}, u32[]{:S(2)}) copy-start(f32[34,32,128]{2,1,0:T(8,128)} %get-tuple-element.45.own) | copy-start | bytes 1671172
  6.2 26.0 %collective-permute-start.1 = (f32[34,32,128]{2,1,0:T(8,128)}, f32[34,32,128]{2,1,0:T(8,128)S(1)}, u32[]{:S(2)}, u32[]{:S(2)}) collective-permute-start(f32[34,32,128]{2,1,0:T(8,128)} %get-tuple-element.45.own), channel_id=1, source_target_pairs={{0,128},{1,129},{2,130},{3,131},{4,132},{5,133},{6,134},{7,135},{8... | collective-permute-start | bytes 1671176 | tf_op jit(solution)/shard_map/ppermute | solution.py:273
  7.3 20.4 %collective-permute-start.2 = (f32[42,16,128]{2,1,0:T(8,128)}, f32[42,16,128]{2,1,0:T(8,128)S(1)}, u32[]{:S(2)}, u32[]{:S(2)}) collective-permute-start(f32[42,16,128]{2,1,0:T(8,128)} %get-tuple-element.46), channel_id=1, source_target_pairs={{0,1},{1,2},{2,3},{3,4},{4,5},{5,6},{6,7},{7,8},{8,9},{9,10},{10,1... | collective-permute-start | bytes 1032200 | tf_op jit(solution)/shard_map/ppermute | solution.py:273
  9.2 22.9 %collective-permute-start.3 = (f32[34,16,128]{2,1,0:T(8,128)}, f32[34,16,128]{2,1,0:T(8,128)S(1)}, u32[]{:S(2)}, u32[]{:S(2)}) collective-permute-start(f32[34,16,128]{2,1,0:T(8,128)} %get-tuple-element.47), channel_id=1, source_target_pairs={{1,128},{2,129},{3,130},{4,131},{5,132},{6,133},{7,134},{8,135},{9... | collective-permute-start | bytes 835592 | tf_op jit(solution)/shard_map/ppermute | solution.py:273
  13.5 21.7 %collective-permute-start.4 = (f32[32,16,128]{2,1,0:T(8,128)}, f32[32,16,128]{2,1,0:T(8,128)S(1)}, u32[]{:S(2)}, u32[]{:S(2)}) collective-permute-start(f32[32,16,128]{2,1,0:T(8,128)} %get-tuple-element.50), channel_id=1, source_target_pairs={{0,32},{32,64},{64,96},{96,0},{1,33},{33,65},{65,97},{97,1},{2,34}... | collective-permute-start | bytes 786440 | tf_op jit(solution)/shard_map/ppermute | solution.py:299
  15.2 21.3 %collective-permute-start.5 = (f32[32,16,128]{2,1,0:T(8,128)}, f32[32,16,128]{2,1,0:T(8,128)S(1)}, u32[]{:S(2)}, u32[]{:S(2)}) collective-permute-start(f32[32,16,128]{2,1,0:T(8,128)} %get-tuple-element.51), channel_id=1, source_target_pairs={{0,64},{32,96},{64,0},{96,32},{1,65},{33,97},{65,1},{97,33},{2,66}... | collective-permute-start | bytes 786440 | tf_op jit(solution)/shard_map/ppermute | solution.py:299
  27.7 8.8 %collective-permute-start.6 = (f32[32,16,128]{2,1,0:T(8,128)}, f32[32,16,128]{2,1,0:T(8,128)S(1)}, u32[]{:S(2)}, u32[]{:S(2)}) collective-permute-start(f32[32,16,128]{2,1,0:T(8,128)} %get-tuple-element.52), channel_id=1, source_target_pairs={{0,96},{32,0},{64,32},{96,64},{1,97},{33,1},{65,33},{97,65},{2,98}... | collective-permute-start | bytes 786440 | tf_op jit(solution)/shard_map/ppermute | solution.py:299
  30.7 8.8 %copy-start.2 = (f32[32,16,128]{2,1,0:T(8,128)S(1)}, f32[32,16,128]{2,1,0:T(8,128)}, u32[]{:S(2)}) copy-start(f32[32,16,128]{2,1,0:T(8,128)} %get-tuple-element.49.first) | copy-start | bytes 786436
  32.1 6.3 %collective-permute-start.7 = (f32[4,32,128]{2,1,0:T(8,128)S(1)}, f32[4,32,128]{2,1,0:T(8,128)S(1)}, u32[]{:S(2)}, u32[]{:S(2)}) collective-permute-start(f32[4,32,128]{2,1,0:T(8,128)S(1)} %get-tuple-element.55), channel_id=1, source_target_pairs={{0,32},{32,64},{64,96},{96,0},{1,33},{33,65},{65,97},{97,1},{2,34}... | collective-permute-start | bytes 196616 | tf_op jit(solution)/shard_map/ppermute | solution.py:299
  32.2 6.2 %collective-permute-start.8 = (f32[4,32,128]{2,1,0:T(8,128)S(1)}, f32[4,32,128]{2,1,0:T(8,128)S(1)}, u32[]{:S(2)}, u32[]{:S(2)}) collective-permute-start(f32[4,32,128]{2,1,0:T(8,128)S(1)} %get-tuple-element.56), channel_id=1, source_target_pairs={{0,64},{32,96},{64,0},{96,32},{1,65},{33,97},{65,1},{97,33},{2,66}... | collective-permute-start | bytes 196616 | tf_op jit(solution)/shard_map/ppermute | solution.py:299
  35.2 4.4 %collective-permute-start.9 = (f32[4,32,128]{2,1,0:T(8,128)S(1)}, f32[4,32,128]{2,1,0:T(8,128)S(1)}, u32[]{:S(2)}, u32[]{:S(2)}) collective-permute-start(f32[4,32,128]{2,1,0:T(8,128)S(1)} %get-tuple-element.57), channel_id=1, source_target_pairs={{0,96},{32,0},{64,32},{96,64},{1,97},{33,1},{65,33},{97,65},{2,98}... | collective-permute-start | bytes 196616 | tf_op jit(solution)/shard_map/ppermute | solution.py:299
  42.3 4.0 %collective-permute-start.10 = (f32[64,128]{1,0:T(8,128)S(1)}, f32[64,128]{1,0:T(8,128)S(1)}, u32[]{:S(2)}, u32[]{:S(2)}) collective-permute-start(f32[64,128]{1,0:T(8,128)S(1)} %get-tuple-element.62), channel_id=1, source_target_pairs={{0,128},{1,129},{2,130},{3,131},{4,132},{5,133},{6,134},{7,135},{8... | collective-permute-start | bytes 98312 | tf_op jit(solution)/shard_map/ppermute | solution.py:273
  46.3 34.3 %all-to-all-start = ((f32[8,16,32,128]{3,2,1,0:T(8,128)}), f32[8,16,32,128]{3,2,1,0:T(8,128)S(1)}, u32[]{:S(2)}, u32[]{:S(2)}) async-start(f32[8,16,32,128]{3,2,1,0:T(8,128)} %shard_map.81), calls=%async_computation | async-start | bytes 4194304 | tf_op jit(solution)/shard_map/all_to_all | solution.py:357
  50.8 23.6 %collective-permute-start.11 = (f32[24,128]{1,0:T(8,128)S(1)}, f32[24,128]{1,0:T(8,128)S(1)}, u32[]{:S(2)}, u32[]{:S(2)}) collective-permute-start(f32[24,128]{1,0:T(8,128)S(1)} %get-tuple-element.67), channel_id=1, source_target_pairs={{1,2},{2,1},{3,4},{4,3},{5,6},{6,5},{7,8},{8,7},{9,10},{10,9},{11,... | collective-permute-start | bytes 36872 | tf_op jit(solution)/shard_map/ppermute | solution.py:364
  54.7 19.8 %collective-permute-start.12 = (f32[24,128]{1,0:T(8,128)S(1)}, f32[24,128]{1,0:T(8,128)S(1)}, u32[]{:S(2)}, u32[]{:S(2)}) collective-permute-start(f32[24,128]{1,0:T(8,128)S(1)} %get-tuple-element.68), channel_id=1, source_target_pairs={{0,1},{1,0},{2,3},{3,2},{4,5},{5,4},{6,7},{7,6},{8,9},{9,8},{10,11... | collective-permute-start | bytes 36872 | tf_op jit(solution)/shard_map/ppermute | solution.py:364
  75.0 7.1 %collective-permute-start.13 = (f32[48,128]{1,0:T(8,128)S(1)}, f32[48,128]{1,0:T(8,128)S(1)}, u32[]{:S(2)}, u32[]{:S(2)}) collective-permute-start(f32[48,128]{1,0:T(8,128)S(1)} %shard_map.84.refs_1_), channel_id=1, source_target_pairs={{0,32},{32,64},{64,96},{96,0},{1,33},{33,65},{65,97},{97,1},{2,34}... | collective-permute-start | bytes 73736 | tf_op jit(solution)/shard_map/ppermute | solution.py:299
  76.5 5.6 %collective-permute-start.14 = (f32[48,128]{1,0:T(8,128)S(1)}, f32[48,128]{1,0:T(8,128)S(1)}, u32[]{:S(2)}, u32[]{:S(2)}) collective-permute-start(f32[48,128]{1,0:T(8,128)S(1)} %shard_map.84.refs_1_), channel_id=1, source_target_pairs={{0,64},{32,96},{64,0},{96,32},{1,65},{33,97},{65,1},{97,33},{2,66}... | collective-permute-start | bytes 73736 | tf_op jit(solution)/shard_map/ppermute | solution.py:299
  79.2 3.8 %collective-permute-start.15 = (f32[48,128]{1,0:T(8,128)S(1)}, f32[48,128]{1,0:T(8,128)S(1)}, u32[]{:S(2)}, u32[]{:S(2)}) collective-permute-start(f32[48,128]{1,0:T(8,128)S(1)} %shard_map.84.refs_1_), channel_id=1, source_target_pairs={{0,96},{32,0},{64,32},{96,64},{1,97},{33,1},{65,33},{97,65},{2,98}... | collective-permute-start | bytes 73736 | tf_op jit(solution)/shard_map/ppermute | solution.py:299

commit v9 on v8

--- a/solution.py
+++ b/solution.py
@@ -306,7 +306,7 @@
         bundles + [message[1:]] * slabs,
         [SMEM] * 2 + [ANY] * 3,
         [octet, dma((slabs + 3,))],
-        limit=ROOM,
+        limit=50,
     )(place, shift, measured, frac, volume)
     index_other = move(angle_index, partner)
     bundle_own, same, cross, index_other, *parts = lax.optimization_barrier(

time: 85.4 us -> 84.8 us (level)
  local copies, waits for them, and re-layouts: 0.03 us -> 1.51 us
  Pallas kernels: 14.7 us -> 13.3 us
    unnamed x12 -> x10, local copies, waits for them, and re-layouts: 0.03 us -> 1.51 us
    pallas_call x1, Pallas kernels: 3.78 us -> 2.34 us  [body(): call(load, bundles + [message[1:]] * slabs, [SMEM] * 2 + [ANY] * 3, [octe...]
  transfers between devices with their start and end apart: 17 -> 17, of which waited for: 6 -> 6; matrix products, arithmetic and copies ran while one was open for 1% -> 0% of each run, Pallas kernels for 12% -> 11%
where the time goes in v9:
time: 84.8 us; the launch traced here: 84.4 us
  waiting for transfers between devices  35.6 us (42%)
  starting transfers between devices  33.1 us (39%)
  Pallas kernels  13.3 us (16%)
  local copies, waits for them, and re-layouts  1.51 us (2%)
    ppermute x1, waiting for transfers between devices, body(): lax.ppermute(side_o, 'tile', pairs_o)  19.8 us
    ppermute x9, starting transfers between devices, around(): lax.ppermute(block, 'slab', [(i, (i + distance) % slabs) for i in range(s...  16.7 us
    ppermute x5, waiting for transfers between devices, move(): return lax.ppermute(block, ('phase', 'tile'), route)  11.5 us
    ppermute x5, starting transfers between devices, move(): return lax.ppermute(block, ('phase', 'tile'), route)  8.51 us
    ppermute x9, waiting for transfers between devices, around(): lax.ppermute(block, 'slab', [(i, (i + distance) % slabs) for i in range(s...  4.28 us
    ppermute x1, starting transfers between devices, body(): lax.ppermute(side_o, 'tile', pairs_o)  3.9 us
    all_to_all x1, starting transfers between devices, body(): parts = lax.all_to_all(parts, ('phase', 'slab'), 0, 0, tiled=True)  3.87 us
    pallas_call x1, Pallas kernels, body(): call(core, [stack, (2 * angles, LANES), canvas, canvas], [SMEM] * 2 + [VM...  2.79 us
  transfers between devices with their start and end apart: 17, of which 6 were waited for; matrix products, arithmetic and copies ran while one was open for 0% of the time, Pallas kernels for 11%

profile of v9, /device:TPU:128, one launch (start us, length us, event | category | flops | bytes accessed | tf_op | source)
XLA Modules:
  0.0 84.4 jit_solution(3083661775162215210)
XLA Ops:
  0.6 1.1 %collective-permute-start = (s32[1,32]{1,0:T(1,128)}, s32[1,32]{1,0:T(1,128)S(1)}, u32[]{:S(2)}, u32[]{:S(2)}) collective-permute-start(s32[1,32]{1,0:T(1,128)} %index.1), channel_id=1, source_target_pairs={{0,128},{1,129},{2,130},{3,131},{4,132},{5,133},{6,134},{7,135},{8... | collective-permute-start | bytes 392 | tf_op jit(solution)/shard_map/ppermute | solution.py:273
  1.7 0.1 pad_add_fusion.place.refs_0_
  1.8 0.8 copy-done.2
  2.7 0.7 copy-done.3
  3.3 2.3 %shard_map.77 = (f32[34,32,128]{2,1,0:T(8,128)S(1)}, f32[42,16,128]{2,1,0:T(8,128)S(1)}, f32[34,16,128]{2,1,0:T(8,128)S(1)}, f32[32,16,128]{2,1,0:T(8,128)S(1)},...) custom-call(s32[4]{0:T(128)S(1)} %pad_add_fusion.place.refs_0_, ...), custom_call_target="tpu_custom_call" | custom-call | flops 4194304 | bytes 2097152 | tf_op jit(solution)/shard_map/pallas_call | solution.py:304
  5.7 0.0 collective-permute-done.other
  5.7 1.1 %collective-permute-start.1 = (f32[34,32,128]{2,1,0:T(8,128)S(1)}, f32[34,32,128]{2,1,0:T(8,128)S(1)}, u32[]{:S(2)}, u32[]{:S(2)}) collective-permute-start(f32[34,32,128]{2,1,0:T(8,128)S(1)} %get-tuple-element.45.own), channel_id=1, source_target_pairs={{0,128},{1,129},{2,130},{3,131},{4,132},{5,133},{6,134},{7,135},{8... | collective-permute-start | bytes 1671176 | tf_op jit(solution)/shard_map/ppermute | solution.py:273
  6.8 1.9 %collective-permute-start.2 = (f32[42,16,128]{2,1,0:T(8,128)S(1)}, f32[42,16,128]{2,1,0:T(8,128)S(1)}, u32[]{:S(2)}, u32[]{:S(2)}) collective-permute-start(f32[42,16,128]{2,1,0:T(8,128)S(1)} %get-tuple-element.46), channel_id=1, source_target_pairs={{0,1},{1,2},{2,3},{3,4},{4,5},{5,6},{6,7},{7,8},{8,9},{9,10},{10,1... | collective-permute-start | bytes 1032200 | tf_op jit(solution)/shard_map/ppermute | solution.py:273
  8.7 4.3 %collective-permute-start.3 = (f32[34,16,128]{2,1,0:T(8,128)S(1)}, f32[34,16,128]{2,1,0:T(8,128)S(1)}, u32[]{:S(2)}, u32[]{:S(2)}) collective-permute-start(f32[34,16,128]{2,1,0:T(8,128)S(1)} %get-tuple-element.47), channel_id=1, source_target_pairs={{1,128},{2,129},{3,130},{4,131},{5,132},{6,133},{7,134},{8,135},{9... | collective-permute-start | bytes 835592 | tf_op jit(solution)/shard_map/ppermute | solution.py:273
  13.0 1.7 %collective-permute-start.4 = (f32[32,16,128]{2,1,0:T(8,128)S(1)}, f32[32,16,128]{2,1,0:T(8,128)S(1)}, u32[]{:S(2)}, u32[]{:S(2)}) collective-permute-start(f32[32,16,128]{2,1,0:T(8,128)S(1)} %get-tuple-element.50), channel_id=1, source_target_pairs={{0,32},{32,64},{64,96},{96,0},{1,33},{33,65},{65,97},{97,1},{2,34}... | collective-permute-start | bytes 786440 | tf_op jit(solution)/shard_map/ppermute | solution.py:299
  14.7 2.9 %collective-permute-start.5 = (f32[32,16,128]{2,1,0:T(8,128)S(1)}, f32[32,16,128]{2,1,0:T(8,128)S(1)}, u32[]{:S(2)}, u32[]{:S(2)}) collective-permute-start(f32[32,16,128]{2,1,0:T(8,128)S(1)} %get-tuple-element.51), channel_id=1, source_target_pairs={{0,64},{32,96},{64,0},{96,32},{1,65},{33,97},{65,1},{97,33},{2,66}... | collective-permute-start | bytes 786440 | tf_op jit(solution)/shard_map/ppermute | solution.py:299
  17.6 9.4 %collective-permute-done.2.same = f32[42,16,128]{2,1,0:T(8,128)S(1)} collective-permute-done((f32[42,16,128]{2,1,0:T(8,128)S(1)}, f32[42,16,128]{2,1,0:T(8,128)S(1)}, u32[]{:S(2)}, u32[]{:S(2)}) %collective-permute-start.2) | collective-permute-done | bytes 344096 | tf_op jit(solution)/shard_map/ppermute | solution.py:273
  27.0 3.0 %collective-permute-start.6 = (f32[32,16,128]{2,1,0:T(8,128)S(1)}, f32[32,16,128]{2,1,0:T(8,128)S(1)}, u32[]{:S(2)}, u32[]{:S(2)}) collective-permute-start(f32[32,16,128]{2,1,0:T(8,128)S(1)} %get-tuple-element.52), channel_id=1, source_target_pairs={{0,96},{32,0},{64,32},{96,64},{1,97},{33,1},{65,33},{97,65},{2,98}... | collective-permute-start | bytes 786440 | tf_op jit(solution)/shard_map/ppermute | solution.py:299
  30.0 0.0 copy-done
  30.0 1.3 %shard_map.79 = (f32[4,32,128]{2,1,0:T(8,128)S(1)}, f32[4,32,128]{2,1,0:T(8,128)S(1)}, f32[4,32,128]{2,1,0:T(8,128)S(1)}, f32[4,32,128]{2,1,0:T(8,128)S(1)}) custom-call(s32[4]{0:T(128)S(1)} %pad_add_fusion.place.refs_0_, s32[1,32]{1,0:T(1,128)S(1)} %copy-done.4, s32[1,32]{1,0:T(1,128)S(1)} %collective-permute-done.other, ...), custom_call_target="tpu_custom_call" | custom-call | flops 4194304 | bytes 2097152 | tf_op jit(solution)/shard_map/pallas_call | solution.py:320
  31.3 0.0 collective-permute-done.3.cross
  31.3 0.1 collective-permute-start.7
  31.4 0.0 collective-permute-done.1.other
  31.5 2.2 %collective-permute-start.8 = (f32[4,32,128]{2,1,0:T(8,128)S(1)}, f32[4,32,128]{2,1,0:T(8,128)S(1)}, u32[]{:S(2)}, u32[]{:S(2)}) collective-permute-start(f32[4,32,128]{2,1,0:T(8,128)S(1)} %get-tuple-element.56), channel_id=1, source_target_pairs={{0,64},{32,96},{64,0},{96,32},{1,65},{33,97},{65,1},{97,33},{2,66}... | collective-permute-start | bytes 196616 | tf_op jit(solution)/shard_map/ppermute | solution.py:299
  33.6 0.8 shard_map.78
  34.5 0.0 collective-permute-done.4.second
  34.5 1.1 %collective-permute-start.9 = (f32[4,32,128]{2,1,0:T(8,128)S(1)}, f32[4,32,128]{2,1,0:T(8,128)S(1)}, u32[]{:S(2)}, u32[]{:S(2)}) collective-permute-start(f32[4,32,128]{2,1,0:T(8,128)S(1)} %get-tuple-element.57), channel_id=1, source_target_pairs={{0,96},{32,0},{64,32},{96,64},{1,97},{33,1},{65,33},{97,65},{2,98}... | collective-permute-start | bytes 196616 | tf_op jit(solution)/shard_map/ppermute | solution.py:299
  35.6 0.1 convert_reduce_fusion.steps
  35.7 0.0 collective-permute-done.5.third
  35.7 0.0 collective-permute-done.6.fourth
  35.7 2.0 %collective-permute-done.7.b = f32[4,32,128]{2,1,0:T(8,128)S(1)} collective-permute-done((f32[4,32,128]{2,1,0:T(8,128)S(1)}, f32[4,32,128]{2,1,0:T(8,128)S(1)}, u32[]{:S(2)}, u32[]{:S(2)}) %collective-permute-start.7) | collective-permute-done | bytes 65568 | tf_op jit(solution)/shard_map/ppermute | solution.py:299
  37.7 0.0 collective-permute-done.8.c
  37.7 1.2 %collective-permute-done.9.d = f32[4,32,128]{2,1,0:T(8,128)S(1)} collective-permute-done((f32[4,32,128]{2,1,0:T(8,128)S(1)}, f32[4,32,128]{2,1,0:T(8,128)S(1)}, u32[]{:S(2)}, u32[]{:S(2)}) %collective-permute-start.9) | collective-permute-done | bytes 65568 | tf_op jit(solution)/shard_map/ppermute | solution.py:299
  38.9 2.8 %shard_map.80 = (f32[20,64,128]{2,1,0:T(8,128)S(1)}, f32[64,128]{1,0:T(8,128)S(1)}, f32[64,128]{1,0:T(8,128)S(1)}, f32[64,128]{1,0:T(8,128)S(1)}) custom-call(s32[4]{0:T(128)S(1)} %pad_add_fusion.place.refs_0_, s32[2,48]{1,0:T(2,128)S(1)} %convert_reduce_fusion.steps, f32[32,16,128]{2,1,0:T(8,128)S(1)} %get-tuple-element.49.first, ...), custom_call_target="tpu_custom_call" | custom-call | flops 4194304 | bytes 2097152 | tf_op jit(solution)/shard_map/pallas_call | solution.py:335
  41.7 0.1 collective-permute-start.10
  41.8 1.9 %shard_map.81 = f32[8,16,32,128]{3,2,1,0:T(8,128)} custom-call(f32[20,64,128]{2,1,0:T(8,128)S(1)} %get-tuple-element.60.grad, f32[64,128]{1,0:T(8,128)S(1)} %get-tuple-element.61.weights), custom_call_target="tpu_custom_call" | custom-call | flops 4194304 | bytes 2097152 | tf_op jit(solution)/shard_map/pallas_call | solution.py:347
  43.7 2.0 %collective-permute-done.10.other = f32[64,128]{1,0:T(8,128)S(1)} collective-permute-done((f32[64,128]{1,0:T(8,128)S(1)}, f32[64,128]{1,0:T(8,128)S(1)}, u32[]{:S(2)}, u32[]{:S(2)}) %collective-permute-start.10) | collective-permute-done | bytes 32800 | tf_op jit(solution)/shard_map/ppermute | solution.py:273
  45.7 3.9 %all-to-all-start = ((f32[8,16,32,128]{3,2,1,0:T(8,128)}), f32[8,16,32,128]{3,2,1,0:T(8,128)S(1)}, u32[]{:S(2)}, u32[]{:S(2)}) async-start(f32[8,16,32,128]{3,2,1,0:T(8,128)} %shard_map.81), calls=%async_computation | async-start | bytes 4194304 | tf_op jit(solution)/shard_map/all_to_all | solution.py:357
  49.5 0.5 shard_map.83
  50.1 3.9 %collective-permute-start.11 = (f32[24,128]{1,0:T(8,128)S(1)}, f32[24,128]{1,0:T(8,128)S(1)}, u32[]{:S(2)}, u32[]{:S(2)}) collective-permute-start(f32[24,128]{1,0:T(8,128)S(1)} %get-tuple-element.67), channel_id=1, source_target_pairs={{1,2},{2,1},{3,4},{4,3},{5,6},{6,5},{7,8},{8,7},{9,10},{10,9},{11,... | collective-permute-start | bytes 36872 | tf_op jit(solution)/shard_map/ppermute | solution.py:364
  54.0 0.1 collective-permute-start.12
  54.1 19.8 %collective-permute-done.11.side_o = f32[24,128]{1,0:T(8,128)S(1)} collective-permute-done((f32[24,128]{1,0:T(8,128)S(1)}, f32[24,128]{1,0:T(8,128)S(1)}, u32[]{:S(2)}, u32[]{:S(2)}) %collective-permute-start.11) | collective-permute-done | bytes 12320 | tf_op jit(solution)/shard_map/ppermute | solution.py:364
  73.9 0.0 collective-permute-done.12.side_e
  73.9 0.6 shard_map.84.refs_1_
  74.5 1.5 %collective-permute-start.13 = (f32[48,128]{1,0:T(8,128)S(1)}, f32[48,128]{1,0:T(8,128)S(1)}, u32[]{:S(2)}, u32[]{:S(2)}) collective-permute-start(f32[48,128]{1,0:T(8,128)S(1)} %shard_map.84.refs_1_), channel_id=1, source_target_pairs={{0,32},{32,64},{64,96},{96,0},{1,33},{33,65},{65,97},{97,1},{2,34}... | collective-permute-start | bytes 73736 | tf_op jit(solution)/shard_map/ppermute | solution.py:299
  76.0 3.0 %collective-permute-start.14 = (f32[48,128]{1,0:T(8,128)S(1)}, f32[48,128]{1,0:T(8,128)S(1)}, u32[]{:S(2)}, u32[]{:S(2)}) collective-permute-start(f32[48,128]{1,0:T(8,128)S(1)} %shard_map.84.refs_1_), channel_id=1, source_target_pairs={{0,64},{32,96},{64,0},{96,32},{1,65},{33,97},{65,1},{97,33},{2,66}... | collective-permute-start | bytes 73736 | tf_op jit(solution)/shard_map/ppermute | solution.py:299
  79.0 1.2 %collective-permute-start.15 = (f32[48,128]{1,0:T(8,128)S(1)}, f32[48,128]{1,0:T(8,128)S(1)}, u32[]{:S(2)}, u32[]{:S(2)}) collective-permute-start(f32[48,128]{1,0:T(8,128)S(1)} %shard_map.84.refs_1_), channel_id=1, source_target_pairs={{0,96},{32,0},{64,32},{96,64},{1,97},{33,1},{65,33},{97,65},{2,98}... | collective-permute-start | bytes 73736 | tf_op jit(solution)/shard_map/ppermute | solution.py:299
  80.2 0.0 all-to-all-done.parts
  80.2 1.4 %shard_map.82 = f32[32,32,512]{2,1,0:T(8,128)} custom-call(f32[8,16,32,128]{3,2,1,0:T(8,128)S(1)} %all-to-all-done.parts), custom_call_target="tpu_custom_call" | custom-call | flops 4194304 | bytes 2097152 | tf_op jit(solution)/shard_map/pallas_call | solution.py:371
  81.7 0.0 collective-permute-done.13.refs_2_
  81.7 0.0 collective-permute-done.14.refs_3_
  81.7 1.1 %collective-permute-done.15.refs_4_ = f32[48,128]{1,0:T(8,128)S(1)} collective-permute-done((f32[48,128]{1,0:T(8,128)S(1)}, f32[48,128]{1,0:T(8,128)S(1)}, u32[]{:S(2)}, u32[]{:S(2)}) %collective-permute-start.15) | collective-permute-done | bytes 24608 | tf_op jit(solution)/shard_map/ppermute | solution.py:299
  82.8 1.6 %shard_map.85 = f32[1,32,512]{2,1,0:T(8,128)} custom-call(s32[4]{0:T(128)S(1)} %pad_add_fusion.place.refs_0_, f32[48,128]{1,0:T(8,128)S(1)} %shard_map.84.refs_1_, f32[48,128]{1,0:T(8,128)S(1)} %collective-permute-done.13.refs_2_, f32[48,128]{1,0:T(8,128)S(1)} %collective-permute-done.14.refs_3_, f32[48,128]{1,0:T(8,128)S(1)} %collective-permute-done.15.refs_4_), custom_call_target="tpu_custom_call" | custom-call | flops 4194304 | bytes 2097152 | tf_op jit(solution)/shard_map/pallas_call | solution.py:375
  (7 shorter events, 0.0 us)
Async XLA Ops:
  0.6 5.0 %collective-permute-start = (s32[1,32]{1,0:T(1,128)}, s32[1,32]{1,0:T(1,128)S(1)}, u32[]{:S(2)}, u32[]{:S(2)}) collective-permute-start(s32[1,32]{1,0:T(1,128)} %index.1), channel_id=1, source_target_pairs={{0,128},{1,129},{2,130},{3,131},{4,132},{5,133},{6,134},{7,135},{8... | collective-permute-start | bytes 392 | tf_op jit(solution)/shard_map/ppermute | solution.py:273
  1.8 0.8 copy-start.2
  2.7 0.7 copy-start.3
  3.3 26.7 %copy-start = (f32[32,32,512]{2,1,0:T(8,128)S(1)}, f32[32,32,512]{2,1,0:T(8,128)}, u32[]{:S(2)}) copy-start(f32[32,32,512]{2,1,0:T(8,128)} %volume.3) | copy-start | bytes 6291460
  3.3 26.7 %copy-start.1 = (f32[680,32]{0,1:T(8,128)S(1)}, f32[680,32]{0,1:T(8,128)}, u32[]{:S(2)}) copy-start(f32[680,32]{0,1:T(8,128)} %param.10) | copy-start | bytes 261124
  3.3 26.7 %copy-start.4 = (s32[1,32]{1,0:T(1,128)S(1)}, s32[1,32]{1,0:T(1,128)}, u32[]{:S(2)}) copy-start(s32[1,32]{1,0:T(1,128)} %index.1) | copy-start | bytes 388
  5.7 25.8 %collective-permute-start.1 = (f32[34,32,128]{2,1,0:T(8,128)S(1)}, f32[34,32,128]{2,1,0:T(8,128)S(1)}, u32[]{:S(2)}, u32[]{:S(2)}) collective-permute-start(f32[34,32,128]{2,1,0:T(8,128)S(1)} %get-tuple-element.45.own), channel_id=1, source_target_pairs={{0,128},{1,129},{2,130},{3,131},{4,132},{5,133},{6,134},{7,135},{8... | collective-permute-start | bytes 1671176 | tf_op jit(solution)/shard_map/ppermute | solution.py:273
  6.8 20.2 %collective-permute-start.2 = (f32[42,16,128]{2,1,0:T(8,128)S(1)}, f32[42,16,128]{2,1,0:T(8,128)S(1)}, u32[]{:S(2)}, u32[]{:S(2)}) collective-permute-start(f32[42,16,128]{2,1,0:T(8,128)S(1)} %get-tuple-element.46), channel_id=1, source_target_pairs={{0,1},{1,2},{2,3},{3,4},{4,5},{5,6},{6,7},{7,8},{8,9},{9,10},{10,1... | collective-permute-start | bytes 1032200 | tf_op jit(solution)/shard_map/ppermute | solution.py:273
  8.7 22.7 %collective-permute-start.3 = (f32[34,16,128]{2,1,0:T(8,128)S(1)}, f32[34,16,128]{2,1,0:T(8,128)S(1)}, u32[]{:S(2)}, u32[]{:S(2)}) collective-permute-start(f32[34,16,128]{2,1,0:T(8,128)S(1)} %get-tuple-element.47), channel_id=1, source_target_pairs={{1,128},{2,129},{3,130},{4,131},{5,132},{6,133},{7,134},{8,135},{9... | collective-permute-start | bytes 835592 | tf_op jit(solution)/shard_map/ppermute | solution.py:273
  13.0 21.5 %collective-permute-start.4 = (f32[32,16,128]{2,1,0:T(8,128)S(1)}, f32[32,16,128]{2,1,0:T(8,128)S(1)}, u32[]{:S(2)}, u32[]{:S(2)}) collective-permute-start(f32[32,16,128]{2,1,0:T(8,128)S(1)} %get-tuple-element.50), channel_id=1, source_target_pairs={{0,32},{32,64},{64,96},{96,0},{1,33},{33,65},{65,97},{97,1},{2,34}... | collective-permute-start | bytes 786440 | tf_op jit(solution)/shard_map/ppermute | solution.py:299
  14.7 21.1 %collective-permute-start.5 = (f32[32,16,128]{2,1,0:T(8,128)S(1)}, f32[32,16,128]{2,1,0:T(8,128)S(1)}, u32[]{:S(2)}, u32[]{:S(2)}) collective-permute-start(f32[32,16,128]{2,1,0:T(8,128)S(1)} %get-tuple-element.51), channel_id=1, source_target_pairs={{0,64},{32,96},{64,0},{96,32},{1,65},{33,97},{65,1},{97,33},{2,66}... | collective-permute-start | bytes 786440 | tf_op jit(solution)/shard_map/ppermute | solution.py:299
  27.0 8.7 %collective-permute-start.6 = (f32[32,16,128]{2,1,0:T(8,128)S(1)}, f32[32,16,128]{2,1,0:T(8,128)S(1)}, u32[]{:S(2)}, u32[]{:S(2)}) collective-permute-start(f32[32,16,128]{2,1,0:T(8,128)S(1)} %get-tuple-element.52), channel_id=1, source_target_pairs={{0,96},{32,0},{64,32},{96,64},{1,97},{33,1},{65,33},{97,65},{2,98}... | collective-permute-start | bytes 786440 | tf_op jit(solution)/shard_map/ppermute | solution.py:299
  31.3 6.4 %collective-permute-start.7 = (f32[4,32,128]{2,1,0:T(8,128)S(1)}, f32[4,32,128]{2,1,0:T(8,128)S(1)}, u32[]{:S(2)}, u32[]{:S(2)}) collective-permute-start(f32[4,32,128]{2,1,0:T(8,128)S(1)} %get-tuple-element.55), channel_id=1, source_target_pairs={{0,32},{32,64},{64,96},{96,0},{1,33},{33,65},{65,97},{97,1},{2,34}... | collective-permute-start | bytes 196616 | tf_op jit(solution)/shard_map/ppermute | solution.py:299
  31.5 6.3 %collective-permute-start.8 = (f32[4,32,128]{2,1,0:T(8,128)S(1)}, f32[4,32,128]{2,1,0:T(8,128)S(1)}, u32[]{:S(2)}, u32[]{:S(2)}) collective-permute-start(f32[4,32,128]{2,1,0:T(8,128)S(1)} %get-tuple-element.56), channel_id=1, source_target_pairs={{0,64},{32,96},{64,0},{96,32},{1,65},{33,97},{65,1},{97,33},{2,66}... | collective-permute-start | bytes 196616 | tf_op jit(solution)/shard_map/ppermute | solution.py:299
  34.5 4.4 %collective-permute-start.9 = (f32[4,32,128]{2,1,0:T(8,128)S(1)}, f32[4,32,128]{2,1,0:T(8,128)S(1)}, u32[]{:S(2)}, u32[]{:S(2)}) collective-permute-start(f32[4,32,128]{2,1,0:T(8,128)S(1)} %get-tuple-element.57), channel_id=1, source_target_pairs={{0,96},{32,0},{64,32},{96,64},{1,97},{33,1},{65,33},{97,65},{2,98}... | collective-permute-start | bytes 196616 | tf_op jit(solution)/shard_map/ppermute | solution.py:299
  41.7 4.0 %collective-permute-start.10 = (f32[64,128]{1,0:T(8,128)S(1)}, f32[64,128]{1,0:T(8,128)S(1)}, u32[]{:S(2)}, u32[]{:S(2)}) collective-permute-start(f32[64,128]{1,0:T(8,128)S(1)} %get-tuple-element.62), channel_id=1, source_target_pairs={{0,128},{1,129},{2,130},{3,131},{4,132},{5,133},{6,134},{7,135},{8... | collective-permute-start | bytes 98312 | tf_op jit(solution)/shard_map/ppermute | solution.py:273
  45.7 34.5 %all-to-all-start = ((f32[8,16,32,128]{3,2,1,0:T(8,128)}), f32[8,16,32,128]{3,2,1,0:T(8,128)S(1)}, u32[]{:S(2)}, u32[]{:S(2)}) async-start(f32[8,16,32,128]{3,2,1,0:T(8,128)} %shard_map.81), calls=%async_computation | async-start | bytes 4194304 | tf_op jit(solution)/shard_map/all_to_all | solution.py:357
  50.1 23.9 %collective-permute-start.11 = (f32[24,128]{1,0:T(8,128)S(1)}, f32[24,128]{1,0:T(8,128)S(1)}, u32[]{:S(2)}, u32[]{:S(2)}) collective-permute-start(f32[24,128]{1,0:T(8,128)S(1)} %get-tuple-element.67), channel_id=1, source_target_pairs={{1,2},{2,1},{3,4},{4,3},{5,6},{6,5},{7,8},{8,7},{9,10},{10,9},{11,... | collective-permute-start | bytes 36872 | tf_op jit(solution)/shard_map/ppermute | solution.py:364
  54.0 19.9 %collective-permute-start.12 = (f32[24,128]{1,0:T(8,128)S(1)}, f32[24,128]{1,0:T(8,128)S(1)}, u32[]{:S(2)}, u32[]{:S(2)}) collective-permute-start(f32[24,128]{1,0:T(8,128)S(1)} %get-tuple-element.68), channel_id=1, source_target_pairs={{0,1},{1,0},{2,3},{3,2},{4,5},{5,4},{6,7},{7,6},{8,9},{9,8},{10,11... | collective-permute-start | bytes 36872 | tf_op jit(solution)/shard_map/ppermute | solution.py:364
  74.5 7.2 %collective-permute-start.13 = (f32[48,128]{1,0:T(8,128)S(1)}, f32[48,128]{1,0:T(8,128)S(1)}, u32[]{:S(2)}, u32[]{:S(2)}) collective-permute-start(f32[48,128]{1,0:T(8,128)S(1)} %shard_map.84.refs_1_), channel_id=1, source_target_pairs={{0,32},{32,64},{64,96},{96,0},{1,33},{33,65},{65,97},{97,1},{2,34}... | collective-permute-start | bytes 73736 | tf_op jit(solution)/shard_map/ppermute | solution.py:299
  76.0 5.6 %collective-permute-start.14 = (f32[48,128]{1,0:T(8,128)S(1)}, f32[48,128]{1,0:T(8,128)S(1)}, u32[]{:S(2)}, u32[]{:S(2)}) collective-permute-start(f32[48,128]{1,0:T(8,128)S(1)} %shard_map.84.refs_1_), channel_id=1, source_target_pairs={{0,64},{32,96},{64,0},{96,32},{1,65},{33,97},{65,1},{97,33},{2,66}... | collective-permute-start | bytes 73736 | tf_op jit(solution)/shard_map/ppermute | solution.py:299
  79.0 3.8 %collective-permute-start.15 = (f32[48,128]{1,0:T(8,128)S(1)}, f32[48,128]{1,0:T(8,128)S(1)}, u32[]{:S(2)}, u32[]{:S(2)}) collective-permute-start(f32[48,128]{1,0:T(8,128)S(1)} %shard_map.84.refs_1_), channel_id=1, source_target_pairs={{0,96},{32,0},{64,32},{96,64},{1,97},{33,1},{65,33},{97,65},{2,98}... | collective-permute-start | bytes 73736 | tf_op jit(solution)/shard_map/ppermute | solution.py:299
